TPU v7x, 256 devices: a whole 4x4x8 slice. The times are simulated.
256 devices in a mesh: fsdp: 16 (over z, x_hi), tp: 16 (over x_lo, y, core).
Axes of the slice: x: 4 (x_hi: 2, x_lo: 2; x = x_hi * 2 + x_lo), y: 4, z: 8, core: 2. Of those that a mesh axis runs over, the one named last changes fastest.
Arguments:
- attention_output: bfloat16 [8192, 8192], P('fsdp', 'tp'), may hold values from -6 to 6
- grad_out: bfloat16 [8192, 8192], P('fsdp', 'tp'), may hold values from -6 to 6
- base_weight: bfloat16 [8192, 8192], P('tp', 'fsdp'), may hold values from -0.0625 to 0.0625
- adapter_down: bfloat16 [8, 8192, 64], P(None, 'tp'), may hold values from -0.0625 to 0.0625
- adapter_up: bfloat16 [8, 64, 8192], P(None, None, 'tp'), may hold values from -0.0625 to 0.0625
- roles: int32 [64, 1], P('fsdp'), may hold values from 0 to 7
- live: int32 [64], P('fsdp'), may hold values 0 or 1
Outputs:
- input_gradient: bfloat16 [8192, 8192], P('fsdp', 'tp')
- down_gradient: float32 [8, 8192, 64], P(None, 'tp')
- up_gradient: float32 [8, 64, 8192], P(None, None, 'tp')
Inputs may be any that keep to these rules, and one draw needn't show every extreme that they name: `roles`: each role id names one adapter.
All inputs are finite; a program needn't handle non-finite values. No bound on the sum of `live` on one device may be relied on, other than what follows from the above.
Results may differ from a plain program's by a relative error of at most 0.0034.
Values may be sent and summed in bfloat16 or wider, within the bound.
No kernel may reach another device: no remote copies, remote signals or barrier semaphores. Data moves between devices by JAX's collectives and lax.ppermute only.
A program may use at most 128 MiB of HBM per device.

v0:
```python
import math

import jax
import jax.numpy as jnp
from jax import lax
from jax.sharding import PartitionSpec as P

adapter_scale = 2.0


def shards(attention_output, grad_out, base_weight, adapter_down, adapter_up, roles, live):
    tok_rows = attention_output.shape[0]
    head_columns = attention_output.shape[1]
    feature_columns = grad_out.shape[1]
    count_of_roles = adapter_down.shape[0]
    adapter_rank = adapter_down.shape[2]
    block_rows = tok_rows // roles.shape[0]
    total_tokens = tok_rows * lax.axis_size("fsdp")
    grad_scale = adapter_scale * math.sqrt(count_of_roles / total_tokens)
    token_role = jnp.repeat(roles[:, 0], block_rows)
    token_live = jnp.repeat(live, block_rows)
    masked_rows = jnp.where(token_live[:, None] > 0, grad_out, jnp.zeros_like(grad_out))
    onehot = (token_role[:, None] == jnp.arange(count_of_roles, dtype=jnp.int32)[None, :]).astype(
        jnp.float32
    )
    flattened_down = jnp.transpose(adapter_down, (1, 0, 2)).reshape(
        head_columns, count_of_roles * adapter_rank
    )
    up_flat = adapter_up.reshape(count_of_roles * adapter_rank, feature_columns)
    low_all = jnp.dot(attention_output, flattened_down, preferred_element_type=jnp.float32).reshape(
        tok_rows, count_of_roles, adapter_rank
    )
    back_all = lax.dot_general(
        masked_rows, up_flat, (((1,), (1,)), ((), ())), preferred_element_type=jnp.float32
    )
    back_all = back_all.reshape(tok_rows, count_of_roles, adapter_rank)
    low_part = jnp.sum(onehot[:, :, None] * low_all, axis=1)
    back_part = jnp.sum(onehot[:, :, None] * back_all, axis=1)
    low, back = lax.psum((low_part, back_part), "tp")
    lowrank_wide_rows = (
        (onehot[:, :, None] * low[:, None, :])
        .reshape(tok_rows, count_of_roles * adapter_rank)
        .astype(jnp.bfloat16)
    )
    backward_wide_rows = (
        (onehot[:, :, None] * back[:, None, :])
        .reshape(tok_rows, count_of_roles * adapter_rank)
        .astype(jnp.bfloat16)
    )
    whole_rows = lax.all_gather(masked_rows, "tp", axis=1, tiled=True)
    frozen_base_term = lax.dot_general(
        whole_rows,
        lax.all_gather(base_weight, "fsdp", axis=1, tiled=True),
        (((1,), (1,)), ((), ())),
        preferred_element_type=jnp.float32,
    )
    adapter_term = lax.dot_general(
        backward_wide_rows,
        flattened_down,
        (((1,), (1,)), ((), ())),
        preferred_element_type=jnp.float32,
    )
    input_gradient = (frozen_base_term + adapter_scale * adapter_term).astype(jnp.bfloat16)
    down_term = lax.dot_general(
        attention_output,
        backward_wide_rows,
        (((0,), (0,)), ((), ())),
        preferred_element_type=jnp.float32,
    )
    up_term = lax.dot_general(
        lowrank_wide_rows, masked_rows, (((0,), (0,)), ((), ())), preferred_element_type=jnp.float32
    )
    summed_down_gradient, summed_up_gradient = lax.psum((down_term, up_term), "fsdp")
    down_gradient = jnp.transpose(
        (grad_scale * summed_down_gradient).reshape(head_columns, count_of_roles, adapter_rank),
        (1, 0, 2),
    )
    up_gradient = (grad_scale * summed_up_gradient).reshape(
        count_of_roles, adapter_rank, feature_columns
    )
    return (input_gradient, down_gradient, up_gradient)


def solution(mesh):
    placed = (
        P("fsdp", "tp"),
        P("fsdp", "tp"),
        P("tp", "fsdp"),
        P(None, "tp", None),
        P(None, None, "tp"),
        P("fsdp", None),
        P("fsdp"),
    )
    return jax.shard_map(
        shards,
        mesh=mesh,
        in_specs=placed,
        out_specs=(P("fsdp", "tp"), P(None, "tp", None), P(None, None, "tp")),
        check_vma=False,
    )
```

profile of v0, /device:TPU:1, one launch (start us, length us, event | category | flops | bytes accessed | tf_op | source)
XLA Modules:
  0.0 533.7 jit_solution(16895016954560470923)
XLA Ops:
  7.2 0.0 copy-start
  7.2 0.0 all-reduce.5.cloned.1.call-start
  7.2 0.7 broadcast_compare_fusion
  7.9 0.1 broadcast_bitcast_fusion.1
  8.0 0.7 broadcast_bitcast_fusion
  8.7 1.2 broadcast_select_fusion
  9.9 0.0 copy-start.1
  9.9 2.4 fusion.3
  12.3 0.0 copy-done
  12.3 2.2 fusion.4
  14.5 0.0 all-reduce.5.cloned.1.call-update
  14.5 0.0 all-reduce.7.cloned.1.call-start
  14.6 125.6 %all-reduce.5.cloned.1.call-done = (f32[512,64]{0,1:T(8,128)}, f32[512,64]{0,1:T(8,128)}) async-done(((f32[512,64]{0,1:T(8,128)}, f32[512,64]{0,1:T(8,128)}), (f32[512,64]{0,1:T(8,128)}, f32[512,64]{0,1:T(8,128)})) %all-reduce.5.cloned.1.call-update) | async-done | bytes 262160 | tf_op jit(solution)/shard_map/psum | solution.py:39
  140.2 1.2 multiply_convert_fusion
  141.3 1.4 convolution_bitcast_fusion
  142.8 1.5 fusion.11
  144.2 0.0 all-reduce.7.cloned.1.call-update
  144.2 0.0 all-gather.3.cloned.1.call-start
  144.3 0.0 copy-done.1
  144.3 0.7 all-gather.3.cloned.1.call-update
  145.0 0.0 all-gather.5.cloned.1.call-start
  145.0 0.5 all-gather.5.cloned.1.call-update
  145.6 157.6 %all-reduce.7.cloned.1.call-done = (f32[512,512]{0,1:T(8,128)}, f32[512,512]{0,1:T(8,128)}) async-done(((f32[512,512]{0,1:T(8,128)}, f32[512,512]{0,1:T(8,128)}), (f32[512,512]{0,1:T(8,128)}, f32[512,512]{0,1:T(8,128)})) %all-reduce.7.cloned.1.call-update) | async-done | bytes 2097168 | tf_op jit(solution)/shard_map/psum | solution.py:73
  303.2 1.3 broadcast_multiply_fusion
  304.5 1.3 copy.13
  305.8 2.3 broadcast_multiply_fusion.1
  308.1 0.0 copy-start.2
  308.1 0.0 copy-start.3
  308.1 59.5 %all-gather.3.cloned.1.call-done = bf16[512,8192]{1,0:T(8,128)(2,1)} async-done(((bf16[512,512]{1,0:T(8,128)(2,1)}), bf16[512,8192]{1,0:T(8,128)(2,1)}) %all-gather.3.cloned.1.call-update) | async-done | bytes 8388624 | tf_op jit(solution)/shard_map/all_gather | solution.py:50
  367.6 148.7 %all-gather.5.cloned.1.call-done = bf16[512,8192]{1,0:T(8,128)(2,1)} async-done(((bf16[512,512]{1,0:T(8,128)(2,1)}), bf16[512,8192]{1,0:T(8,128)(2,1)}) %all-gather.5.cloned.1.call-update) | async-done | bytes 8388624 | tf_op jit(solution)/shard_map/all_gather | solution.py:53
  516.3 9.5 %fusion.10 = f32[512,512]{1,0:T(8,128)S(1)} fusion(bf16[512,8192]{1,0:T(8,128)(2,1)} %all-gather.3.cloned.1.call-done, bf16[512,8192]{1,0:T(8,128)(2,1)} %all-gather.5.cloned.1.call-done), kind=kOutput, calls=%fused_computation.23 | convolution fusion | flops 4294967296 | bytes 17825792 | tf_op jit(solution)/shard_map/dot_general | solution.py:51
  525.8 0.0 copy-done.2
  525.8 0.0 copy-done.3
  525.9 1.3 fusion.2
  (1 shorter events, 0.0 us)
Async XLA Ops:
  7.2 5.1 copy-start
  7.2 133.0 %all-reduce.5.cloned.1.call-start = ((), (), s32[]{:S(2)}) async-start(), calls=%async_computation.2 | async-start | bytes 524288 | tf_op jit(solution)/shard_map/psum | solution.py:39
  9.9 134.4 %copy-start.1 = (bf16[512,512]{1,0:T(8,128)(2,1)}, bf16[512,512]{1,0:T(8,128)(2,1)S(1)}, u32[]{:S(2)}) copy-start(bf16[512,512]{1,0:T(8,128)(2,1)S(1)} %broadcast_select_fusion) | copy-start | bytes 1572868
  14.5 288.7 %all-reduce.7.cloned.1.call-start = ((), (), s32[]{:S(2)}) async-start(), calls=%async_computation.3 | async-start | bytes 4194304 | tf_op jit(solution)/shard_map/psum | solution.py:73
  144.2 223.4 %all-gather.3.cloned.1.call-start = ((), (), s32[]{:S(2)}) async-start(), calls=%async_computation | async-start | bytes 8912896 | tf_op jit(solution)/shard_map/all_gather | solution.py:50
  145.0 371.3 %all-gather.5.cloned.1.call-start = ((), (), s32[]{:S(2)}) async-start(), calls=%async_computation.1 | async-start | bytes 8912896 | tf_op jit(solution)/shard_map/all_gather | solution.py:53
  308.1 217.8 %copy-start.2 = (f32[512,64]{0,1:T(8,128)S(1)}, f32[512,64]{0,1:T(8,128)}, u32[]{:S(2)}) copy-start(f32[512,64]{0,1:T(8,128)} %get-tuple-element.6) | copy-start | bytes 393220
  308.1 217.8 %copy-start.3 = (bf16[8,512,64]{1,2,0:T(8,128)(2,1)S(1)}, bf16[8,512,64]{1,2,0:T(8,128)(2,1)}, u32[]{:S(2)}) copy-start(bf16[8,512,64]{1,2,0:T(8,128)(2,1)} %param.10) | copy-start | bytes 1572868
Sparse Core Ops, SparseCore 0:
  14.6 125.4 all-reduce.4
  144.4 158.7 all-reduce.6
  305.7 61.8 all-gather.2
  370.3 146.0 all-gather.4
where the time goes:
time: 535 us; the launch traced here: 534 us
  waiting for transfers between devices  493 us (92%)
  matrix products  18.2 us (3%)
  between operations  13.8 us (3%)
  other arithmetic  6.67 us (1%)
    psum x1, waiting for transfers between devices, shards(): lax.psum((down_term, up_term), 'fsdp')  158 us
    all_gather x1, waiting for transfers between devices, shards(): lax.all_gather(base_weight, 'fsdp', axis=1, tiled=True)  149 us
    psum x1, waiting for transfers between devices, shards(): low, back = lax.psum((low_part, back_part), 'tp')  126 us
    all_gather x1, waiting for transfers between devices, shards(): whole_rows = lax.all_gather(masked_rows, 'tp', axis=1, tiled=True)  59.5 us
  transfers between devices with their start and end apart: 4, of which 4 were waited for; matrix products, arithmetic and copies ran while one was open for 1% of the time, Pallas kernels for 0%

commit v1 on v0

v1 whole, which is shorter than its diff:
```python
import functools
import math

import jax
import jax.numpy as jnp
from jax import lax
from jax.experimental import pallas as pl
from jax.experimental.pallas import tpu as pltpu
from jax.sharding import Mesh, PartitionSpec as P

adapter_scale = 2.0
Z, XH, XL, Y, C = 8, 2, 2, 4, 2
FS = ("z", "xh")
TP = ("xl", "y", "c")
ROLES = 8
RANK = 64
BLOCK = 128
BLOCKS = 4
GROUP = RANK // Z
ROWS = 512
COLS = 512
PAD = 128
OFFSETS = (0, -1, 1, -2, 2, -3, 3, -4)
f32 = jnp.float32
bf16 = jnp.bfloat16


def dot(a, b, ca, cb):
    return lax.dot_general(a, b, (((ca,), (cb,)), ((), ())), preferred_element_type=f32)


def rank_kernel(roles, att, g, down, up, out):
    out[:, :RANK] = dot(att[...], down[0], 1, 1)
    out[:, RANK:] = dot(g[...], up[0], 1, 1)


def rank_parts(roles, att, g, down, up):
    spec = pltpu.PrefetchScalarGridSpec(
        num_scalar_prefetch=1,
        grid=(BLOCKS,),
        in_specs=[
            pl.BlockSpec((BLOCK, COLS), lambda i, r: (i, 0)),
            pl.BlockSpec((BLOCK, COLS), lambda i, r: (i, 0)),
            pl.BlockSpec((1, RANK, COLS), lambda i, r: (r[i], 0, 0)),
            pl.BlockSpec((1, RANK, COLS), lambda i, r: (r[i], 0, 0)),
        ],
        out_specs=pl.BlockSpec((BLOCK, 2 * RANK), lambda i, r: (i, 0)),
    )
    return pl.pallas_call(
        rank_kernel,
        grid_spec=spec,
        out_shape=jax.ShapeDtypeStruct((ROWS, 2 * RANK), f32),
        cost_estimate=pl.CostEstimate(flops=2 * 2 * ROWS * COLS * RANK, bytes_accessed=2 << 20, transcendentals=0),
    )(roles, att, g, down, up)


def outer_kernel(roles, live, lb, att, g, out):
    for pair in range(BLOCKS // 2):
        ups, downs = [], []
        for b in (2 * pair, 2 * pair + 1):
            rows = pl.ds(b * BLOCK, BLOCK)
            ranks = lb[rows, :]
            ranks = jnp.where(live[b] > 0, ranks, jnp.zeros_like(ranks))
            ups.append(dot(ranks[:, :RANK], g[rows, :], 0, 0))
            downs.append(dot(ranks[:, RANK:], att[rows, :], 0, 0))
        at = pl.ds(2 * GROUP * pair, 2 * GROUP)
        first = lax.broadcasted_iota(jnp.int32, (2 * GROUP, PAD), 0) < GROUP
        ids = jnp.where(first, roles[2 * pair], roles[2 * pair + 1]).astype(f32).astype(bf16)
        for z in range(Z):
            for o, terms in enumerate((ups, downs)):
                part = [t[GROUP * z : GROUP * (z + 1), :] for t in terms]
                out[2 * z + o, at, :COLS] = jnp.concatenate(part, axis=0).astype(bf16)
                out[2 * z + o, at, COLS:] = ids


def outer_parts(roles, live, lb, att, g):
    spec = pltpu.PrefetchScalarGridSpec(
        num_scalar_prefetch=2,
        grid=(1,),
        in_specs=[
            pl.BlockSpec((ROWS, 2 * RANK), lambda i, r, l: (0, 0)),
            pl.BlockSpec((ROWS, COLS), lambda i, r, l: (0, 0)),
            pl.BlockSpec((ROWS, COLS), lambda i, r, l: (0, 0)),
        ],
        out_specs=pl.BlockSpec((Z * XH, BLOCKS * GROUP, COLS + PAD), lambda i, r, l: (0, 0, 0)),
    )
    return pl.pallas_call(
        outer_kernel,
        grid_spec=spec,
        out_shape=jax.ShapeDtypeStruct((Z * XH, BLOCKS * GROUP, COLS + PAD), bf16),
        compiler_params=pltpu.CompilerParams(vmem_limit_bytes=16 << 20),
        cost_estimate=pl.CostEstimate(flops=2 * 2 * ROWS * COLS * RANK, bytes_accessed=2 << 20, transcendentals=0),
    )(roles, live, lb, att, g)


def sum_kernel(scale, recv, out):
    got = recv[...]
    shape = (Z * XH * BLOCKS * GROUP, PAD)
    row = lax.broadcasted_iota(jnp.int32, shape, 0)
    lane = lax.broadcasted_iota(jnp.int32, shape, 1)
    role = got[:, COLS:].astype(f32)
    pick = (role == (lane // GROUP).astype(f32)) & (lane % GROUP == row % GROUP)
    total = dot(pick.astype(f32).astype(bf16), got[:, :COLS], 0, 0)
    total = (scale * total[: ROLES * GROUP, :]).astype(bf16)
    for i in range(Z * XH):
        out[i] = total


def sum_parts(recv, scale):
    rows = Z * XH * BLOCKS * GROUP
    return pl.pallas_call(
        functools.partial(sum_kernel, scale),
        out_shape=jax.ShapeDtypeStruct((Z * XH, ROLES * GROUP, COLS), bf16),
        compiler_params=pltpu.CompilerParams(vmem_limit_bytes=16 << 20),
        cost_estimate=pl.CostEstimate(flops=2 * rows * PAD * COLS, bytes_accessed=2 << 20, transcendentals=0),
    )(recv.reshape(rows, COLS + PAD))


def spread_kernel(recv, up, down):
    for half in range(2):
        ups, downs = [], []
        for z in range(Z):
            ups.append(recv[2 * z].astype(f32)[GROUP * half : GROUP * (half + 1), :])
            downs.append(recv[2 * z + 1].astype(f32)[GROUP * half : GROUP * (half + 1), :])
        up[half] = jnp.concatenate(ups, axis=0)
        down[half] = jnp.concatenate(downs, axis=0)


def spread(recv):
    return pl.pallas_call(
        spread_kernel,
        grid=(ROLES // 2,),
        in_specs=[pl.BlockSpec((Z * XH, 2 * GROUP, COLS), lambda i: (0, i, 0))],
        out_specs=[
            pl.BlockSpec((2, RANK, COLS), lambda i: (i, 0, 0)),
            pl.BlockSpec((2, RANK, COLS), lambda i: (i, 0, 0)),
        ],
        out_shape=[
            jax.ShapeDtypeStruct((ROLES, RANK, COLS), f32),
            jax.ShapeDtypeStruct((ROLES, RANK, COLS), f32),
        ],
        compiler_params=pltpu.CompilerParams(vmem_limit_bytes=16 << 20),
        cost_estimate=pl.CostEstimate(flops=0, bytes_accessed=4 << 20, transcendentals=0),
    )(recv)


def base_sum(place, a, weights):
    total = None
    for off, w in zip(OFFSETS, weights):
        j = lax.rem(place[0] + (off + Z), Z)
        term = dot(a[j, 0], w[...], 1, 1)
        total = term if total is None else total + term
    return total


def partner_kernel(place, a, *rest):
    rest[-1][...] = base_sum(place, a, rest[:Z]).astype(bf16)


def own_kernel(place, roles, live, a, *rest):
    weights, lb, down, out = rest[:Z], rest[Z], rest[Z + 1], rest[Z + 2]
    total = base_sum(place, a, weights)
    for b in range(BLOCKS):
        rows = pl.ds(b * BLOCK, BLOCK)
        term = dot(lb[rows, RANK:], down[roles[b]], 1, 0)
        mine = total[b * BLOCK : (b + 1) * BLOCK, :] + adapter_scale * term
        out[rows, :] = jnp.where(live[b] > 0, mine, jnp.zeros_like(mine))


def partner_part(place, a, weights):
    whole = pl.BlockSpec((COLS, COLS), lambda i, p: (0, 0))
    spec = pltpu.PrefetchScalarGridSpec(
        num_scalar_prefetch=1,
        grid=(1,),
        in_specs=[pl.BlockSpec((Z, 1, ROWS, COLS), lambda i, p: (0, 1 - p[1], 0, 0))] + [whole] * Z,
        out_specs=pl.BlockSpec((ROWS, COLS), lambda i, p: (0, 0)),
    )
    return pl.pallas_call(
        partner_kernel,
        grid_spec=spec,
        out_shape=jax.ShapeDtypeStruct((ROWS, COLS), bf16),
        compiler_params=pltpu.CompilerParams(vmem_limit_bytes=32 << 20),
        cost_estimate=pl.CostEstimate(flops=2 * ROWS * COLS * COLS * Z, bytes_accessed=8 << 20, transcendentals=0),
    )(place, a, *weights)


def own_part(place, roles, live, a, weights, lb, down):
    whole = pl.BlockSpec((COLS, COLS), lambda i, p, r, l: (0, 0))
    spec = pltpu.PrefetchScalarGridSpec(
        num_scalar_prefetch=3,
        grid=(1,),
        in_specs=[pl.BlockSpec((Z, 1, ROWS, COLS), lambda i, p, r, l: (0, p[1], 0, 0))]
        + [whole] * Z
        + [
            pl.BlockSpec((ROWS, 2 * RANK), lambda i, p, r, l: (0, 0)),
            pl.BlockSpec((ROLES, RANK, COLS), lambda i, p, r, l: (0, 0, 0)),
        ],
        out_specs=pl.BlockSpec((ROWS, COLS), lambda i, p, r, l: (0, 0)),
    )
    return pl.pallas_call(
        own_kernel,
        grid_spec=spec,
        out_shape=jax.ShapeDtypeStruct((ROWS, COLS), f32),
        compiler_params=pltpu.CompilerParams(vmem_limit_bytes=40 << 20),
        cost_estimate=pl.CostEstimate(flops=2 * ROWS * COLS * COLS * Z, bytes_accessed=8 << 20, transcendentals=0),
    )(place, roles, live, a, *weights, lb, down)


def along_z(x, step):
    return lax.ppermute(x, "z", [(i, (i + step) % Z) for i in range(Z)])


def shards(attention_output, grad_out, base_weight, adapter_down, adapter_up, roles, live):
    roles = roles[:, 0]
    adapter_down = jnp.transpose(adapter_down, (0, 2, 1))
    tokens = attention_output.shape[0] * Z * XH
    grad_scale = adapter_scale * math.sqrt(ROLES / tokens)
    place = jnp.stack([lax.axis_index("z"), lax.axis_index("xh")]).astype(jnp.int32)

    turned = lax.ppermute(grad_out, ("xh", "c"), [(0, 0), (1, 2), (2, 1), (3, 3)])
    whole = lax.all_gather(turned, TP)

    weights = [base_weight]
    one = two = base_weight
    for step in range(4):
        one = along_z(one, 1)
        weights.append(one)
        if step < 3:
            two = along_z(two, -1)
            weights.append(two)

    parts = rank_parts(roles, attention_output, grad_out, adapter_down, adapter_up)
    parts = lax.all_to_all(parts.reshape(16, ROWS // 16, 2 * RANK), TP, 0, 0)
    mine = jnp.sum(parts, axis=0).astype(bf16)
    lb = lax.all_to_all(jnp.broadcast_to(mine[None], (16,) + mine.shape), TP, 0, 0)
    lb = lb.reshape(ROWS, 2 * RANK)

    outer = outer_parts(roles, live, lb, attention_output, grad_out)
    outer = lax.all_to_all(outer, FS, 0, 0)
    total = sum_parts(outer, grad_scale)
    total = lax.all_to_all(total, FS, 0, 0)
    up_gradient, down_gradient = spread(total)

    a = whole.reshape(Z, XH, ROWS, COLS)
    partner = partner_part(place, a, weights)
    got = lax.ppermute(partner, "xh", [(0, 1), (1, 0)])
    own = own_part(place, roles, live, a, weights, lb, adapter_down)
    token_live = jnp.repeat(live, BLOCK)[:, None] > 0
    input_gradient = jnp.where(token_live, own + got.astype(f32), 0.0).astype(bf16)
    return (input_gradient, jnp.transpose(down_gradient, (0, 2, 1)), up_gradient)


def solution(mesh):
    fine = Mesh(mesh.devices.reshape(Z, XH, XL, Y, C), ("z", "xh", "xl", "y", "c"))
    placed = (
        P(FS, TP),
        P(FS, TP),
        P(TP, FS),
        P(None, TP, None),
        P(None, None, TP),
        P(FS, None),
        P(FS),
    )
    return jax.shard_map(
        shards,
        mesh=fine,
        in_specs=placed,
        out_specs=(P(FS, TP), P(None, TP, None), P(None, None, TP)),
        check_vma=False,
    )
```

time: 535 us -> 188 us (0.35)
  waiting for transfers between devices: 493 us -> 79.8 us
  starting transfers between devices: 0.16 us -> 35.5 us
  blocking collectives: 0 us -> 23.3 us
  Pallas kernels: 0 us -> 20.1 us
  matrix products: 18.2 us -> 0 us
  local copies, waits for them, and re-layouts: 2.13 us -> 11.1 us
    psum x2 -> x0, waiting for transfers between devices: 283 us -> none  [the longest x1 158 us: shards(): lax.psum((down_term, up_term), 'fsdp')]
    all_gather x2 -> x1, waiting for transfers between devices: 208 us -> 0.01 us  [shards(): whole = lax.all_gather(turned, TP)]
    ppermute x0 -> x9, waiting for transfers between devices: none -> 79.8 us  [the longest x7 72.7 us: along_z(): return lax.ppermute(x, 'z', [(i, (i + step) % Z) for i in range(Z)])]
    all_to_all x0 -> x2, blocking collectives: none -> 23.3 us  [the longest x1 12.6 us: shards(): parts = lax.all_to_all(parts.reshape(16, ROWS // 16, 2 * RANK), TP, 0, 0)]
    all_to_all x0 -> x2, starting transfers between devices: none -> 20.3 us  [the longest x1 12.1 us: shards(): outer = lax.all_to_all(outer, FS, 0, 0)]
    pallas_call x0 -> x6, Pallas kernels: none -> 20.1 us  [the longest x1 5.64 us: partner_part(): pl.pallas_call(partner_kernel, grid_spec=spec, out_shape=jax.ShapeDtypeSt...]
    dot_general x6 -> x0, matrix products: 18.2 us -> none  [the longest x1 9.51 us: shards(): lax.dot_general(whole_rows, lax.all_gather(base_weight, 'fsdp', axis=1, t...]
    ppermute x0 -> x9, starting transfers between devices: none -> 15.2 us  [the longest x7 6.32 us: along_z(): return lax.ppermute(x, 'z', [(i, (i + step) % Z) for i in range(Z)])]
  transfers between devices with their start and end apart: 4 -> 12, of which waited for: 4 -> 7; matrix products, arithmetic and copies ran while one was open for 1% -> 0% of each run, Pallas kernels for 0% -> 11%
where the time goes in v1:
time: 188 us; the launch traced here: 186 us
  waiting for transfers between devices  79.8 us (42%)
  starting transfers between devices  35.5 us (19%)
  blocking collectives  23.3 us (12%)
  Pallas kernels  20.1 us (11%)
  between operations  14.1 us (8%)
  local copies, waits for them, and re-layouts  11.1 us (6%)
  other arithmetic  2.1 us (1%)
    ppermute x7, waiting for transfers between devices, along_z(): return lax.ppermute(x, 'z', [(i, (i + step) % Z) for i in range(Z)])  72.7 us
    all_to_all x1, blocking collectives, shards(): parts = lax.all_to_all(parts.reshape(16, ROWS // 16, 2 * RANK), TP, 0, 0)  12.6 us
    all_to_all x1, starting transfers between devices, shards(): outer = lax.all_to_all(outer, FS, 0, 0)  12.1 us
    unnamed x22, local copies, waits for them, and re-layouts  11 us
    all_to_all x1, blocking collectives, shards(): lax.all_to_all(jnp.broadcast_to(mine[None], (16,) + mine.shape), TP, 0, 0)  10.7 us
    all_to_all x1, starting transfers between devices, shards(): total = lax.all_to_all(total, FS, 0, 0)  8.19 us
    ppermute x1, waiting for transfers between devices, shards(): lax.ppermute(grad_out, ('xh', 'c'), [(0, 0), (1, 2), (2, 1), (3, 3)])  7.06 us
    ppermute x7, starting transfers between devices, along_z(): return lax.ppermute(x, 'z', [(i, (i + step) % Z) for i in range(Z)])  6.32 us
  transfers between devices with their start and end apart: 12, of which 7 were waited for; matrix products, arithmetic and copies ran while one was open for 0% of the time, Pallas kernels for 11%

profile of v1, /device:TPU:1, one launch (start us, length us, event | category | flops | bytes accessed | tf_op | source)
XLA Modules:
  0.0 186.1 jit_solution(14000957069216332233)
XLA Ops:
  7.2 0.0 copy-start.4
  7.2 0.0 all-gather.3.cloned.1.call-start
  7.2 6.2 %collective-permute-start = (bf16[512,512]{1,0:T(8,128)(2,1)}, bf16[512,512]{1,0:T(8,128)(2,1)S(1)}, u32[]{:S(2)}, u32[]{:S(2)}) collective-permute-start(bf16[512,512]{1,0:T(8,128)(2,1)} %g.3), channel_id=1, source_target_pairs={{0,0},{1,16},{16,1},{17,17},{2,2},{3,18},{18,3},{19,19},{4,4},{5,2... | collective-permute-start | bytes 1572872 | tf_op jit(solution)/shard_map/ppermute | solution.py:220
  13.4 7.1 %collective-permute-done = bf16[512,512]{1,0:T(8,128)(2,1)S(1)} collective-permute-done((bf16[512,512]{1,0:T(8,128)(2,1)}, bf16[512,512]{1,0:T(8,128)(2,1)S(1)}, u32[]{:S(2)}, u32[]{:S(2)}) %collective-permute-start) | collective-permute-done | bytes 524320 | tf_op jit(solution)/shard_map/ppermute | solution.py:220
  20.5 0.0 copy-start.10
  20.5 0.8 copy-done.10
  21.3 0.0 all-gather.3.cloned.1.call-update
  21.3 4.5 %shard_map.94 = f32[512,128]{1,0:T(8,128)} custom-call(s32[4]{0:T(128)} %bitcast.18, bf16[512,512]{1,0:T(8,128)(2,1)} %att.3, bf16[512,512]{1,0:T(8,128)(2,1)} %g.3, bf16[8,64,512]{2,1,0:T(8,128)(2,1)} %bitcast.14, bf16[8,64,512]{2,1,0:T(8,128)(2,1)} %up.1), custom_call_target="tpu_custom_call" | custom-call | flops 67108864 | bytes 2097152 | tf_op jit(solution)/shard_map/pallas_call | solution.py:49
  25.8 12.6 %all_to_all.20 = f32[16,32,128]{2,1,0:T(8,128)S(1)} all-to-all(f32[16,32,128]{2,1,0:T(8,128)} %bitcast.21), channel_id=1, replica_groups=mesh['z'=8,'xh'=2,'xl'=2,'y'=4,'c'=2] {'xl','y','c'}, dimensions={0} | all-to-all | bytes 524288 | tf_op jit(solution)/shard_map/all_to_all | solution.py:233
  38.5 10.7 %all_to_all.21 = bf16[16,32,128]{2,1,0:T(8,128)(2,1)S(1)} all-to-all(bf16[16,32,128]{2,1,0:T(8,128)(2,1)S(1)} %broadcast_in_dim.23), channel_id=1, replica_groups=mesh['z'=8,'xh'=2,'xl'=2,'y'=4,'c'=2] {'xl','y','c'}, dimensions={0} | all-to-all | bytes 262144 | tf_op jit(solution)/shard_map/all_to_all | solution.py:235
  49.2 1.0 copy-done.2
  50.2 1.0 copy-done.3
  51.3 0.7 copy-done.6
  51.9 0.7 copy-done.8
  52.6 1.8 shard_map.97
  54.4 12.1 %all-to-all-start.2 = ((bf16[16,32,640]{2,1,0:T(8,128)(2,1)}), bf16[16,32,640]{2,1,0:T(8,128)(2,1)S(1)}, u32[]{:S(2)}, u32[]{:S(2)}) async-start(bf16[16,32,640]{2,1,0:T(8,128)(2,1)} %shard_map.97), calls=%async_computation.2 | async-start | bytes 1310720 | tf_op jit(solution)/shard_map/all_to_all | solution.py:239
  66.5 1.4 collective-permute-start.1
  67.9 1.4 collective-permute-start.2
  69.2 25.5 %collective-permute-done.1.rest_1_ = bf16[512,512]{1,0:T(8,128)(2,1)S(1)} collective-permute-done((bf16[512,512]{1,0:T(8,128)(2,1)}, bf16[512,512]{1,0:T(8,128)(2,1)S(1)}, u32[]{:S(2)}, u32[]{:S(2)}) %collective-permute-start.1) | collective-permute-done | bytes 524320 | tf_op jit(solution)/shard_map/ppermute | solution.py:210
  94.7 0.0 collective-permute-start.3
  94.7 0.0 all-to-all-done.2
  94.7 1.3 shard_map.98
  96.1 8.2 %all-to-all-start.3 = ((bf16[16,64,512]{2,1,0:T(8,128)(2,1)}), bf16[16,64,512]{2,1,0:T(8,128)(2,1)S(1)}, u32[]{:S(2)}, u32[]{:S(2)}) async-start(bf16[16,64,512]{2,1,0:T(8,128)(2,1)} %shard_map.98), calls=%async_computation.3 | async-start | bytes 2097152 | tf_op jit(solution)/shard_map/all_to_all | solution.py:241
  104.3 0.0 collective-permute-done.2.rest_2_
  104.3 2.7 %collective-permute-start.4 = (bf16[512,512]{1,0:T(8,128)(2,1)S(1)}, bf16[512,512]{1,0:T(8,128)(2,1)}, u32[]{:S(2)}, u32[]{:S(2)}) collective-permute-start(bf16[512,512]{1,0:T(8,128)(2,1)S(1)} %collective-permute-done.2.rest_2_), channel_id=1, source_target_pairs={{0,224},{32,0},{64,32},{96,64},{128,96},{160,128},{192,160},{224,1... | collective-permute-start | bytes 1572872 | tf_op jit(solution)/shard_map/ppermute | solution.py:210
  106.9 1.1 collective-permute-done.3.rest_3_
  108.0 0.0 collective-permute-start.5
  108.0 31.9 %collective-permute-done.4.rest_4_ = bf16[512,512]{1,0:T(8,128)(2,1)} collective-permute-done((bf16[512,512]{1,0:T(8,128)(2,1)S(1)}, bf16[512,512]{1,0:T(8,128)(2,1)}, u32[]{:S(2)}, u32[]{:S(2)}) %collective-permute-start.4) | collective-permute-done | bytes 524320 | tf_op jit(solution)/shard_map/ppermute | solution.py:210
  139.9 0.9 collective-permute-start.6
  140.8 1.4 collective-permute-done.5.rest_5_
  142.2 0.0 collective-permute-start.7
  142.2 0.1 pad_add_fusion.place
  142.2 9.9 %collective-permute-done.6.rest_6_ = bf16[512,512]{1,0:T(8,128)(2,1)} collective-permute-done((bf16[512,512]{1,0:T(8,128)(2,1)}, bf16[512,512]{1,0:T(8,128)(2,1)}, u32[]{:S(2)}, u32[]{:S(2)}) %collective-permute-start.6) | collective-permute-done | bytes 524320 | tf_op jit(solution)/shard_map/ppermute | solution.py:210
  152.1 3.0 %collective-permute-done.7.rest_7_ = bf16[512,512]{1,0:T(8,128)(2,1)} collective-permute-done((bf16[512,512]{1,0:T(8,128)(2,1)}, bf16[512,512]{1,0:T(8,128)(2,1)}, u32[]{:S(2)}, u32[]{:S(2)}) %collective-permute-start.7) | collective-permute-done | bytes 524320 | tf_op jit(solution)/shard_map/ppermute | solution.py:210
  155.2 0.0 copy-done.4
  155.2 3.4 %copy-done = bf16[8192,512]{1,0:T(8,128)(2,1)S(1)} copy-done((bf16[8192,512]{1,0:T(8,128)(2,1)S(1)}, bf16[8192,512]{1,0:T(8,128)(2,1)}, u32[]{:S(2)}) %copy-start) | copy-done | bytes 8388632
  158.6 5.6 %shard_map.96 = bf16[512,512]{1,0:T(8,128)(2,1)} custom-call(s32[2]{0:T(128)S(1)} %pad_add_fusion.place, bf16[8,2,512,512]{3,2,1,0:T(8,128)(2,1)S(1)} %bitcast.11, bf16[512,512]{1,0:T(8,128)(2,1)S(1)} %copy-done.4, bf16[512,512]{1,0:T(8,128)(2,1)S(1)} %collective-permute-done.1.rest_1_, bf16[512,512]{1,0:T(8,128)(2,1)S(1)} %collective-permute-done.2.rest_2_, ...), custom_call_target="tpu_custom_call" | custom-call | flops 2147483648 | bytes 8388608 | tf_op jit(solution)/shard_map/pallas_call | solution.py:178
  164.2 2.7 %collective-permute-start.8 = (bf16[512,512]{1,0:T(8,128)(2,1)}, bf16[512,512]{1,0:T(8,128)(2,1)}, u32[]{:S(2)}, u32[]{:S(2)}) collective-permute-start(bf16[512,512]{1,0:T(8,128)(2,1)} %shard_map.96), channel_id=1, source_target_pairs={{0,16},{16,0},{1,17},{17,1},{2,18},{18,2},{3,19},{19,3},{4,20},{20... | collective-permute-start | bytes 1572872 | tf_op jit(solution)/shard_map/ppermute | solution.py:246
  166.9 0.0 copy-done.9
  166.9 0.1 broadcast_bitcast_fusion
  167.0 0.0 all-to-all-done.3.recv
  167.0 1.9 %shard_map.99 = (f32[8,64,512]{2,1,0:T(8,128)}, f32[8,64,512]{2,1,0:T(8,128)}) custom-call(bf16[16,64,512]{2,1,0:T(8,128)(2,1)S(1)} %all-to-all-done.3.recv), custom_call_target="tpu_custom_call" | custom-call | bytes 4194304 | tf_op jit(solution)/shard_map/pallas_call | solution.py:130
  168.8 0.0 copy-done.5
  168.9 0.0 copy-done.7
  168.9 3.4 %copy-done.1 = bf16[8192,512]{1,0:T(8,128)(2,1)S(1)} copy-done((bf16[8192,512]{1,0:T(8,128)(2,1)S(1)}, bf16[8192,512]{1,0:T(8,128)(2,1)}, u32[]{:S(2)}) %copy-start.1) | copy-done | bytes 8388632
  172.2 5.0 %shard_map.95 = f32[512,512]{1,0:T(8,128)S(1)} custom-call(s32[2]{0:T(128)S(1)} %pad_add_fusion.place, s32[4]{0:T(128)S(1)} %bitcast.20, s32[4]{0:T(128)S(1)} %copy-done.9, bf16[8,2,512,512]{3,2,1,0:T(8,128)(2,1)S(1)} %bitcast.12, bf16[512,512]{1,0:T(8,128)(2,1)S(1)} %copy-done.4, bf16[512,512]{1,0:T(8,128)(2,1)S(1)} %collective-permute-done.1.rest_1_, ...), custom_call_target="tpu_custom_call" | custom-call | flops 2147483648 | bytes 8388608 | tf_op jit(solution)/shard_map/pallas_call | solution.py:200
  177.2 0.0 collective-permute-done.8
  177.2 2.0 %select_convert_fusion = bf16[512,512]{1,0:T(8,128)(2,1)} fusion(f32[512,512]{1,0:T(8,128)S(1)} %shard_map.95, bf16[512,512]{1,0:T(8,128)(2,1)} %collective-permute-done.8, pred[512]{0:T(512)(128)(4,1)S(1)} %broadcast_bitcast_fusion), kind=kLoop, calls=%fused_computation | loop fusion | flops 1048576 | bytes 2097664 | tf_op jit(solution)/shard_map/convert_element_type | solution.py:249
  (13 shorter events, 0.1 us)
Async XLA Ops:
  7.2 148.0 %copy-start.4 = (bf16[512,512]{1,0:T(8,128)(2,1)S(1)}, bf16[512,512]{1,0:T(8,128)(2,1)}, u32[]{:S(2)}) copy-start(bf16[512,512]{1,0:T(8,128)(2,1)} %rest_0_.3) | copy-start | bytes 1572868
  7.2 148.0 %all-gather.3.cloned.1.call-start = ((), (), s32[]{:S(2)}) async-start(), calls=%async_computation.4 | async-start | bytes 8912896 | tf_op jit(solution)/shard_map/all_gather | solution.py:221
  7.2 13.2 %collective-permute-start = (bf16[512,512]{1,0:T(8,128)(2,1)}, bf16[512,512]{1,0:T(8,128)(2,1)S(1)}, u32[]{:S(2)}, u32[]{:S(2)}) collective-permute-start(bf16[512,512]{1,0:T(8,128)(2,1)} %g.3), channel_id=1, source_target_pairs={{0,0},{1,16},{16,1},{17,17},{2,2},{3,18},{18,3},{19,19},{4,4},{5,2... | collective-permute-start | bytes 1572872 | tf_op jit(solution)/shard_map/ppermute | solution.py:220
  20.5 0.8 copy-start.10
  49.2 1.0 copy-start.2
  50.2 1.0 copy-start.3
  51.3 0.7 copy-start.6
  51.9 0.7 copy-start.8
  54.4 40.3 %all-to-all-start.2 = ((bf16[16,32,640]{2,1,0:T(8,128)(2,1)}), bf16[16,32,640]{2,1,0:T(8,128)(2,1)S(1)}, u32[]{:S(2)}, u32[]{:S(2)}) async-start(bf16[16,32,640]{2,1,0:T(8,128)(2,1)} %shard_map.97), calls=%async_computation.2 | async-start | bytes 1310720 | tf_op jit(solution)/shard_map/all_to_all | solution.py:239
  66.5 28.2 %collective-permute-start.1 = (bf16[512,512]{1,0:T(8,128)(2,1)}, bf16[512,512]{1,0:T(8,128)(2,1)S(1)}, u32[]{:S(2)}, u32[]{:S(2)}) collective-permute-start(bf16[512,512]{1,0:T(8,128)(2,1)} %rest_0_.3), channel_id=1, source_target_pairs={{0,32},{32,64},{64,96},{96,128},{128,160},{160,192},{192,224},{224... | collective-permute-start | bytes 1572872 | tf_op jit(solution)/shard_map/ppermute | solution.py:210
  67.9 36.4 %collective-permute-start.2 = (bf16[512,512]{1,0:T(8,128)(2,1)}, bf16[512,512]{1,0:T(8,128)(2,1)S(1)}, u32[]{:S(2)}, u32[]{:S(2)}) collective-permute-start(bf16[512,512]{1,0:T(8,128)(2,1)} %rest_0_.3), channel_id=1, source_target_pairs={{0,224},{32,0},{64,32},{96,64},{128,96},{160,128},{192,160},{224,1... | collective-permute-start | bytes 1572872 | tf_op jit(solution)/shard_map/ppermute | solution.py:210
  94.7 13.3 %collective-permute-start.3 = (bf16[512,512]{1,0:T(8,128)(2,1)S(1)}, bf16[512,512]{1,0:T(8,128)(2,1)}, u32[]{:S(2)}, u32[]{:S(2)}) collective-permute-start(bf16[512,512]{1,0:T(8,128)(2,1)S(1)} %collective-permute-done.1.rest_1_), channel_id=1, source_target_pairs={{0,32},{32,64},{64,96},{96,128},{128,160},{160,192},{192,224},{224... | collective-permute-start | bytes 1572872 | tf_op jit(solution)/shard_map/ppermute | solution.py:210
  94.7 72.2 %copy-start.9 = (s32[4]{0:T(128)S(1)}, s32[4]{0:T(128)}, u32[]{:S(2)}) copy-start(s32[4]{0:T(128)} %live.3) | copy-start | bytes 52
  96.1 72.8 %copy-start.5 = (bf16[8,512,64]{1,2,0:T(8,128)(2,1)S(1)}, bf16[8,512,64]{1,2,0:T(8,128)(2,1)}, u32[]{:S(2)}) copy-start(bf16[8,512,64]{1,2,0:T(8,128)(2,1)} %param.10) | copy-start | bytes 1572868
  96.1 72.8 %copy-start.7 = (s32[4,1]{0,1:T(1,128)S(1)}, s32[4,1]{0,1:T(1,128)}, u32[]{:S(2)}) copy-start(s32[4,1]{0,1:T(1,128)} %param.12) | copy-start | bytes 52
  96.1 70.9 %all-to-all-start.3 = ((bf16[16,64,512]{2,1,0:T(8,128)(2,1)}), bf16[16,64,512]{2,1,0:T(8,128)(2,1)S(1)}, u32[]{:S(2)}, u32[]{:S(2)}) async-start(bf16[16,64,512]{2,1,0:T(8,128)(2,1)} %shard_map.98), calls=%async_computation.3 | async-start | bytes 2097152 | tf_op jit(solution)/shard_map/all_to_all | solution.py:241
  104.3 35.6 %collective-permute-start.4 = (bf16[512,512]{1,0:T(8,128)(2,1)S(1)}, bf16[512,512]{1,0:T(8,128)(2,1)}, u32[]{:S(2)}, u32[]{:S(2)}) collective-permute-start(bf16[512,512]{1,0:T(8,128)(2,1)S(1)} %collective-permute-done.2.rest_2_), channel_id=1, source_target_pairs={{0,224},{32,0},{64,32},{96,64},{128,96},{160,128},{192,160},{224,1... | collective-permute-start | bytes 1572872 | tf_op jit(solution)/shard_map/ppermute | solution.py:210
  108.0 34.2 %collective-permute-start.5 = (bf16[512,512]{1,0:T(8,128)(2,1)}, bf16[512,512]{1,0:T(8,128)(2,1)}, u32[]{:S(2)}, u32[]{:S(2)}) collective-permute-start(bf16[512,512]{1,0:T(8,128)(2,1)} %collective-permute-done.3.rest_3_), channel_id=1, source_target_pairs={{0,32},{32,64},{64,96},{96,128},{128,160},{160,192},{192,224},{224... | collective-permute-start | bytes 1572872 | tf_op jit(solution)/shard_map/ppermute | solution.py:210
  139.9 12.3 %collective-permute-start.6 = (bf16[512,512]{1,0:T(8,128)(2,1)}, bf16[512,512]{1,0:T(8,128)(2,1)}, u32[]{:S(2)}, u32[]{:S(2)}) collective-permute-start(bf16[512,512]{1,0:T(8,128)(2,1)} %collective-permute-done.4.rest_4_), channel_id=1, source_target_pairs={{0,224},{32,0},{64,32},{96,64},{128,96},{160,128},{192,160},{224,1... | collective-permute-start | bytes 1572872 | tf_op jit(solution)/shard_map/ppermute | solution.py:210
  142.2 13.0 %collective-permute-start.7 = (bf16[512,512]{1,0:T(8,128)(2,1)}, bf16[512,512]{1,0:T(8,128)(2,1)}, u32[]{:S(2)}, u32[]{:S(2)}) collective-permute-start(bf16[512,512]{1,0:T(8,128)(2,1)} %collective-permute-done.5.rest_5_), channel_id=1, source_target_pairs={{0,32},{32,64},{64,96},{96,128},{128,160},{160,192},{192,224},{224... | collective-permute-start | bytes 1572872 | tf_op jit(solution)/shard_map/ppermute | solution.py:210
  155.2 3.4 %copy-start = (bf16[8192,512]{1,0:T(8,128)(2,1)S(1)}, bf16[8192,512]{1,0:T(8,128)(2,1)}, u32[]{:S(2)}) copy-start(bf16[8192,512]{1,0:T(8,128)(2,1)} %all-gather.3.cloned.1.call-done) | copy-start | bytes 25165828
  164.2 13.0 %collective-permute-start.8 = (bf16[512,512]{1,0:T(8,128)(2,1)}, bf16[512,512]{1,0:T(8,128)(2,1)}, u32[]{:S(2)}, u32[]{:S(2)}) collective-permute-start(bf16[512,512]{1,0:T(8,128)(2,1)} %shard_map.96), channel_id=1, source_target_pairs={{0,16},{16,0},{1,17},{17,1},{2,18},{18,2},{3,19},{19,3},{4,20},{20... | collective-permute-start | bytes 1572872 | tf_op jit(solution)/shard_map/ppermute | solution.py:246
  168.9 3.4 %copy-start.1 = (bf16[8192,512]{1,0:T(8,128)(2,1)S(1)}, bf16[8192,512]{1,0:T(8,128)(2,1)}, u32[]{:S(2)}) copy-start(bf16[8192,512]{1,0:T(8,128)(2,1)} %all-gather.3.cloned.1.call-done) | copy-start | bytes 25165828
Sparse Core Ops, SparseCore 0:
  21.4 66.1 all-gather.2

commit v2 on v1

v2 whole, which is shorter than its diff:
```python
import functools
import math

import jax
import jax.numpy as jnp
from jax import lax
from jax.experimental import pallas as pl
from jax.experimental.pallas import tpu as pltpu
from jax.sharding import Mesh, PartitionSpec as P

adapter_scale = 2.0
Z, XH, XL, Y, C = 8, 2, 2, 4, 2
FS = ("z", "xh")
TP = ("xl", "y", "c")
ROLES = 8
RANK = 64
BLOCK = 128
BLOCKS = 4
GROUP = RANK // Z
ROWS = 512
COLS = 512
PAD = 128
VMEM = 24 << 20
FULL = 56 << 20
OFFSETS = (0, -1, 1, -2, 2, -3, 3, -4)
MOST = 50 << 20
TILE = 256
f32 = jnp.float32
bf16 = jnp.bfloat16


def dot(a, b, ca, cb):
    return lax.dot_general(a, b, (((ca,), (cb,)), ((), ())), preferred_element_type=f32)


def rank_kernel(roles, att, g, down, up, out):
    for b in range(BLOCKS):
        rows = pl.ds(b * BLOCK, BLOCK)
        out[rows, :RANK] = dot(att[rows, :], down[roles[b]], 1, 1)
        out[rows, RANK:] = dot(g[rows, :], up[roles[b]], 1, 1)


def whole(shape):
    return pl.BlockSpec(shape, lambda i, p: (0,) * len(shape))


def rank_parts(roles, att, g, down, up):
    spec = pltpu.PrefetchScalarGridSpec(
        num_scalar_prefetch=1,
        grid=(1,),
        in_specs=[
            whole((ROWS, COLS)),
            whole((ROWS, COLS)),
            whole((ROLES, RANK, COLS)),
            whole((ROLES, RANK, COLS)),
        ],
        out_specs=whole((ROWS, 2 * RANK)),
    )
    return pl.pallas_call(
        rank_kernel,
        grid_spec=spec,
        out_shape=jax.ShapeDtypeStruct((ROWS, 2 * RANK), f32),
        compiler_params=pltpu.CompilerParams(vmem_limit_bytes=FULL),
        cost_estimate=pl.CostEstimate(flops=2 * 2 * ROWS * COLS * RANK, bytes_accessed=2 << 20, transcendentals=0),
    )(roles, att, g, down, up)


def outer_kernel(roles, live, lb, att_far, g_far, out, att, g, sems):
    copies = []
    for b in range(BLOCKS):
        rows = pl.ds(b * BLOCK, BLOCK)
        pairs = ((g_far.at[rows], g.at[rows]), (att_far.at[rows], att.at[rows]))
        copies.append([pltpu.make_async_copy(x, y, sems.at[b, i]) for i, (x, y) in enumerate(pairs)])
        for copy in copies[b]:
            copy.start()
    for pair in range(BLOCKS // 2):
        ups, downs = [], []
        for b in (2 * pair, 2 * pair + 1):
            rows = pl.ds(b * BLOCK, BLOCK)
            for copy in copies[b]:
                copy.wait()
            ranks = lb[rows, :]
            ranks = jnp.where(live[b] > 0, ranks, jnp.zeros_like(ranks))
            ups.append(dot(ranks[:, :RANK], g[rows, :], 0, 0))
            downs.append(dot(ranks[:, RANK:], att[rows, :], 0, 0))
        at = pl.ds(2 * GROUP * pair, 2 * GROUP)
        first = lax.broadcasted_iota(jnp.int32, (2 * GROUP, PAD), 0) < GROUP
        ids = jnp.where(first, roles[2 * pair], roles[2 * pair + 1])
        ids = ids.astype(f32).astype(bf16)
        for z in range(Z):
            for o, terms in enumerate((ups, downs)):
                part = [t[GROUP * z : GROUP * (z + 1), :] for t in terms]
                out[2 * z + o, at, :COLS] = jnp.concatenate(part, axis=0).astype(bf16)
                out[2 * z + o, at, COLS:] = ids


def outer_parts(roles, live, lb, att, g):
    return pl.pallas_call(
        outer_kernel,
        in_specs=[pl.BlockSpec(memory_space=pltpu.SMEM)] * 2
        + [pl.BlockSpec(memory_space=pltpu.VMEM)]
        + [pl.BlockSpec(memory_space=pl.ANY)] * 2,
        out_specs=pl.BlockSpec(memory_space=pltpu.VMEM),
        scratch_shapes=[
            pltpu.VMEM((ROWS, COLS), bf16),
            pltpu.VMEM((ROWS, COLS), bf16),
            pltpu.SemaphoreType.DMA((BLOCKS, 2)),
        ],
        out_shape=jax.ShapeDtypeStruct((Z * XH, BLOCKS * GROUP, COLS + PAD), bf16),
        compiler_params=pltpu.CompilerParams(vmem_limit_bytes=FULL),
        cost_estimate=pl.CostEstimate(flops=2 * 2 * ROWS * COLS * RANK, bytes_accessed=2 << 20, transcendentals=0),
    )(roles, live, lb, att, g)


def sum_kernel(scale, recv, out):
    got = recv[...]
    shape = (Z * XH * BLOCKS * GROUP, PAD)
    row = lax.broadcasted_iota(jnp.int32, shape, 0)
    lane = lax.broadcasted_iota(jnp.int32, shape, 1)
    role = got[:, COLS:].astype(f32)
    pick = (role == (lane // GROUP).astype(f32)) & (lane % GROUP == row % GROUP)
    total = dot(pick.astype(f32).astype(bf16), got[:, :COLS], 0, 0)
    total = (scale * total[: ROLES * GROUP, :]).astype(bf16)
    for i in range(Z * XH):
        out[i] = total


def sum_parts(recv, scale):
    rows = Z * XH * BLOCKS * GROUP
    return pl.pallas_call(
        functools.partial(sum_kernel, scale),
        out_shape=jax.ShapeDtypeStruct((Z * XH, ROLES * GROUP, COLS), bf16),
        compiler_params=pltpu.CompilerParams(vmem_limit_bytes=16 << 20),
        cost_estimate=pl.CostEstimate(flops=2 * rows * PAD * COLS, bytes_accessed=2 << 20, transcendentals=0),
    )(recv.reshape(rows, COLS + PAD))


def spread_kernel(recv, up, down):
    for half in range(2):
        ups, downs = [], []
        for z in range(Z):
            ups.append(recv[2 * z].astype(f32)[GROUP * half : GROUP * (half + 1), :])
            downs.append(recv[2 * z + 1].astype(f32)[GROUP * half : GROUP * (half + 1), :])
        up[half] = jnp.concatenate(ups, axis=0)
        down[half] = jnp.concatenate(downs, axis=0)


def spread(recv):
    return pl.pallas_call(
        spread_kernel,
        grid=(ROLES // 2,),
        in_specs=[pl.BlockSpec((Z * XH, 2 * GROUP, COLS), lambda i: (0, i, 0))],
        out_specs=[pl.BlockSpec((2, RANK, COLS), lambda i: (i, 0, 0))] * 2,
        out_shape=[jax.ShapeDtypeStruct((ROLES, RANK, COLS), f32)] * 2,
        compiler_params=pltpu.CompilerParams(vmem_limit_bytes=VMEM),
        cost_estimate=pl.CostEstimate(flops=0, bytes_accessed=4 << 20, transcendentals=0),
    )(recv)


def base_kernel(place, roles, live, wide, *refs):
    pieces, (lb, down), (far, near, own), (sheets, total, sems) = refs[:8], refs[8:10], refs[10:13], refs[13:]
    x_hi, x_lo, y, core = place[1], place[2], place[3], place[4]
    columns = (x_lo, 1 - x_lo, x_lo, x_lo, 1 - x_lo, 1 - x_lo, x_lo, 1 - x_lo)
    steps = (0, 0, -1, 1, -1, 1, 2, 2)
    blocks = [(p, column, y + Y + step) for p, column, step in zip(pieces, columns, steps)]
    copies = []
    for s, (_, column, row) in enumerate(blocks):
        j = column * Y + lax.rem(row, Y)
        copies.append(pltpu.make_async_copy(wide.at[j], sheets.at[s], sems.at[s]))
        copies[s].start()
    for s, (block, _, _) in enumerate(blocks):
        copies[s].wait()
        for half in range(C):
            term = dot(block[...], sheets[s, half], 1, 1)
            total[half] = term if s == 0 else total[half] + term

    mine = core == x_hi
    far[...] = total[1 - core].astype(bf16)
    near[...] = total[jnp.where(mine, 1 - core, core)].astype(bf16)
    for b in range(BLOCKS):
        rows = pl.ds(b * BLOCK, BLOCK)
        term = adapter_scale * dot(lb[rows, RANK:], down[roles[b]], 1, 0)
        part = total[core, rows, :]
        part = jnp.where(mine, part, jnp.zeros_like(part)) + term
        own[rows, :] = jnp.where(live[b] > 0, part, jnp.zeros_like(part))


def base_parts(place, roles, live, wide, *pieces):
    here = pl.BlockSpec(memory_space=pltpu.VMEM)
    return pl.pallas_call(
        base_kernel,
        in_specs=[pl.BlockSpec(memory_space=pltpu.SMEM)] * 3
        + [pl.BlockSpec(memory_space=pl.ANY)]
        + [here] * len(pieces),
        out_specs=[here] * 3,
        scratch_shapes=[
            pltpu.VMEM((Z, C, COLS, COLS), bf16),
            pltpu.VMEM((C, ROWS, COLS), f32),
            pltpu.SemaphoreType.DMA((Z,)),
        ],
        out_shape=[
            jax.ShapeDtypeStruct((ROWS, COLS), bf16),
            jax.ShapeDtypeStruct((ROWS, COLS), bf16),
            jax.ShapeDtypeStruct((ROWS, COLS), f32),
        ],
        compiler_params=pltpu.CompilerParams(vmem_limit_bytes=MOST),
        cost_estimate=pl.CostEstimate(flops=4 * ROWS * COLS * COLS * Z, bytes_accessed=14 << 20, transcendentals=0),
    )(place, roles, live, wide, *pieces)


def shift(x, axis, size, step):
    return lax.ppermute(x, axis, [(i, (i + step) % size) for i in range(size)])


def tie(*values):
    return lax.optimization_barrier(values)


def trade(x, axis, size, bit):
    return lax.ppermute(x, axis, [(i, i ^ bit) for i in range(size)])


def shards(attention_output, grad_out, base_weight, adapter_down, adapter_up, roles, live):
    adapter_down = jnp.transpose(adapter_down, (0, 2, 1))
    tokens = attention_output.shape[0] * Z * XH
    grad_scale = adapter_scale * math.sqrt(ROLES / tokens)
    roles = roles[:, 0]
    place = jnp.stack([lax.axis_index(name) for name in ("z", "xh", "xl", "y", "c")]).astype(jnp.int32)

    wide = lax.all_gather(base_weight, ("z", "c")).reshape(Z, C, COLS, COLS)
    turned = lax.ppermute(grad_out, ("xh", "c"), [(0, 0), (1, 2), (2, 1), (3, 3)])
    ranks = rank_parts(roles, attention_output, grad_out, adapter_down, adapter_up)
    ranks = lax.all_to_all(ranks.reshape(16, ROWS // 16, 2 * RANK), TP, 0, 0)
    ranks, turned = tie(ranks, turned)

    beside = trade(turned, "xl", XL, 1)
    up1, down1 = shift(turned, "y", Y, 1), shift(turned, "y", Y, -1)
    mine = jnp.sum(ranks, axis=0).astype(bf16)
    lb = lax.all_to_all(jnp.broadcast_to(mine[None], (16,) + mine.shape), TP, 0, 0)
    lb, beside, up1, down1 = tie(lb.reshape(ROWS, 2 * RANK), beside, up1, down1)

    up2, beside_down1 = shift(up1, "y", Y, 1), shift(beside, "y", Y, -1)
    outer = outer_parts(roles, live, lb, attention_output, grad_out)
    outer = lax.all_to_all(outer, FS, 0, 0)
    beside_up1, beside_down2 = shift(beside, "y", Y, 1), shift(beside_down1, "y", Y, -1)
    outer, up2, beside_up1, beside_down2 = tie(outer, up2, beside_up1, beside_down2)
    pieces = [turned, beside, up1, down1, beside_up1, beside_down1, up2, beside_down2]

    total = lax.all_to_all(sum_parts(outer, grad_scale), FS, 0, 0)
    far, near, own = base_parts(place, roles, live, wide, *pieces, lb, adapter_down)
    far = lax.ppermute(far, ("xh", "c"), [(1, 2), (2, 1)])
    near = lax.ppermute(near, ("xh", "c"), [(0, 1), (1, 3), (2, 0), (3, 2)])
    total, own = tie(total, own)
    up_gradient, down_gradient = spread(total)
    token_live = jnp.repeat(live, BLOCK)[:, None] > 0
    input_gradient = jnp.where(token_live, own + far.astype(f32) + near.astype(f32), 0.0).astype(bf16)
    return (input_gradient, jnp.transpose(down_gradient, (0, 2, 1)), up_gradient)


def solution(mesh):
    fine = Mesh(mesh.devices.reshape(Z, XH, XL, Y, C), ("z", "xh", "xl", "y", "c"))
    placed = (
        P(FS, TP),
        P(FS, TP),
        P(TP, FS),
        P(None, TP, None),
        P(None, None, TP),
        P(FS, None),
        P(FS),
    )
    return jax.shard_map(
        shards,
        mesh=fine,
        in_specs=placed,
        out_specs=(P(FS, TP), P(None, TP, None), P(None, None, TP)),
        check_vma=False,
    )
```

time: 188 us -> 144 us (0.77)
  waiting for transfers between devices: 79.8 us -> 36.5 us
  local copies, waits for them, and re-layouts: 11.1 us -> 3.73 us
  starting transfers between devices: 35.5 us -> 41.4 us
  blocking collectives: 23.3 us -> 25.7 us
    ppermute x8 -> x9, waiting for transfers between devices: 72.8 us -> 28.9 us  [the longest x6 20.7 us: shift(): return lax.ppermute(x, axis, [(i, (i + step) % size) for i in range(size)])]
    ppermute x8 -> x9, starting transfers between devices: 9.01 us -> 17.2 us  [the longest x6 8.95 us: shift(): return lax.ppermute(x, axis, [(i, (i + step) % size) for i in range(size)])]
    unnamed x22 -> x14, local copies, waits for them, and re-layouts: 11 us -> 3.55 us
    ppermute x1, waiting for transfers between devices: 7.06 us -> 0.01 us  [shards(): lax.ppermute(grad_out, ('xh', 'c'), [(0, 0), (1, 2), (2, 1), (3, 3)])]
    all_to_all x1, waiting for transfers between devices: 0.01 us -> 6.93 us  [shards(): total = lax.all_to_all(sum_parts(outer, grad_scale), FS, 0, 0)]
    all_to_all x1, blocking collectives: 10.7 us -> 13.9 us  [shards(): lax.all_to_all(jnp.broadcast_to(mine[None], (16,) + mine.shape), TP, 0, 0)]
    all_to_all x1, starting transfers between devices: 12.1 us -> 9.47 us  [shards(): outer = lax.all_to_all(outer, FS, 0, 0)]
    pallas_call x3 -> x2, Pallas kernels: 12.4 us -> 13.3 us  [the longest x1 9.42 us: base_parts(): pl.pallas_call(base_kernel, in_specs=[pl.BlockSpec(memory_space=pltpu.SME...]
  transfers between devices with their start and end apart: 12 -> 13, of which waited for: 7 -> 5; matrix products, arithmetic and copies ran while one was open for 0% -> 0% of each run, Pallas kernels for 11% -> 14%
where the time goes in v2:
time: 144 us
  starting transfers between devices  41.4 us (29%)
  waiting for transfers between devices  36.5 us (25%)
  blocking collectives  25.7 us (18%)
  Pallas kernels  19.8 us (14%)
  between operations  14.2 us (10%)
  local copies, waits for them, and re-layouts  3.73 us (3%)
  other arithmetic  2.27 us (2%)
    ppermute x6, waiting for transfers between devices, shift(): return lax.ppermute(x, axis, [(i, (i + step) % size) for i in range(size)])  20.7 us
    all_to_all x1, blocking collectives, shards(): lax.all_to_all(jnp.broadcast_to(mine[None], (16,) + mine.shape), TP, 0, 0)  13.9 us
    all_to_all x1, blocking collectives, shards(): ranks = lax.all_to_all(ranks.reshape(16, ROWS // 16, 2 * RANK), TP, 0, 0)  11.8 us
    all_to_all x1, starting transfers between devices, shards(): outer = lax.all_to_all(outer, FS, 0, 0)  9.47 us
    pallas_call x1, Pallas kernels, base_parts(): pl.pallas_call(base_kernel, in_specs=[pl.BlockSpec(memory_space=pltpu.SME...  9.42 us
    ppermute x6, starting transfers between devices, shift(): return lax.ppermute(x, axis, [(i, (i + step) % size) for i in range(size)])  8.95 us
    all_to_all x1, starting transfers between devices, shards(): total = lax.all_to_all(sum_parts(outer, grad_scale), FS, 0, 0)  8.69 us
    ppermute x1, starting transfers between devices, shards(): far = lax.ppermute(far, ('xh', 'c'), [(1, 2), (2, 1)])  7.31 us
  transfers between devices with their start and end apart: 13, of which 5 were waited for; matrix products, arithmetic and copies ran while one was open for 0% of the time, Pallas kernels for 14%

profile of v2, /device:TPU:1, one launch (start us, length us, event | category | flops | bytes accessed | tf_op | source)
XLA Modules:
  0.0 143.6 jit_solution(2702035457554714988)
XLA Ops:
  7.2 0.0 copy-start.1
  7.2 0.0 copy-start.2
  7.2 0.0 all-gather.3.cloned.1.call-start
  7.2 0.7 all-gather.3.cloned.1.call-update
  7.9 6.0 %collective-permute-start = (bf16[512,512]{1,0:T(8,128)(2,1)}, bf16[512,512]{1,0:T(8,128)(2,1)S(1)}, u32[]{:S(2)}, u32[]{:S(2)}) collective-permute-start(bf16[512,512]{1,0:T(8,128)(2,1)} %g_far.1), channel_id=1, source_target_pairs={{0,0},{1,16},{16,1},{17,17},{2,2},{3,18},{18,3},{19,19},{4,4},{5,2... | collective-permute-start | bytes 1572872 | tf_op jit(solution)/shard_map/ppermute | solution.py:231
  14.0 3.4 %shard_map.94 = f32[512,128]{1,0:T(8,128)} custom-call(s32[4]{0:T(128)} %bitcast.17, bf16[512,512]{1,0:T(8,128)(2,1)} %att_far.1, bf16[512,512]{1,0:T(8,128)(2,1)} %g_far.1, bf16[8,64,512]{2,1,0:T(8,128)(2,1)} %bitcast.21, bf16[8,64,512]{2,1,0:T(8,128)(2,1)} %up.1), custom_call_target="tpu_custom_call" | custom-call | flops 67108864 | bytes 2097152 | tf_op jit(solution)/shard_map/pallas_call | solution.py:59
  17.3 11.8 %all_to_all.20 = f32[16,32,128]{2,1,0:T(8,128)S(1)} all-to-all(f32[16,32,128]{2,1,0:T(8,128)} %bitcast.20), channel_id=1, replica_groups=mesh['z'=8,'xh'=2,'xl'=2,'y'=4,'c'=2] {'xl','y','c'}, dimensions={0} | all-to-all | bytes 524288 | tf_op jit(solution)/shard_map/all_to_all | solution.py:233
  29.1 0.0 collective-permute-done.refs_0_
  29.1 0.8 collective-permute-start.1
  29.9 0.2 collective-permute-start.2
  30.2 2.5 %collective-permute-start.3 = (bf16[512,512]{1,0:T(8,128)(2,1)S(1)}, bf16[512,512]{1,0:T(8,128)(2,1)S(1)}, u32[]{:S(2)}, u32[]{:S(2)}) collective-permute-start(bf16[512,512]{1,0:T(8,128)(2,1)S(1)} %collective-permute-done.refs_0_), channel_id=1, source_target_pairs={{0,6},{2,0},{4,2},{6,4},{1,7},{3,1},{5,3},{7,5},{8,14},{10,8},{12,... | collective-permute-start | bytes 1572872 | tf_op jit(solution)/shard_map/ppermute | solution.py:212
  32.7 13.9 %all_to_all.21 = bf16[16,32,128]{2,1,0:T(8,128)(2,1)} all-to-all(bf16[16,32,128]{2,1,0:T(8,128)(2,1)S(1)} %broadcast_in_dim.23), channel_id=1, replica_groups=mesh['z'=8,'xh'=2,'xl'=2,'y'=4,'c'=2] {'xl','y','c'}, dimensions={0} | all-to-all | bytes 262144 | tf_op jit(solution)/shard_map/all_to_all | solution.py:239
  46.6 0.0 collective-permute-done.1.refs_1_
  46.6 0.0 collective-permute-done.2.refs_2_
  46.6 0.0 collective-permute-done.3.refs_3_
  46.6 3.8 %shard_map.95 = bf16[16,32,640]{2,1,0:T(8,128)(2,1)} custom-call(s32[4]{0:T(128)} %bitcast.18, s32[4]{0:T(128)} %live.3, bf16[512,128]{1,0:T(8,128)(2,1)} %bitcast.15, bf16[512,512]{1,0:T(8,128)(2,1)} %att_far.1, bf16[512,512]{1,0:T(8,128)(2,1)} %g_far.1), custom_call_target="tpu_custom_call" | custom-call | flops 67108864 | bytes 2097152 | tf_op jit(solution)/shard_map/pallas_call | solution.py:98
  50.5 9.5 %all-to-all-start.2 = ((bf16[16,32,640]{2,1,0:T(8,128)(2,1)}), bf16[16,32,640]{2,1,0:T(8,128)(2,1)S(1)}, u32[]{:S(2)}, u32[]{:S(2)}) async-start(bf16[16,32,640]{2,1,0:T(8,128)(2,1)} %shard_map.95), calls=%async_computation.2 | async-start | bytes 1310720 | tf_op jit(solution)/shard_map/all_to_all | solution.py:244
  59.9 2.7 %collective-permute-start.6 = (bf16[512,512]{1,0:T(8,128)(2,1)S(1)}, bf16[512,512]{1,0:T(8,128)(2,1)S(1)}, u32[]{:S(2)}, u32[]{:S(2)}) collective-permute-start(bf16[512,512]{1,0:T(8,128)(2,1)S(1)} %collective-permute-done.1.refs_1_), channel_id=1, source_target_pairs={{0,6},{2,0},{4,2},{6,4},{1,7},{3,1},{5,3},{7,5},{8,14},{10,8},{12,... | collective-permute-start | bytes 1572872 | tf_op jit(solution)/shard_map/ppermute | solution.py:212
  62.7 0.0 collective-permute-start.5
  62.7 0.0 collective-permute-start.4
  62.7 10.6 %collective-permute-done.6.refs_5_ = bf16[512,512]{1,0:T(8,128)(2,1)S(1)} collective-permute-done((bf16[512,512]{1,0:T(8,128)(2,1)S(1)}, bf16[512,512]{1,0:T(8,128)(2,1)S(1)}, u32[]{:S(2)}, u32[]{:S(2)}) %collective-permute-start.6) | collective-permute-done | bytes 524320 | tf_op jit(solution)/shard_map/ppermute | solution.py:212
  73.3 0.0 copy-start.5
  73.3 3.5 %collective-permute-start.7 = (bf16[512,512]{1,0:T(8,128)(2,1)S(1)}, bf16[512,512]{1,0:T(8,128)(2,1)}, u32[]{:S(2)}, u32[]{:S(2)}) collective-permute-start(bf16[512,512]{1,0:T(8,128)(2,1)S(1)} %collective-permute-done.6.refs_5_), channel_id=1, source_target_pairs={{0,6},{2,0},{4,2},{6,4},{1,7},{3,1},{5,3},{7,5},{8,14},{10,8},{12,... | collective-permute-start | bytes 1572872 | tf_op jit(solution)/shard_map/ppermute | solution.py:212
  76.9 0.0 collective-permute-done.5.refs_4_
  76.9 0.0 copy-start.3
  76.9 0.8 copy-done.3
  77.7 10.0 %collective-permute-done.4.refs_6_ = bf16[512,512]{1,0:T(8,128)(2,1)S(1)} collective-permute-done((bf16[512,512]{1,0:T(8,128)(2,1)S(1)}, bf16[512,512]{1,0:T(8,128)(2,1)S(1)}, u32[]{:S(2)}, u32[]{:S(2)}) %collective-permute-start.4) | collective-permute-done | bytes 524320 | tf_op jit(solution)/shard_map/ppermute | solution.py:212
  87.7 0.0 copy-done.5
  87.7 0.8 copy-done.6
  88.5 0.0 collective-permute-done.7.refs_7_
  88.5 0.0 all-to-all-done.2
  88.5 1.3 shard_map.96
  89.8 8.7 %all-to-all-start.3 = ((bf16[16,64,512]{2,1,0:T(8,128)(2,1)}), bf16[16,64,512]{2,1,0:T(8,128)(2,1)S(1)}, u32[]{:S(2)}, u32[]{:S(2)}) async-start(bf16[16,64,512]{2,1,0:T(8,128)(2,1)} %shard_map.96), calls=%async_computation.3 | async-start | bytes 2097152 | tf_op jit(solution)/shard_map/all_to_all | solution.py:249
  98.5 0.1 stack.23.place
  98.6 0.0 all-gather.3.cloned.1.call-done
  98.6 0.0 copy-done.1
  98.6 0.0 copy-done.2
  98.6 0.9 copy-done
  99.5 1.0 copy-done.4
  100.5 9.4 %shard_map.97 = (bf16[512,512]{1,0:T(8,128)(2,1)}, bf16[512,512]{1,0:T(8,128)(2,1)}, f32[512,512]{1,0:T(8,128)}) custom-call(s32[5]{0:T(128)S(1)} %stack.23.place, s32[4]{0:T(128)S(1)} %bitcast.19, s32[4]{0:T(128)S(1)} %copy-done.2, bf16[8,2,512,512]{3,2,1,0:T(8,128)(2,1)} %bitcast.23, bf16[512,512]{1,0:T(8,128)(2,1)S(1)} %collective-permute-done.refs_0_, ...), custom_call_target="tpu_custom_call" | custom-call | flops 4294967296 | bytes 14680064 | tf_op jit(solution)/shard_map/pallas_call | solution.py:190
  110.0 7.3 %collective-permute-start.8 = (bf16[512,512]{1,0:T(8,128)(2,1)}, bf16[512,512]{1,0:T(8,128)(2,1)S(1)}, u32[]{:S(2)}, u32[]{:S(2)}) collective-permute-start(bf16[512,512]{1,0:T(8,128)(2,1)} %get-tuple-element.32), channel_id=1, source_target_pairs={{1,16},{16,1},{3,18},{18,3},{5,20},{20,5},{7,22},{22,7},{9,24},{24... | collective-permute-start | bytes 1572872 | tf_op jit(solution)/shard_map/ppermute | solution.py:251
  117.3 0.1 collective-permute-start.9
  117.4 0.1 broadcast_bitcast_fusion
  117.5 6.9 %all-to-all-done.3.recv = bf16[16,64,512]{2,1,0:T(8,128)(2,1)S(1)} async-done(((bf16[16,64,512]{2,1,0:T(8,128)(2,1)}), bf16[16,64,512]{2,1,0:T(8,128)(2,1)S(1)}, u32[]{:S(2)}, u32[]{:S(2)}) %all-to-all-start.3) | async-done | bytes 1048608 | tf_op jit(solution)/shard_map/all_to_all | solution.py:249
  124.4 1.9 %shard_map.98 = (f32[8,64,512]{2,1,0:T(8,128)}, f32[8,64,512]{2,1,0:T(8,128)}) custom-call(bf16[16,64,512]{2,1,0:T(8,128)(2,1)S(1)} %all-to-all-done.3.recv), custom_call_target="tpu_custom_call" | custom-call | bytes 4194304 | tf_op jit(solution)/shard_map/pallas_call | solution.py:149
  126.3 4.5 %collective-permute-done.8 = bf16[512,512]{1,0:T(8,128)(2,1)S(1)} collective-permute-done((bf16[512,512]{1,0:T(8,128)(2,1)}, bf16[512,512]{1,0:T(8,128)(2,1)S(1)}, u32[]{:S(2)}, u32[]{:S(2)}) %collective-permute-start.8) | collective-permute-done | bytes 524320 | tf_op jit(solution)/shard_map/ppermute | solution.py:251
  130.8 3.8 %collective-permute-done.9 = bf16[512,512]{1,0:T(8,128)(2,1)S(1)} collective-permute-done((bf16[512,512]{1,0:T(8,128)(2,1)}, bf16[512,512]{1,0:T(8,128)(2,1)S(1)}, u32[]{:S(2)}, u32[]{:S(2)}) %collective-permute-start.9) | collective-permute-done | bytes 524320 | tf_op jit(solution)/shard_map/ppermute | solution.py:252
  134.5 2.2 %select_convert_fusion = bf16[512,512]{1,0:T(8,128)(2,1)} fusion(bf16[512,512]{1,0:T(8,128)(2,1)S(1)} %collective-permute-done.9, f32[512,512]{1,0:T(8,128)} %get-tuple-element.31, bf16[512,512]{1,0:T(8,128)(2,1)S(1)} %collective-permute-done.8, pred[512]{0:T(512)(128)(4,1)S(1)} %broadcast_bitcast_fusion), kind=kLoop, calls=%fused_computation | loop fusion | flops 1572864 | bytes 2621952 | tf_op jit(solution)/shard_map/convert_element_type | solution.py:256
  (6 shorter events, 0.1 us)
Async XLA Ops:
  7.2 91.4 %copy-start.1 = (s32[4,1]{0,1:T(1,128)S(1)}, s32[4,1]{0,1:T(1,128)}, u32[]{:S(2)}) copy-start(s32[4,1]{0,1:T(1,128)} %param.12) | copy-start | bytes 52
  7.2 91.4 %copy-start.2 = (s32[4]{0:T(128)S(1)}, s32[4]{0:T(128)}, u32[]{:S(2)}) copy-start(s32[4]{0:T(128)} %live.3) | copy-start | bytes 52
  7.2 91.4 %all-gather.3.cloned.1.call-start = ((), (), s32[]{:S(2)}) async-start(), calls=%async_computation.4 | async-start | bytes 8912896 | tf_op jit(solution)/shard_map/all_gather | solution.py:230
  7.9 21.2 %collective-permute-start = (bf16[512,512]{1,0:T(8,128)(2,1)}, bf16[512,512]{1,0:T(8,128)(2,1)S(1)}, u32[]{:S(2)}, u32[]{:S(2)}) collective-permute-start(bf16[512,512]{1,0:T(8,128)(2,1)} %g_far.1), channel_id=1, source_target_pairs={{0,0},{1,16},{16,1},{17,17},{2,2},{3,18},{18,3},{19,19},{4,4},{5,2... | collective-permute-start | bytes 1572872 | tf_op jit(solution)/shard_map/ppermute | solution.py:231
  29.1 17.5 %collective-permute-start.1 = (bf16[512,512]{1,0:T(8,128)(2,1)S(1)}, bf16[512,512]{1,0:T(8,128)(2,1)S(1)}, u32[]{:S(2)}, u32[]{:S(2)}) collective-permute-start(bf16[512,512]{1,0:T(8,128)(2,1)S(1)} %collective-permute-done.refs_0_), channel_id=1, source_target_pairs={{0,8},{8,0},{1,9},{9,1},{2,10},{10,2},{3,11},{11,3},{4,12},{12,4},... | collective-permute-start | bytes 1572872 | tf_op jit(solution)/shard_map/ppermute | solution.py:220
  29.9 16.7 %collective-permute-start.2 = (bf16[512,512]{1,0:T(8,128)(2,1)S(1)}, bf16[512,512]{1,0:T(8,128)(2,1)S(1)}, u32[]{:S(2)}, u32[]{:S(2)}) collective-permute-start(bf16[512,512]{1,0:T(8,128)(2,1)S(1)} %collective-permute-done.refs_0_), channel_id=1, source_target_pairs={{0,2},{2,4},{4,6},{6,0},{1,3},{3,5},{5,7},{7,1},{8,10},{10,12},{12... | collective-permute-start | bytes 1572872 | tf_op jit(solution)/shard_map/ppermute | solution.py:212
  30.2 16.5 %collective-permute-start.3 = (bf16[512,512]{1,0:T(8,128)(2,1)S(1)}, bf16[512,512]{1,0:T(8,128)(2,1)S(1)}, u32[]{:S(2)}, u32[]{:S(2)}) collective-permute-start(bf16[512,512]{1,0:T(8,128)(2,1)S(1)} %collective-permute-done.refs_0_), channel_id=1, source_target_pairs={{0,6},{2,0},{4,2},{6,4},{1,7},{3,1},{5,3},{7,5},{8,14},{10,8},{12,... | collective-permute-start | bytes 1572872 | tf_op jit(solution)/shard_map/ppermute | solution.py:212
  50.5 38.0 %all-to-all-start.2 = ((bf16[16,32,640]{2,1,0:T(8,128)(2,1)}), bf16[16,32,640]{2,1,0:T(8,128)(2,1)S(1)}, u32[]{:S(2)}, u32[]{:S(2)}) async-start(bf16[16,32,640]{2,1,0:T(8,128)(2,1)} %shard_map.95), calls=%async_computation.2 | async-start | bytes 1310720 | tf_op jit(solution)/shard_map/all_to_all | solution.py:244
  59.9 13.4 %collective-permute-start.6 = (bf16[512,512]{1,0:T(8,128)(2,1)S(1)}, bf16[512,512]{1,0:T(8,128)(2,1)S(1)}, u32[]{:S(2)}, u32[]{:S(2)}) collective-permute-start(bf16[512,512]{1,0:T(8,128)(2,1)S(1)} %collective-permute-done.1.refs_1_), channel_id=1, source_target_pairs={{0,6},{2,0},{4,2},{6,4},{1,7},{3,1},{5,3},{7,5},{8,14},{10,8},{12,... | collective-permute-start | bytes 1572872 | tf_op jit(solution)/shard_map/ppermute | solution.py:212
  62.7 14.2 %collective-permute-start.5 = (bf16[512,512]{1,0:T(8,128)(2,1)S(1)}, bf16[512,512]{1,0:T(8,128)(2,1)S(1)}, u32[]{:S(2)}, u32[]{:S(2)}) collective-permute-start(bf16[512,512]{1,0:T(8,128)(2,1)S(1)} %collective-permute-done.1.refs_1_), channel_id=1, source_target_pairs={{0,2},{2,4},{4,6},{6,0},{1,3},{3,5},{5,7},{7,1},{8,10},{10,12},{12... | collective-permute-start | bytes 1572872 | tf_op jit(solution)/shard_map/ppermute | solution.py:212
  62.7 25.0 %collective-permute-start.4 = (bf16[512,512]{1,0:T(8,128)(2,1)S(1)}, bf16[512,512]{1,0:T(8,128)(2,1)S(1)}, u32[]{:S(2)}, u32[]{:S(2)}) collective-permute-start(bf16[512,512]{1,0:T(8,128)(2,1)S(1)} %collective-permute-done.2.refs_2_), channel_id=1, source_target_pairs={{0,2},{2,4},{4,6},{6,0},{1,3},{3,5},{5,7},{7,1},{8,10},{10,12},{12... | collective-permute-start | bytes 1572872 | tf_op jit(solution)/shard_map/ppermute | solution.py:212
  73.3 14.3 %copy-start.5 = (bf16[512,512]{1,0:T(8,128)(2,1)}, bf16[512,512]{1,0:T(8,128)(2,1)S(1)}, u32[]{:S(2)}) copy-start(bf16[512,512]{1,0:T(8,128)(2,1)S(1)} %collective-permute-done.6.refs_5_) | copy-start | bytes 1572868
  73.3 15.1 %collective-permute-start.7 = (bf16[512,512]{1,0:T(8,128)(2,1)S(1)}, bf16[512,512]{1,0:T(8,128)(2,1)}, u32[]{:S(2)}, u32[]{:S(2)}) collective-permute-start(bf16[512,512]{1,0:T(8,128)(2,1)S(1)} %collective-permute-done.6.refs_5_), channel_id=1, source_target_pairs={{0,6},{2,0},{4,2},{6,4},{1,7},{3,1},{5,3},{7,5},{8,14},{10,8},{12,... | collective-permute-start | bytes 1572872 | tf_op jit(solution)/shard_map/ppermute | solution.py:212
  76.9 0.8 copy-start.3
  87.7 0.8 copy-start.6
  89.8 34.6 %all-to-all-start.3 = ((bf16[16,64,512]{2,1,0:T(8,128)(2,1)}), bf16[16,64,512]{2,1,0:T(8,128)(2,1)S(1)}, u32[]{:S(2)}, u32[]{:S(2)}) async-start(bf16[16,64,512]{2,1,0:T(8,128)(2,1)} %shard_map.96), calls=%async_computation.3 | async-start | bytes 2097152 | tf_op jit(solution)/shard_map/all_to_all | solution.py:249
  98.6 0.9 copy-start
  99.5 1.0 copy-start.4
  110.0 20.8 %collective-permute-start.8 = (bf16[512,512]{1,0:T(8,128)(2,1)}, bf16[512,512]{1,0:T(8,128)(2,1)S(1)}, u32[]{:S(2)}, u32[]{:S(2)}) collective-permute-start(bf16[512,512]{1,0:T(8,128)(2,1)} %get-tuple-element.32), channel_id=1, source_target_pairs={{1,16},{16,1},{3,18},{18,3},{5,20},{20,5},{7,22},{22,7},{9,24},{24... | collective-permute-start | bytes 1572872 | tf_op jit(solution)/shard_map/ppermute | solution.py:251
  117.3 17.2 %collective-permute-start.9 = (bf16[512,512]{1,0:T(8,128)(2,1)}, bf16[512,512]{1,0:T(8,128)(2,1)S(1)}, u32[]{:S(2)}, u32[]{:S(2)}) collective-permute-start(bf16[512,512]{1,0:T(8,128)(2,1)} %get-tuple-element.33), channel_id=1, source_target_pairs={{0,1},{1,17},{16,0},{17,16},{2,3},{3,19},{18,2},{19,18},{4,5},{5,2... | collective-permute-start | bytes 1572872 | tf_op jit(solution)/shard_map/ppermute | solution.py:252
Sparse Core Ops, SparseCore 0:
  9.9 69.2 all-gather.2

commit v3 on v2

--- a/solution.py
+++ b/solution.py
@@ -120,59 +120,78 @@
     role = got[:, COLS:].astype(f32)
     pick = (role == (lane // GROUP).astype(f32)) & (lane % GROUP == row % GROUP)
     total = dot(pick.astype(f32).astype(bf16), got[:, :COLS], 0, 0)
-    total = (scale * total[: ROLES * GROUP, :]).astype(bf16)
-    for i in range(Z * XH):
-        out[i] = total
+    out[...] = (scale * total[: ROLES * GROUP, :]).astype(bf16)
 
 
 def sum_parts(recv, scale):
     rows = Z * XH * BLOCKS * GROUP
     return pl.pallas_call(
         functools.partial(sum_kernel, scale),
-        out_shape=jax.ShapeDtypeStruct((Z * XH, ROLES * GROUP, COLS), bf16),
+        out_shape=jax.ShapeDtypeStruct((ROLES * GROUP, COLS), bf16),
         compiler_params=pltpu.CompilerParams(vmem_limit_bytes=16 << 20),
         cost_estimate=pl.CostEstimate(flops=2 * rows * PAD * COLS, bytes_accessed=2 << 20, transcendentals=0),
     )(recv.reshape(rows, COLS + PAD))
 
 
-def spread_kernel(recv, up, down):
-    for half in range(2):
-        ups, downs = [], []
-        for z in range(Z):
-            ups.append(recv[2 * z].astype(f32)[GROUP * half : GROUP * (half + 1), :])
-            downs.append(recv[2 * z + 1].astype(f32)[GROUP * half : GROUP * (half + 1), :])
-        up[half] = jnp.concatenate(ups, axis=0)
-        down[half] = jnp.concatenate(downs, axis=0)
-
-
-def spread(recv):
+def spread_kernel(place, *refs):
+    pieces, up, down = refs[:Z], refs[Z], refs[Z + 1]
+    for off, piece in zip(OFFSETS, pieces):
+        z = lax.rem(place[0] + (off + Z), Z)
+        at = pl.ds(pl.multiple_of(GROUP * z, GROUP), GROUP)
+        for o, out in enumerate((up, down)):
+            rows = piece[o].astype(f32)
+            for k in range(ROLES):
+                out[k, at, :] = rows[GROUP * k : GROUP * (k + 1), :]
+
+
+def spread(place, pieces):
+    spec = pltpu.PrefetchScalarGridSpec(
+        num_scalar_prefetch=1,
+        grid=(1,),
+        in_specs=[whole((2, ROLES * GROUP, COLS))] * Z,
+        out_specs=[whole((ROLES, RANK, COLS))] * 2,
+    )
     return pl.pallas_call(
         spread_kernel,
-        grid=(ROLES // 2,),
-        in_specs=[pl.BlockSpec((Z * XH, 2 * GROUP, COLS), lambda i: (0, i, 0))],
-        out_specs=[pl.BlockSpec((2, RANK, COLS), lambda i: (i, 0, 0))] * 2,
+        grid_spec=spec,
         out_shape=[jax.ShapeDtypeStruct((ROLES, RANK, COLS), f32)] * 2,
         compiler_params=pltpu.CompilerParams(vmem_limit_bytes=VMEM),
         cost_estimate=pl.CostEstimate(flops=0, bytes_accessed=4 << 20, transcendentals=0),
-    )(recv)
+    )(place, *pieces)
 
 
 def base_kernel(place, roles, live, wide, *refs):
-    pieces, (lb, down), (far, near, own), (sheets, total, sems) = refs[:8], refs[8:10], refs[10:13], refs[13:]
+    pieces, (lb_far, down_far), (far, near, own) = refs[:Z], refs[Z : Z + 2], refs[Z + 2 : Z + 5]
+    held, sheets, total, lb, down, sems = refs[Z + 5 :]
     x_hi, x_lo, y, core = place[1], place[2], place[3], place[4]
     columns = (x_lo, 1 - x_lo, x_lo, x_lo, 1 - x_lo, 1 - x_lo, x_lo, 1 - x_lo)
     steps = (0, 0, -1, 1, -1, 1, 2, 2)
-    blocks = [(p, column, y + Y + step) for p, column, step in zip(pieces, columns, steps)]
     copies = []
-    for s, (_, column, row) in enumerate(blocks):
-        j = column * Y + lax.rem(row, Y)
-        copies.append(pltpu.make_async_copy(wide.at[j], sheets.at[s], sems.at[s]))
-        copies[s].start()
-    for s, (block, _, _) in enumerate(blocks):
-        copies[s].wait()
+    for s, (piece, column, step) in enumerate(zip(pieces, columns, steps)):
+        j = column * Y + lax.rem(y + Y + step, Y)
+        copies.append(
+            (
+                pltpu.make_async_copy(piece, held.at[s], sems.at[s, 0]),
+                pltpu.make_async_copy(wide.at[j], sheets.at[s], sems.at[s, 1]),
+            )
+        )
+    copies.append(
+        (
+            pltpu.make_async_copy(lb_far, lb, sems.at[Z, 0]),
+            pltpu.make_async_copy(down_far, down, sems.at[Z, 1]),
+        )
+    )
+    for pair in copies:
+        for copy in pair:
+            copy.start()
+    for s in range(Z):
+        for copy in copies[s]:
+            copy.wait()
         for half in range(C):
-            term = dot(block[...], sheets[s, half], 1, 1)
+            term = dot(held[s], sheets[s, half], 1, 1)
             total[half] = term if s == 0 else total[half] + term
+    for copy in copies[Z]:
+        copy.wait()
 
     mine = core == x_hi
     far[...] = total[1 - core].astype(bf16)
@@ -186,18 +205,23 @@
 
 
 def base_parts(place, roles, live, wide, *pieces):
-    here = pl.BlockSpec(memory_space=pltpu.VMEM)
-    return pl.pallas_call(
-        base_kernel,
-        in_specs=[pl.BlockSpec(memory_space=pltpu.SMEM)] * 3
-        + [pl.BlockSpec(memory_space=pl.ANY)]
-        + [here] * len(pieces),
-        out_specs=[here] * 3,
+    spec = pltpu.PrefetchScalarGridSpec(
+        num_scalar_prefetch=3,
+        grid=(1,),
+        in_specs=[pl.BlockSpec(memory_space=pl.ANY)] * (1 + len(pieces)),
+        out_specs=[pl.BlockSpec((ROWS, COLS), lambda i, p, r, l: (0, 0))] * 3,
         scratch_shapes=[
+            pltpu.VMEM((Z, ROWS, COLS), bf16),
             pltpu.VMEM((Z, C, COLS, COLS), bf16),
             pltpu.VMEM((C, ROWS, COLS), f32),
-            pltpu.SemaphoreType.DMA((Z,)),
+            pltpu.VMEM((ROWS, 2 * RANK), bf16),
+            pltpu.VMEM((ROLES, RANK, COLS), bf16),
+            pltpu.SemaphoreType.DMA((Z + 1, 2)),
         ],
+    )
+    return pl.pallas_call(
+        base_kernel,
+        grid_spec=spec,
         out_shape=[
             jax.ShapeDtypeStruct((ROWS, COLS), bf16),
             jax.ShapeDtypeStruct((ROWS, COLS), bf16),
@@ -241,19 +265,27 @@
 
     up2, beside_down1 = shift(up1, "y", Y, 1), shift(beside, "y", Y, -1)
     outer = outer_parts(roles, live, lb, attention_output, grad_out)
+    up2, beside_down1, beside, _ = tie(up2, beside_down1, beside, outer)
     outer = lax.all_to_all(outer, FS, 0, 0)
     beside_up1, beside_down2 = shift(beside, "y", Y, 1), shift(beside_down1, "y", Y, -1)
-    outer, up2, beside_up1, beside_down2 = tie(outer, up2, beside_up1, beside_down2)
     pieces = [turned, beside, up1, down1, beside_up1, beside_down1, up2, beside_down2]
 
-    total = lax.all_to_all(sum_parts(outer, grad_scale), FS, 0, 0)
+    total = sum_parts(outer, grad_scale)
+    other = trade(total, "xh", XH, 1)
     far, near, own = base_parts(place, roles, live, wide, *pieces, lb, adapter_down)
+    total, other, far, near, own = tie(total, other, far, near, own)
+
     far = lax.ppermute(far, ("xh", "c"), [(1, 2), (2, 1)])
     near = lax.ppermute(near, ("xh", "c"), [(0, 1), (1, 3), (2, 0), (3, 2)])
-    total, own = tie(total, own)
-    up_gradient, down_gradient = spread(total)
+    pair = jnp.where(place[1] == 0, jnp.stack([total, other]), jnp.stack([other, total]))
+    s1, t1 = shift(pair, "z", Z, 1), shift(pair, "z", Z, -1)
+    s2, t2 = shift(pair, "z", Z, 2), shift(pair, "z", Z, -2)
+    s3, t3 = shift(s2, "z", Z, 1), shift(t2, "z", Z, -1)
+    s4 = shift(s2, "z", Z, 2)
     token_live = jnp.repeat(live, BLOCK)[:, None] > 0
     input_gradient = jnp.where(token_live, own + far.astype(f32) + near.astype(f32), 0.0).astype(bf16)
+    input_gradient, s3, t3, s4 = tie(input_gradient, s3, t3, s4)
+    up_gradient, down_gradient = spread(place, [pair, s1, t1, s2, t2, s3, t3, s4])
     return (input_gradient, jnp.transpose(down_gradient, (0, 2, 1)), up_gradient)
 
 

time: 144 us -> 134 us (0.931)
  waiting for transfers between devices: 36.5 us -> 25 us
  starting transfers between devices: 41.4 us -> 45.6 us
  Pallas kernels: 19.8 us -> 18 us
    ppermute x6 -> x13, starting transfers between devices: 8.95 us -> 21.5 us  [shift(): return lax.ppermute(x, axis, [(i, (i + step) % size) for i in range(size)])]
    all_to_all x1 -> x0, starting transfers between devices: 8.69 us -> none  [shards(): total = lax.all_to_all(sum_parts(outer, grad_scale), FS, 0, 0)]
    all_to_all x1 -> x0, waiting for transfers between devices: 6.93 us -> none  [shards(): total = lax.all_to_all(sum_parts(outer, grad_scale), FS, 0, 0)]
    all_to_all x1, waiting for transfers between devices: 0.01 us -> 6.71 us  [shards(): outer = lax.all_to_all(outer, FS, 0, 0)]
    ppermute x1, waiting for transfers between devices: 4.5 us -> 0.01 us  [shards(): far = lax.ppermute(far, ('xh', 'c'), [(1, 2), (2, 1)])]
    ppermute x1, waiting for transfers between devices: 3.76 us -> 0.01 us  [shards(): near = lax.ppermute(near, ('xh', 'c'), [(0, 1), (1, 3), (2, 0), (3, 2)])]
    ppermute x6 -> x13, waiting for transfers between devices: 20.7 us -> 17.6 us  [shift(): return lax.ppermute(x, axis, [(i, (i + step) % size) for i in range(size)])]
    ppermute x1, starting transfers between devices: 7.31 us -> 5.17 us  [shards(): far = lax.ppermute(far, ('xh', 'c'), [(1, 2), (2, 1)])]
  transfers between devices with their start and end apart: 13 -> 20, of which waited for: 5 -> 4; matrix products, arithmetic and copies ran while one was open for 0% -> 2% of each run, Pallas kernels for 14% -> 12%
where the time goes in v3:
time: 134 us
  starting transfers between devices  45.6 us (34%)
  blocking collectives  25.7 us (19%)
  waiting for transfers between devices  25 us (19%)
  Pallas kernels  18 us (13%)
  between operations  14.2 us (11%)
  local copies, waits for them, and re-layouts  3.18 us (2%)
  other arithmetic  2.3 us (2%)
    ppermute x13, starting transfers between devices, shift(): return lax.ppermute(x, axis, [(i, (i + step) % size) for i in range(size)])  21.5 us
    ppermute x13, waiting for transfers between devices, shift(): return lax.ppermute(x, axis, [(i, (i + step) % size) for i in range(size)])  17.6 us
    all_to_all x1, blocking collectives, shards(): lax.all_to_all(jnp.broadcast_to(mine[None], (16,) + mine.shape), TP, 0, 0)  13.9 us
    all_to_all x1, blocking collectives, shards(): ranks = lax.all_to_all(ranks.reshape(16, ROWS // 16, 2 * RANK), TP, 0, 0)  11.8 us
    all_to_all x1, starting transfers between devices, shards(): outer = lax.all_to_all(outer, FS, 0, 0)  9.47 us
    pallas_call x1, Pallas kernels, base_parts(): pl.pallas_call(base_kernel, grid_spec=spec, out_shape=[jax.ShapeDtypeStru...  8.49 us
    all_to_all x1, waiting for transfers between devices, shards(): outer = lax.all_to_all(outer, FS, 0, 0)  6.71 us
    ppermute x1, starting transfers between devices, shards(): lax.ppermute(grad_out, ('xh', 'c'), [(0, 0), (1, 2), (2, 1), (3, 3)])  6.04 us
  transfers between devices with their start and end apart: 20, of which 4 were waited for; matrix products, arithmetic and copies ran while one was open for 2% of the time, Pallas kernels for 12%

profile of v3, /device:TPU:1, one launch (start us, length us, event | category | flops | bytes accessed | tf_op | source)
XLA Modules:
  0.0 133.9 jit_solution(4228161880104296561)
XLA Ops:
  7.2 0.0 all-gather.3.cloned.1.call-start
  7.2 0.7 all-gather.3.cloned.1.call-update
  7.9 6.0 %collective-permute-start = (bf16[512,512]{1,0:T(8,128)(2,1)}, bf16[512,512]{1,0:T(8,128)(2,1)S(1)}, u32[]{:S(2)}, u32[]{:S(2)}) collective-permute-start(bf16[512,512]{1,0:T(8,128)(2,1)} %g_far.1), channel_id=1, source_target_pairs={{0,0},{1,16},{16,1},{17,17},{2,2},{3,18},{18,3},{19,19},{4,4},{5,2... | collective-permute-start | bytes 1572872 | tf_op jit(solution)/shard_map/ppermute | solution.py:255
  13.9 3.4 %shard_map.94 = f32[512,128]{1,0:T(8,128)} custom-call(s32[4]{0:T(128)} %bitcast.20, bf16[512,512]{1,0:T(8,128)(2,1)} %att_far.1, bf16[512,512]{1,0:T(8,128)(2,1)} %g_far.1, bf16[8,64,512]{2,1,0:T(8,128)(2,1)} %bitcast.24, bf16[8,64,512]{2,1,0:T(8,128)(2,1)} %up.1), custom_call_target="tpu_custom_call" | custom-call | flops 67108864 | bytes 2097152 | tf_op jit(solution)/shard_map/pallas_call | solution.py:59
  17.3 11.8 %all_to_all.15 = f32[16,32,128]{2,1,0:T(8,128)S(1)} all-to-all(f32[16,32,128]{2,1,0:T(8,128)} %bitcast.23), channel_id=1, replica_groups=mesh['z'=8,'xh'=2,'xl'=2,'y'=4,'c'=2] {'xl','y','c'}, dimensions={0} | all-to-all | bytes 524288 | tf_op jit(solution)/shard_map/all_to_all | solution.py:257
  29.1 0.0 collective-permute-done.refs_0_
  29.1 0.8 collective-permute-start.1
  29.9 0.2 collective-permute-start.2
  30.1 2.5 %collective-permute-start.3 = (bf16[512,512]{1,0:T(8,128)(2,1)S(1)}, bf16[512,512]{1,0:T(8,128)(2,1)S(1)}, u32[]{:S(2)}, u32[]{:S(2)}) collective-permute-start(bf16[512,512]{1,0:T(8,128)(2,1)S(1)} %collective-permute-done.refs_0_), channel_id=1, source_target_pairs={{0,6},{2,0},{4,2},{6,4},{1,7},{3,1},{5,3},{7,5},{8,14},{10,8},{12,... | collective-permute-start | bytes 1572872 | tf_op jit(solution)/shard_map/ppermute | solution.py:236
  32.6 13.9 %all_to_all.16 = bf16[16,32,128]{2,1,0:T(8,128)(2,1)} all-to-all(bf16[16,32,128]{2,1,0:T(8,128)(2,1)S(1)} %broadcast_in_dim.23), channel_id=1, replica_groups=mesh['z'=8,'xh'=2,'xl'=2,'y'=4,'c'=2] {'xl','y','c'}, dimensions={0} | all-to-all | bytes 262144 | tf_op jit(solution)/shard_map/all_to_all | solution.py:263
  46.6 0.0 collective-permute-done.1.refs_1_
  46.6 3.8 %shard_map.95 = bf16[16,32,640]{2,1,0:T(8,128)(2,1)} custom-call(s32[4]{0:T(128)} %bitcast.21, s32[4]{0:T(128)} %live.3, bf16[512,128]{1,0:T(8,128)(2,1)} %bitcast.17, bf16[512,512]{1,0:T(8,128)(2,1)} %att_far.1, bf16[512,512]{1,0:T(8,128)(2,1)} %g_far.1), custom_call_target="tpu_custom_call" | custom-call | flops 67108864 | bytes 2097152 | tf_op jit(solution)/shard_map/pallas_call | solution.py:98
  50.4 9.5 %all-to-all-start.2 = ((bf16[16,32,640]{2,1,0:T(8,128)(2,1)}), bf16[16,32,640]{2,1,0:T(8,128)(2,1)S(1)}, u32[]{:S(2)}, u32[]{:S(2)}) async-start(bf16[16,32,640]{2,1,0:T(8,128)(2,1)} %shard_map.95), calls=%async_computation.2 | async-start | bytes 1310720 | tf_op jit(solution)/shard_map/all_to_all | solution.py:269
  59.9 0.6 collective-permute-start.5
  60.5 2.3 %collective-permute-start.6 = (bf16[512,512]{1,0:T(8,128)(2,1)S(1)}, bf16[512,512]{1,0:T(8,128)(2,1)}, u32[]{:S(2)}, u32[]{:S(2)}) collective-permute-start(bf16[512,512]{1,0:T(8,128)(2,1)S(1)} %collective-permute-done.1.refs_1_), channel_id=1, source_target_pairs={{0,6},{2,0},{4,2},{6,4},{1,7},{3,1},{5,3},{7,5},{8,14},{10,8},{12,... | collective-permute-start | bytes 1572872 | tf_op jit(solution)/shard_map/ppermute | solution.py:236
  62.8 11.4 %collective-permute-done.5.refs_6_ = bf16[512,512]{1,0:T(8,128)(2,1)S(1)} collective-permute-done((bf16[512,512]{1,0:T(8,128)(2,1)S(1)}, bf16[512,512]{1,0:T(8,128)(2,1)S(1)}, u32[]{:S(2)}, u32[]{:S(2)}) %collective-permute-start.5) | collective-permute-done | bytes 524320 | tf_op jit(solution)/shard_map/ppermute | solution.py:236
  74.2 0.8 copy-done.3
  75.0 0.0 collective-permute-done.6.refs_5_
  75.0 0.0 collective-permute-start.7
  75.0 2.6 %collective-permute-start.8 = (bf16[512,512]{1,0:T(8,128)(2,1)}, bf16[512,512]{1,0:T(8,128)(2,1)}, u32[]{:S(2)}, u32[]{:S(2)}) collective-permute-start(bf16[512,512]{1,0:T(8,128)(2,1)} %collective-permute-done.6.refs_5_), channel_id=1, source_target_pairs={{0,6},{2,0},{4,2},{6,4},{1,7},{3,1},{5,3},{7,5},{8,14},{10,8},{12,... | collective-permute-start | bytes 1572872 | tf_op jit(solution)/shard_map/ppermute | solution.py:236
  77.7 0.1 stack.37.place
  77.7 6.7 %all-to-all-done.2 = bf16[16,32,640]{2,1,0:T(8,128)(2,1)S(1)} async-done(((bf16[16,32,640]{2,1,0:T(8,128)(2,1)}), bf16[16,32,640]{2,1,0:T(8,128)(2,1)S(1)}, u32[]{:S(2)}, u32[]{:S(2)}) %all-to-all-start.2) | async-done | bytes 655392 | tf_op jit(solution)/shard_map/all_to_all | solution.py:269
  84.5 0.3 shard_map.96
  84.7 0.3 collective-permute-start.4
  85.0 3.2 %collective-permute-done.7.refs_4_ = bf16[512,512]{1,0:T(8,128)(2,1)S(1)} collective-permute-done((bf16[512,512]{1,0:T(8,128)(2,1)S(1)}, bf16[512,512]{1,0:T(8,128)(2,1)S(1)}, u32[]{:S(2)}, u32[]{:S(2)}) %collective-permute-start.7) | collective-permute-done | bytes 524320 | tf_op jit(solution)/shard_map/ppermute | solution.py:236
  88.3 0.9 copy-done
  89.2 0.7 copy-done.1
  89.8 0.7 copy-done.2
  90.5 8.5 %shard_map.97 = (bf16[512,512]{1,0:T(8,128)(2,1)S(1)}, bf16[512,512]{1,0:T(8,128)(2,1)S(1)}, f32[512,512]{1,0:T(8,128)}) custom-call(s32[5]{0:T(128)S(1)} %stack.37.place, s32[4]{0:T(128)S(1)} %bitcast.22, s32[4]{0:T(128)S(1)} %copy-done.2, bf16[8,2,512,512]{3,2,1,0:T(8,128)(2,1)} %bitcast.27, bf16[512,512]{1,0:T(8,128)(2,1)S(1)} %collective-permute-done.refs_0_, ...), custom_call_target="tpu_custom_call" | custom-call | flops 4294967296 | bytes 14680064 | tf_op jit(solution)/shard_map/pallas_call | solution.py:222
  99.0 0.0 collective-permute-done.4
  99.0 2.2 %collective-permute-start.10 = (bf16[512,512]{1,0:T(8,128)(2,1)S(1)}, bf16[512,512]{1,0:T(8,128)(2,1)S(1)}, u32[]{:S(2)}, u32[]{:S(2)}) collective-permute-start(bf16[512,512]{1,0:T(8,128)(2,1)S(1)} %get-tuple-element.40), channel_id=1, source_target_pairs={{0,1},{1,17},{16,0},{17,16},{2,3},{3,19},{18,2},{19,18},{4,5},{5,2... | collective-permute-start | bytes 1572872 | tf_op jit(solution)/shard_map/ppermute | solution.py:279
  101.2 5.2 %collective-permute-start.9 = (bf16[512,512]{1,0:T(8,128)(2,1)S(1)}, bf16[512,512]{1,0:T(8,128)(2,1)S(1)}, u32[]{:S(2)}, u32[]{:S(2)}) collective-permute-start(bf16[512,512]{1,0:T(8,128)(2,1)S(1)} %get-tuple-element.39), channel_id=1, source_target_pairs={{1,16},{16,1},{3,18},{18,3},{5,20},{20,5},{7,22},{22,7},{9,24},{24... | collective-permute-start | bytes 1572872 | tf_op jit(solution)/shard_map/ppermute | solution.py:278
  106.4 2.0 %collective-permute-start.11 = (bf16[2,64,512]{2,1,0:T(8,128)(2,1)S(1)}, bf16[2,64,512]{2,1,0:T(8,128)(2,1)S(1)}, u32[]{:S(2)}, u32[]{:S(2)}) collective-permute-start(bf16[2,64,512]{2,1,0:T(8,128)(2,1)S(1)} %maximum_select_fusion.refs_0_), channel_id=1, source_target_pairs={{0,64},{32,96},{64,128},{96,160},{128,192},{160,224},{192,0},{224,... | collective-permute-start | bytes 393224 | tf_op jit(solution)/shard_map/ppermute | solution.py:236
  108.4 1.8 %collective-permute-start.13 = (bf16[2,64,512]{2,1,0:T(8,128)(2,1)S(1)}, bf16[2,64,512]{2,1,0:T(8,128)(2,1)S(1)}, u32[]{:S(2)}, u32[]{:S(2)}) collective-permute-start(bf16[2,64,512]{2,1,0:T(8,128)(2,1)S(1)} %maximum_select_fusion.refs_0_), channel_id=1, source_target_pairs={{0,192},{32,224},{64,0},{96,32},{128,64},{160,96},{192,128},{224,1... | collective-permute-start | bytes 393224 | tf_op jit(solution)/shard_map/ppermute | solution.py:236
  110.3 0.1 broadcast_bitcast_fusion
  110.3 0.9 collective-permute-start.16
  111.2 2.9 %collective-permute-done.11.refs_3_ = bf16[2,64,512]{2,1,0:T(8,128)(2,1)S(1)} collective-permute-done((bf16[2,64,512]{2,1,0:T(8,128)(2,1)S(1)}, bf16[2,64,512]{2,1,0:T(8,128)(2,1)S(1)}, u32[]{:S(2)}, u32[]{:S(2)}) %collective-permute-start.11) | collective-permute-done | bytes 131104 | tf_op jit(solution)/shard_map/ppermute | solution.py:236
  114.1 1.9 %collective-permute-start.17 = (bf16[2,64,512]{2,1,0:T(8,128)(2,1)S(1)}, bf16[2,64,512]{2,1,0:T(8,128)(2,1)S(1)}, u32[]{:S(2)}, u32[]{:S(2)}) collective-permute-start(bf16[2,64,512]{2,1,0:T(8,128)(2,1)S(1)} %maximum_select_fusion.refs_0_), channel_id=1, source_target_pairs={{0,224},{32,0},{64,32},{96,64},{128,96},{160,128},{192,160},{224,1... | collective-permute-start | bytes 393224 | tf_op jit(solution)/shard_map/ppermute | solution.py:236
  116.1 0.0 collective-permute-done.13.refs_4_
  116.1 1.5 %collective-permute-start.12 = (bf16[2,64,512]{2,1,0:T(8,128)(2,1)S(1)}, bf16[2,64,512]{2,1,0:T(8,128)(2,1)S(1)}, u32[]{:S(2)}, u32[]{:S(2)}) collective-permute-start(bf16[2,64,512]{2,1,0:T(8,128)(2,1)S(1)} %collective-permute-done.11.refs_3_), channel_id=1, source_target_pairs={{0,32},{32,64},{64,96},{96,128},{128,160},{160,192},{192,224},{224... | collective-permute-start | bytes 393224 | tf_op jit(solution)/shard_map/ppermute | solution.py:236
  117.5 0.0 collective-permute-done.10
  117.5 2.6 %collective-permute-start.15 = (bf16[2,64,512]{2,1,0:T(8,128)(2,1)S(1)}, bf16[2,64,512]{2,1,0:T(8,128)(2,1)S(1)}, u32[]{:S(2)}, u32[]{:S(2)}) collective-permute-start(bf16[2,64,512]{2,1,0:T(8,128)(2,1)S(1)} %collective-permute-done.11.refs_3_), channel_id=1, source_target_pairs={{0,64},{32,96},{64,128},{96,160},{128,192},{160,224},{192,0},{224,... | collective-permute-start | bytes 393224 | tf_op jit(solution)/shard_map/ppermute | solution.py:236
  120.1 2.7 %collective-permute-start.14 = (bf16[2,64,512]{2,1,0:T(8,128)(2,1)S(1)}, bf16[2,64,512]{2,1,0:T(8,128)(2,1)S(1)}, u32[]{:S(2)}, u32[]{:S(2)}) collective-permute-start(bf16[2,64,512]{2,1,0:T(8,128)(2,1)S(1)} %collective-permute-done.13.refs_4_), channel_id=1, source_target_pairs={{0,224},{32,0},{64,32},{96,64},{128,96},{160,128},{192,160},{224,1... | collective-permute-start | bytes 393224 | tf_op jit(solution)/shard_map/ppermute | solution.py:236
  122.8 2.2 %select_convert_fusion = bf16[512,512]{1,0:T(8,128)(2,1)} fusion(bf16[512,512]{1,0:T(8,128)(2,1)S(1)} %collective-permute-done.10, f32[512,512]{1,0:T(8,128)} %get-tuple-element.38, bf16[512,512]{1,0:T(8,128)(2,1)S(1)} %collective-permute-done.9, pred[512]{0:T(512)(128)(4,1)S(1)} %broadcast_bitcast_fusion), kind=kLoop, calls=%fused_computation | loop fusion | flops 1572864 | bytes 2621952 | tf_op jit(solution)/shard_map/convert_element_type | solution.py:286
  125.0 0.0 collective-permute-done.15.refs_7_
  125.0 0.0 collective-permute-done.16.refs_1_
  125.0 0.0 collective-permute-done.17.refs_2_
  125.0 2.0 %shard_map.98 = (f32[8,64,512]{2,1,0:T(8,128)}, f32[8,64,512]{2,1,0:T(8,128)}) custom-call(s32[5]{0:T(128)S(1)} %stack.37.place, bf16[2,64,512]{2,1,0:T(8,128)(2,1)S(1)} %maximum_select_fusion.refs_0_, bf16[2,64,512]{2,1,0:T(8,128)(2,1)S(1)} %collective-permute-done.16.refs_1_, bf16[2,64,512]{2,1,0:T(8,128)(2,1)S(1)} %collective-permute-done.17.refs_2_, ...), custom_call_target="tpu_custom_call" | custom-call | bytes 4194304 | tf_op jit(solution)/shard_map/pallas_call | solution.py:154
  (15 shorter events, 0.1 us)
Async XLA Ops:
  7.2 81.1 %all-gather.3.cloned.1.call-start = ((), (), s32[]{:S(2)}) async-start(), calls=%async_computation.3 | async-start | bytes 8912896 | tf_op jit(solution)/shard_map/all_gather | solution.py:254
  7.9 21.2 %collective-permute-start = (bf16[512,512]{1,0:T(8,128)(2,1)}, bf16[512,512]{1,0:T(8,128)(2,1)S(1)}, u32[]{:S(2)}, u32[]{:S(2)}) collective-permute-start(bf16[512,512]{1,0:T(8,128)(2,1)} %g_far.1), channel_id=1, source_target_pairs={{0,0},{1,16},{16,1},{17,17},{2,2},{3,18},{18,3},{19,19},{4,4},{5,2... | collective-permute-start | bytes 1572872 | tf_op jit(solution)/shard_map/ppermute | solution.py:255
  29.1 17.5 %collective-permute-start.1 = (bf16[512,512]{1,0:T(8,128)(2,1)S(1)}, bf16[512,512]{1,0:T(8,128)(2,1)S(1)}, u32[]{:S(2)}, u32[]{:S(2)}) collective-permute-start(bf16[512,512]{1,0:T(8,128)(2,1)S(1)} %collective-permute-done.refs_0_), channel_id=1, source_target_pairs={{0,8},{8,0},{1,9},{9,1},{2,10},{10,2},{3,11},{11,3},{4,12},{12,4},... | collective-permute-start | bytes 1572872 | tf_op jit(solution)/shard_map/ppermute | solution.py:244
  29.9 16.7 %collective-permute-start.2 = (bf16[512,512]{1,0:T(8,128)(2,1)S(1)}, bf16[512,512]{1,0:T(8,128)(2,1)S(1)}, u32[]{:S(2)}, u32[]{:S(2)}) collective-permute-start(bf16[512,512]{1,0:T(8,128)(2,1)S(1)} %collective-permute-done.refs_0_), channel_id=1, source_target_pairs={{0,2},{2,4},{4,6},{6,0},{1,3},{3,5},{5,7},{7,1},{8,10},{10,12},{12... | collective-permute-start | bytes 1572872 | tf_op jit(solution)/shard_map/ppermute | solution.py:236
  30.1 16.5 %collective-permute-start.3 = (bf16[512,512]{1,0:T(8,128)(2,1)S(1)}, bf16[512,512]{1,0:T(8,128)(2,1)S(1)}, u32[]{:S(2)}, u32[]{:S(2)}) collective-permute-start(bf16[512,512]{1,0:T(8,128)(2,1)S(1)} %collective-permute-done.refs_0_), channel_id=1, source_target_pairs={{0,6},{2,0},{4,2},{6,4},{1,7},{3,1},{5,3},{7,5},{8,14},{10,8},{12,... | collective-permute-start | bytes 1572872 | tf_op jit(solution)/shard_map/ppermute | solution.py:236
  50.4 34.0 %all-to-all-start.2 = ((bf16[16,32,640]{2,1,0:T(8,128)(2,1)}), bf16[16,32,640]{2,1,0:T(8,128)(2,1)S(1)}, u32[]{:S(2)}, u32[]{:S(2)}) async-start(bf16[16,32,640]{2,1,0:T(8,128)(2,1)} %shard_map.95), calls=%async_computation.2 | async-start | bytes 1310720 | tf_op jit(solution)/shard_map/all_to_all | solution.py:269
  59.9 14.3 %collective-permute-start.5 = (bf16[512,512]{1,0:T(8,128)(2,1)S(1)}, bf16[512,512]{1,0:T(8,128)(2,1)S(1)}, u32[]{:S(2)}, u32[]{:S(2)}) collective-permute-start(bf16[512,512]{1,0:T(8,128)(2,1)S(1)} %collective-permute-done.2.refs_2_), channel_id=1, source_target_pairs={{0,2},{2,4},{4,6},{6,0},{1,3},{3,5},{5,7},{7,1},{8,10},{10,12},{12... | collective-permute-start | bytes 1572872 | tf_op jit(solution)/shard_map/ppermute | solution.py:236
  60.5 14.5 %collective-permute-start.6 = (bf16[512,512]{1,0:T(8,128)(2,1)S(1)}, bf16[512,512]{1,0:T(8,128)(2,1)}, u32[]{:S(2)}, u32[]{:S(2)}) collective-permute-start(bf16[512,512]{1,0:T(8,128)(2,1)S(1)} %collective-permute-done.1.refs_1_), channel_id=1, source_target_pairs={{0,6},{2,0},{4,2},{6,4},{1,7},{3,1},{5,3},{7,5},{8,14},{10,8},{12,... | collective-permute-start | bytes 1572872 | tf_op jit(solution)/shard_map/ppermute | solution.py:236
  74.2 0.8 copy-start.3
  75.0 13.3 %collective-permute-start.7 = (bf16[512,512]{1,0:T(8,128)(2,1)S(1)}, bf16[512,512]{1,0:T(8,128)(2,1)S(1)}, u32[]{:S(2)}, u32[]{:S(2)}) collective-permute-start(bf16[512,512]{1,0:T(8,128)(2,1)S(1)} %collective-permute-done.1.refs_1_), channel_id=1, source_target_pairs={{0,2},{2,4},{4,6},{6,0},{1,3},{3,5},{5,7},{7,1},{8,10},{10,12},{12... | collective-permute-start | bytes 1572872 | tf_op jit(solution)/shard_map/ppermute | solution.py:236
  75.0 13.2 %collective-permute-start.8 = (bf16[512,512]{1,0:T(8,128)(2,1)}, bf16[512,512]{1,0:T(8,128)(2,1)}, u32[]{:S(2)}, u32[]{:S(2)}) collective-permute-start(bf16[512,512]{1,0:T(8,128)(2,1)} %collective-permute-done.6.refs_5_), channel_id=1, source_target_pairs={{0,6},{2,0},{4,2},{6,4},{1,7},{3,1},{5,3},{7,5},{8,14},{10,8},{12,... | collective-permute-start | bytes 1572872 | tf_op jit(solution)/shard_map/ppermute | solution.py:236
  84.7 14.3 %collective-permute-start.4 = (bf16[64,512]{1,0:T(8,128)(2,1)S(1)}, bf16[64,512]{1,0:T(8,128)(2,1)S(1)}, u32[]{:S(2)}, u32[]{:S(2)}) collective-permute-start(bf16[64,512]{1,0:T(8,128)(2,1)S(1)} %shard_map.96), channel_id=1, source_target_pairs={{0,16},{16,0},{1,17},{17,1},{2,18},{18,2},{3,19},{19,3},{4,20},{20... | collective-permute-start | bytes 196616 | tf_op jit(solution)/shard_map/ppermute | solution.py:244
  88.3 0.9 copy-start
  89.2 0.7 copy-start.1
  89.8 0.7 copy-start.2
  99.0 18.5 %collective-permute-start.10 = (bf16[512,512]{1,0:T(8,128)(2,1)S(1)}, bf16[512,512]{1,0:T(8,128)(2,1)S(1)}, u32[]{:S(2)}, u32[]{:S(2)}) collective-permute-start(bf16[512,512]{1,0:T(8,128)(2,1)S(1)} %get-tuple-element.40), channel_id=1, source_target_pairs={{0,1},{1,17},{16,0},{17,16},{2,3},{3,19},{18,2},{19,18},{4,5},{5,2... | collective-permute-start | bytes 1572872 | tf_op jit(solution)/shard_map/ppermute | solution.py:279
  101.2 18.9 %collective-permute-start.9 = (bf16[512,512]{1,0:T(8,128)(2,1)S(1)}, bf16[512,512]{1,0:T(8,128)(2,1)S(1)}, u32[]{:S(2)}, u32[]{:S(2)}) collective-permute-start(bf16[512,512]{1,0:T(8,128)(2,1)S(1)} %get-tuple-element.39), channel_id=1, source_target_pairs={{1,16},{16,1},{3,18},{18,3},{5,20},{20,5},{7,22},{22,7},{9,24},{24... | collective-permute-start | bytes 1572872 | tf_op jit(solution)/shard_map/ppermute | solution.py:278
  106.4 7.7 %collective-permute-start.11 = (bf16[2,64,512]{2,1,0:T(8,128)(2,1)S(1)}, bf16[2,64,512]{2,1,0:T(8,128)(2,1)S(1)}, u32[]{:S(2)}, u32[]{:S(2)}) collective-permute-start(bf16[2,64,512]{2,1,0:T(8,128)(2,1)S(1)} %maximum_select_fusion.refs_0_), channel_id=1, source_target_pairs={{0,64},{32,96},{64,128},{96,160},{128,192},{160,224},{192,0},{224,... | collective-permute-start | bytes 393224 | tf_op jit(solution)/shard_map/ppermute | solution.py:236
  108.4 7.6 %collective-permute-start.13 = (bf16[2,64,512]{2,1,0:T(8,128)(2,1)S(1)}, bf16[2,64,512]{2,1,0:T(8,128)(2,1)S(1)}, u32[]{:S(2)}, u32[]{:S(2)}) collective-permute-start(bf16[2,64,512]{2,1,0:T(8,128)(2,1)S(1)} %maximum_select_fusion.refs_0_), channel_id=1, source_target_pairs={{0,192},{32,224},{64,0},{96,32},{128,64},{160,96},{192,128},{224,1... | collective-permute-start | bytes 393224 | tf_op jit(solution)/shard_map/ppermute | solution.py:236
  110.3 14.7 %collective-permute-start.16 = (bf16[2,64,512]{2,1,0:T(8,128)(2,1)S(1)}, bf16[2,64,512]{2,1,0:T(8,128)(2,1)S(1)}, u32[]{:S(2)}, u32[]{:S(2)}) collective-permute-start(bf16[2,64,512]{2,1,0:T(8,128)(2,1)S(1)} %maximum_select_fusion.refs_0_), channel_id=1, source_target_pairs={{0,32},{32,64},{64,96},{96,128},{128,160},{160,192},{192,224},{224... | collective-permute-start | bytes 393224 | tf_op jit(solution)/shard_map/ppermute | solution.py:236
  114.1 10.9 %collective-permute-start.17 = (bf16[2,64,512]{2,1,0:T(8,128)(2,1)S(1)}, bf16[2,64,512]{2,1,0:T(8,128)(2,1)S(1)}, u32[]{:S(2)}, u32[]{:S(2)}) collective-permute-start(bf16[2,64,512]{2,1,0:T(8,128)(2,1)S(1)} %maximum_select_fusion.refs_0_), channel_id=1, source_target_pairs={{0,224},{32,0},{64,32},{96,64},{128,96},{160,128},{192,160},{224,1... | collective-permute-start | bytes 393224 | tf_op jit(solution)/shard_map/ppermute | solution.py:236
  116.1 8.9 %collective-permute-start.12 = (bf16[2,64,512]{2,1,0:T(8,128)(2,1)S(1)}, bf16[2,64,512]{2,1,0:T(8,128)(2,1)S(1)}, u32[]{:S(2)}, u32[]{:S(2)}) collective-permute-start(bf16[2,64,512]{2,1,0:T(8,128)(2,1)S(1)} %collective-permute-done.11.refs_3_), channel_id=1, source_target_pairs={{0,32},{32,64},{64,96},{96,128},{128,160},{160,192},{192,224},{224... | collective-permute-start | bytes 393224 | tf_op jit(solution)/shard_map/ppermute | solution.py:236
  117.5 7.5 %collective-permute-start.15 = (bf16[2,64,512]{2,1,0:T(8,128)(2,1)S(1)}, bf16[2,64,512]{2,1,0:T(8,128)(2,1)S(1)}, u32[]{:S(2)}, u32[]{:S(2)}) collective-permute-start(bf16[2,64,512]{2,1,0:T(8,128)(2,1)S(1)} %collective-permute-done.11.refs_3_), channel_id=1, source_target_pairs={{0,64},{32,96},{64,128},{96,160},{128,192},{160,224},{192,0},{224,... | collective-permute-start | bytes 393224 | tf_op jit(solution)/shard_map/ppermute | solution.py:236
  120.1 4.9 %collective-permute-start.14 = (bf16[2,64,512]{2,1,0:T(8,128)(2,1)S(1)}, bf16[2,64,512]{2,1,0:T(8,128)(2,1)S(1)}, u32[]{:S(2)}, u32[]{:S(2)}) collective-permute-start(bf16[2,64,512]{2,1,0:T(8,128)(2,1)S(1)} %collective-permute-done.13.refs_4_), channel_id=1, source_target_pairs={{0,224},{32,0},{64,32},{96,64},{128,96},{160,128},{192,160},{224,1... | collective-permute-start | bytes 393224 | tf_op jit(solution)/shard_map/ppermute | solution.py:236
Sparse Core Ops, SparseCore 0:
  9.8 69.2 all-gather.2

commit v4 on v3

--- a/solution.py
+++ b/solution.py
@@ -204,6 +204,21 @@
         own[rows, :] = jnp.where(live[b] > 0, part, jnp.zeros_like(part))
 
 
+def arrived_kernel(x, *refs):
+    for i in range(refs[-1].shape[0]):
+        refs[-1][i] = x[i]
+
+
+def arrived(x, *blocks):
+    return pl.pallas_call(
+        arrived_kernel,
+        in_specs=[pl.BlockSpec(memory_space=pltpu.SMEM)] + [pl.BlockSpec(memory_space=pl.ANY)] * len(blocks),
+        out_specs=pl.BlockSpec(memory_space=pltpu.SMEM),
+        out_shape=jax.ShapeDtypeStruct(x.shape, x.dtype),
+        cost_estimate=pl.CostEstimate(flops=4 << 30, bytes_accessed=14 << 20, transcendentals=0),
+    )(x, *blocks)
+
+
 def base_parts(place, roles, live, wide, *pieces):
     spec = pltpu.PrefetchScalarGridSpec(
         num_scalar_prefetch=3,
@@ -270,6 +285,8 @@
     beside_up1, beside_down2 = shift(beside, "y", Y, 1), shift(beside_down1, "y", Y, -1)
     pieces = [turned, beside, up1, down1, beside_up1, beside_down1, up2, beside_down2]
 
+    place = arrived(place, up2, beside_up1, beside_down2)
+    outer, place = tie(outer, place)
     total = sum_parts(outer, grad_scale)
     other = trade(total, "xh", XH, 1)
     far, near, own = base_parts(place, roles, live, wide, *pieces, lb, adapter_down)

time: 134 us -> 131 us (0.978)
  waiting for transfers between devices: 25 us -> 21.2 us
  starting transfers between devices: 45.6 us -> 42.6 us
  local copies, waits for them, and re-layouts: 3.18 us -> 4.53 us
    ppermute x13, starting transfers between devices: 21.5 us -> 17.8 us  [shift(): return lax.ppermute(x, axis, [(i, (i + step) % size) for i in range(size)])]
    ppermute x13, waiting for transfers between devices: 17.6 us -> 15.5 us  [shift(): return lax.ppermute(x, axis, [(i, (i + step) % size) for i in range(size)])]
    all_to_all x1, waiting for transfers between devices: 6.71 us -> 4.99 us  [shards(): outer = lax.all_to_all(outer, FS, 0, 0)]
    unnamed x8 -> x14, local copies, waits for them, and re-layouts: 3.01 us -> 3.25 us
  transfers between devices with their start and end apart: 20 -> 20, of which waited for: 4 -> 5; matrix products, arithmetic and copies ran while one was open for 2% -> 3% of each run, Pallas kernels for 12% -> 13%
where the time goes in v4:
time: 131 us; the launch traced here: 130 us
  starting transfers between devices  42.6 us (33%)
  blocking collectives  25.7 us (20%)
  waiting for transfers between devices  21.2 us (16%)
  Pallas kernels  19.1 us (15%)
  between operations  14.8 us (11%)
  local copies, waits for them, and re-layouts  4.53 us (3%)
  other arithmetic  2.29 us (2%)
    ppermute x13, starting transfers between devices, shift(): return lax.ppermute(x, axis, [(i, (i + step) % size) for i in range(size)])  17.8 us
    ppermute x13, waiting for transfers between devices, shift(): return lax.ppermute(x, axis, [(i, (i + step) % size) for i in range(size)])  15.5 us
    all_to_all x1, blocking collectives, shards(): lax.all_to_all(jnp.broadcast_to(mine[None], (16,) + mine.shape), TP, 0, 0)  13.9 us
    all_to_all x1, blocking collectives, shards(): ranks = lax.all_to_all(ranks.reshape(16, ROWS // 16, 2 * RANK), TP, 0, 0)  11.8 us
    all_to_all x1, starting transfers between devices, shards(): outer = lax.all_to_all(outer, FS, 0, 0)  9.47 us
    pallas_call x1, Pallas kernels, base_parts(): pl.pallas_call(base_kernel, grid_spec=spec, out_shape=[jax.ShapeDtypeStru...  8.49 us
    ppermute x1, starting transfers between devices, shards(): lax.ppermute(grad_out, ('xh', 'c'), [(0, 0), (1, 2), (2, 1), (3, 3)])  6.04 us
    ppermute x1, starting transfers between devices, shards(): far = lax.ppermute(far, ('xh', 'c'), [(1, 2), (2, 1)])  5.36 us
  transfers between devices with their start and end apart: 20, of which 5 were waited for; matrix products, arithmetic and copies ran while one was open for 3% of the time, Pallas kernels for 13%

profile of v4, /device:TPU:1, one launch (start us, length us, event | category | flops | bytes accessed | tf_op | source)
XLA Modules:
  0.0 130.3 jit_solution(14307552277387757380)
XLA Ops:
  7.2 0.0 all-gather.3.cloned.1.call-start
  7.2 0.7 all-gather.3.cloned.1.call-update
  7.9 6.0 %collective-permute-start = (bf16[512,512]{1,0:T(8,128)(2,1)}, bf16[512,512]{1,0:T(8,128)(2,1)S(1)}, u32[]{:S(2)}, u32[]{:S(2)}) collective-permute-start(bf16[512,512]{1,0:T(8,128)(2,1)} %g_far.1), channel_id=1, source_target_pairs={{0,0},{1,16},{16,1},{17,17},{2,2},{3,18},{18,3},{19,19},{4,4},{5,2... | collective-permute-start | bytes 1572872 | tf_op jit(solution)/shard_map/ppermute | solution.py:270
  13.9 3.4 %shard_map.94 = f32[512,128]{1,0:T(8,128)} custom-call(s32[4]{0:T(128)} %bitcast.21, bf16[512,512]{1,0:T(8,128)(2,1)} %att_far.1, bf16[512,512]{1,0:T(8,128)(2,1)} %g_far.1, bf16[8,64,512]{2,1,0:T(8,128)(2,1)} %bitcast.25, bf16[8,64,512]{2,1,0:T(8,128)(2,1)} %up.1), custom_call_target="tpu_custom_call" | custom-call | flops 67108864 | bytes 2097152 | tf_op jit(solution)/shard_map/pallas_call | solution.py:59
  17.3 11.8 %all_to_all.15 = f32[16,32,128]{2,1,0:T(8,128)S(1)} all-to-all(f32[16,32,128]{2,1,0:T(8,128)} %bitcast.24), channel_id=1, replica_groups=mesh['z'=8,'xh'=2,'xl'=2,'y'=4,'c'=2] {'xl','y','c'}, dimensions={0} | all-to-all | bytes 524288 | tf_op jit(solution)/shard_map/all_to_all | solution.py:272
  29.1 0.0 collective-permute-done.refs_0_
  29.1 0.8 collective-permute-start.1
  29.9 0.2 collective-permute-start.2
  30.1 2.5 %collective-permute-start.3 = (bf16[512,512]{1,0:T(8,128)(2,1)S(1)}, bf16[512,512]{1,0:T(8,128)(2,1)S(1)}, u32[]{:S(2)}, u32[]{:S(2)}) collective-permute-start(bf16[512,512]{1,0:T(8,128)(2,1)S(1)} %collective-permute-done.refs_0_), channel_id=1, source_target_pairs={{0,6},{2,0},{4,2},{6,4},{1,7},{3,1},{5,3},{7,5},{8,14},{10,8},{12,... | collective-permute-start | bytes 1572872 | tf_op jit(solution)/shard_map/ppermute | solution.py:251
  32.6 13.9 %all_to_all.16 = bf16[16,32,128]{2,1,0:T(8,128)(2,1)} all-to-all(bf16[16,32,128]{2,1,0:T(8,128)(2,1)S(1)} %broadcast_in_dim.23), channel_id=1, replica_groups=mesh['z'=8,'xh'=2,'xl'=2,'y'=4,'c'=2] {'xl','y','c'}, dimensions={0} | all-to-all | bytes 262144 | tf_op jit(solution)/shard_map/all_to_all | solution.py:278
  46.6 0.0 collective-permute-done.1.refs_1_
  46.6 0.0 collective-permute-done.2.refs_2_
  46.6 0.6 collective-permute-start.4
  47.2 2.3 %collective-permute-start.5 = (bf16[512,512]{1,0:T(8,128)(2,1)S(1)}, bf16[512,512]{1,0:T(8,128)(2,1)}, u32[]{:S(2)}, u32[]{:S(2)}) collective-permute-start(bf16[512,512]{1,0:T(8,128)(2,1)S(1)} %collective-permute-done.1.refs_1_), channel_id=1, source_target_pairs={{0,6},{2,0},{4,2},{6,4},{1,7},{3,1},{5,3},{7,5},{8,14},{10,8},{12,... | collective-permute-start | bytes 1572872 | tf_op jit(solution)/shard_map/ppermute | solution.py:251
  49.4 3.8 %shard_map.95 = bf16[16,32,640]{2,1,0:T(8,128)(2,1)} custom-call(s32[4]{0:T(128)} %bitcast.22, s32[4]{0:T(128)} %live.3, bf16[512,128]{1,0:T(8,128)(2,1)} %bitcast.18, bf16[512,512]{1,0:T(8,128)(2,1)} %att_far.1, bf16[512,512]{1,0:T(8,128)(2,1)} %g_far.1), custom_call_target="tpu_custom_call" | custom-call | flops 67108864 | bytes 2097152 | tf_op jit(solution)/shard_map/pallas_call | solution.py:98
  53.3 9.5 %all-to-all-start.2 = ((bf16[16,32,640]{2,1,0:T(8,128)(2,1)}), bf16[16,32,640]{2,1,0:T(8,128)(2,1)S(1)}, u32[]{:S(2)}, u32[]{:S(2)}) async-start(bf16[16,32,640]{2,1,0:T(8,128)(2,1)} %shard_map.95), calls=%async_computation.2 | async-start | bytes 1310720 | tf_op jit(solution)/shard_map/all_to_all | solution.py:284
  62.8 0.0 copy-start.1
  62.8 0.0 copy-start.2
  62.8 0.0 collective-permute-done.4.refs_0_.refs_6_
  62.8 0.0 copy-start.6
  62.8 0.8 copy-done.6
  63.6 0.0 collective-permute-start.6
  63.6 2.7 %collective-permute-start.7 = (bf16[512,512]{1,0:T(8,128)(2,1)}, bf16[512,512]{1,0:T(8,128)(2,1)}, u32[]{:S(2)}, u32[]{:S(2)}) collective-permute-start(bf16[512,512]{1,0:T(8,128)(2,1)} %collective-permute-done.5.refs_5_), channel_id=1, source_target_pairs={{0,6},{2,0},{4,2},{6,4},{1,7},{3,1},{5,3},{7,5},{8,14},{10,8},{12,... | collective-permute-start | bytes 1572872 | tf_op jit(solution)/shard_map/ppermute | solution.py:251
  66.3 0.6 stack.37.x
  66.9 10.3 %collective-permute-done.6.refs_1_.refs_4_ = bf16[512,512]{1,0:T(8,128)(2,1)S(1)} collective-permute-done((bf16[512,512]{1,0:T(8,128)(2,1)S(1)}, bf16[512,512]{1,0:T(8,128)(2,1)S(1)}, u32[]{:S(2)}, u32[]{:S(2)}) %collective-permute-start.6) | collective-permute-done | bytes 524320 | tf_op jit(solution)/shard_map/ppermute | solution.py:251
  77.2 0.0 collective-permute-done.7.refs_2_.refs_7_
  77.2 0.8 copy-done.4
  78.0 1.2 shard_map.96.place
  79.2 5.0 %all-to-all-done.2 = bf16[16,32,640]{2,1,0:T(8,128)(2,1)S(1)} async-done(((bf16[16,32,640]{2,1,0:T(8,128)(2,1)}), bf16[16,32,640]{2,1,0:T(8,128)(2,1)S(1)}, u32[]{:S(2)}, u32[]{:S(2)}) %all-to-all-start.2) | async-done | bytes 655392 | tf_op jit(solution)/shard_map/all_to_all | solution.py:284
  84.2 0.3 shard_map.97
  84.4 0.3 collective-permute-start.8
  84.8 0.6 copy-done.3
  85.4 1.0 copy-done.5
  86.4 8.5 %shard_map.98 = (bf16[512,512]{1,0:T(8,128)(2,1)S(1)}, bf16[512,512]{1,0:T(8,128)(2,1)S(1)}, f32[512,512]{1,0:T(8,128)}) custom-call(s32[5]{0:T(128)S(1)} %copy-done.3, s32[4]{0:T(128)S(1)} %bitcast.23, s32[4]{0:T(128)S(1)} %copy-done.2, bf16[8,2,512,512]{3,2,1,0:T(8,128)(2,1)} %bitcast.28, bf16[512,512]{1,0:T(8,128)(2,1)S(1)} %collective-permute-done.refs_0_, ...), custom_call_target="tpu_custom_call" | custom-call | flops 4294967296 | bytes 14680064 | tf_op jit(solution)/shard_map/pallas_call | solution.py:237
  94.9 2.8 %collective-permute-start.10 = (bf16[512,512]{1,0:T(8,128)(2,1)S(1)}, bf16[512,512]{1,0:T(8,128)(2,1)S(1)}, u32[]{:S(2)}, u32[]{:S(2)}) collective-permute-start(bf16[512,512]{1,0:T(8,128)(2,1)S(1)} %get-tuple-element.44), channel_id=1, source_target_pairs={{0,1},{1,17},{16,0},{17,16},{2,3},{3,19},{18,2},{19,18},{4,5},{5,2... | collective-permute-start | bytes 1572872 | tf_op jit(solution)/shard_map/ppermute | solution.py:296
  97.8 5.4 %collective-permute-start.9 = (bf16[512,512]{1,0:T(8,128)(2,1)S(1)}, bf16[512,512]{1,0:T(8,128)(2,1)S(1)}, u32[]{:S(2)}, u32[]{:S(2)}) collective-permute-start(bf16[512,512]{1,0:T(8,128)(2,1)S(1)} %get-tuple-element.43), channel_id=1, source_target_pairs={{1,16},{16,1},{3,18},{18,3},{5,20},{20,5},{7,22},{22,7},{9,24},{24... | collective-permute-start | bytes 1572872 | tf_op jit(solution)/shard_map/ppermute | solution.py:295
  103.1 0.6 slice.3
  104.4 0.6 collective-permute-start.11
  105.0 3.2 %collective-permute-start.13 = (bf16[2,64,512]{2,1,0:T(8,128)(2,1)S(1)}, bf16[2,64,512]{2,1,0:T(8,128)(2,1)S(1)}, u32[]{:S(2)}, u32[]{:S(2)}) collective-permute-start(bf16[2,64,512]{2,1,0:T(8,128)(2,1)S(1)} %maximum_select_fusion.refs_0_), channel_id=1, source_target_pairs={{0,192},{32,224},{64,0},{96,32},{128,64},{160,96},{192,128},{224,1... | collective-permute-start | bytes 393224 | tf_op jit(solution)/shard_map/ppermute | solution.py:251
  108.2 0.1 broadcast_bitcast_fusion
  108.3 3.1 %collective-permute-done.11.refs_3_ = bf16[2,64,512]{2,1,0:T(8,128)(2,1)S(1)} collective-permute-done((bf16[2,64,512]{2,1,0:T(8,128)(2,1)S(1)}, bf16[2,64,512]{2,1,0:T(8,128)(2,1)S(1)}, u32[]{:S(2)}, u32[]{:S(2)}) %collective-permute-start.11) | collective-permute-done | bytes 131104 | tf_op jit(solution)/shard_map/ppermute | solution.py:251
  111.4 0.8 collective-permute-done.13.refs_4_
  112.2 0.6 collective-permute-start.12
  112.8 2.5 %collective-permute-start.15 = (bf16[2,64,512]{2,1,0:T(8,128)(2,1)S(1)}, bf16[2,64,512]{2,1,0:T(8,128)(2,1)S(1)}, u32[]{:S(2)}, u32[]{:S(2)}) collective-permute-start(bf16[2,64,512]{2,1,0:T(8,128)(2,1)S(1)} %collective-permute-done.11.refs_3_), channel_id=1, source_target_pairs={{0,64},{32,96},{64,128},{96,160},{128,192},{160,224},{192,0},{224,... | collective-permute-start | bytes 393224 | tf_op jit(solution)/shard_map/ppermute | solution.py:251
  115.3 2.7 %collective-permute-start.14 = (bf16[2,64,512]{2,1,0:T(8,128)(2,1)S(1)}, bf16[2,64,512]{2,1,0:T(8,128)(2,1)S(1)}, u32[]{:S(2)}, u32[]{:S(2)}) collective-permute-start(bf16[2,64,512]{2,1,0:T(8,128)(2,1)S(1)} %collective-permute-done.13.refs_4_), channel_id=1, source_target_pairs={{0,224},{32,0},{64,32},{96,64},{128,96},{160,128},{192,160},{224,1... | collective-permute-start | bytes 393224 | tf_op jit(solution)/shard_map/ppermute | solution.py:251
  118.0 2.2 %select_convert_fusion = bf16[512,512]{1,0:T(8,128)(2,1)} fusion(bf16[512,512]{1,0:T(8,128)(2,1)S(1)} %collective-permute-done.10, f32[512,512]{1,0:T(8,128)} %get-tuple-element.42, bf16[512,512]{1,0:T(8,128)(2,1)S(1)} %collective-permute-done.9, pred[512]{0:T(512)(128)(4,1)S(1)} %broadcast_bitcast_fusion), kind=kLoop, calls=%fused_computation | loop fusion | flops 1572864 | bytes 2621952 | tf_op jit(solution)/shard_map/convert_element_type | solution.py:303
  120.2 1.3 collective-permute-done.15.refs_7_
  121.5 2.0 %shard_map.99 = (f32[8,64,512]{2,1,0:T(8,128)}, f32[8,64,512]{2,1,0:T(8,128)}) custom-call(s32[5]{0:T(128)S(1)} %copy-done.3, bf16[2,64,512]{2,1,0:T(8,128)(2,1)S(1)} %maximum_select_fusion.refs_0_, bf16[2,64,512]{2,1,0:T(8,128)(2,1)S(1)} %collective-permute-done.16.refs_1_, bf16[2,64,512]{2,1,0:T(8,128)(2,1)S(1)} %collective-permute-done.17.refs_2_, ...), custom_call_target="tpu_custom_call" | custom-call | bytes 4194304 | tf_op jit(solution)/shard_map/pallas_call | solution.py:154
  (23 shorter events, 0.1 us)
Async XLA Ops:
  7.2 77.6 %all-gather.3.cloned.1.call-start = ((), (), s32[]{:S(2)}) async-start(), calls=%async_computation.3 | async-start | bytes 8912896 | tf_op jit(solution)/shard_map/all_gather | solution.py:269
  7.9 21.2 %collective-permute-start = (bf16[512,512]{1,0:T(8,128)(2,1)}, bf16[512,512]{1,0:T(8,128)(2,1)S(1)}, u32[]{:S(2)}, u32[]{:S(2)}) collective-permute-start(bf16[512,512]{1,0:T(8,128)(2,1)} %g_far.1), channel_id=1, source_target_pairs={{0,0},{1,16},{16,1},{17,17},{2,2},{3,18},{18,3},{19,19},{4,4},{5,2... | collective-permute-start | bytes 1572872 | tf_op jit(solution)/shard_map/ppermute | solution.py:270
  29.1 17.5 %collective-permute-start.1 = (bf16[512,512]{1,0:T(8,128)(2,1)S(1)}, bf16[512,512]{1,0:T(8,128)(2,1)S(1)}, u32[]{:S(2)}, u32[]{:S(2)}) collective-permute-start(bf16[512,512]{1,0:T(8,128)(2,1)S(1)} %collective-permute-done.refs_0_), channel_id=1, source_target_pairs={{0,8},{8,0},{1,9},{9,1},{2,10},{10,2},{3,11},{11,3},{4,12},{12,4},... | collective-permute-start | bytes 1572872 | tf_op jit(solution)/shard_map/ppermute | solution.py:259
  29.9 16.7 %collective-permute-start.2 = (bf16[512,512]{1,0:T(8,128)(2,1)S(1)}, bf16[512,512]{1,0:T(8,128)(2,1)S(1)}, u32[]{:S(2)}, u32[]{:S(2)}) collective-permute-start(bf16[512,512]{1,0:T(8,128)(2,1)S(1)} %collective-permute-done.refs_0_), channel_id=1, source_target_pairs={{0,2},{2,4},{4,6},{6,0},{1,3},{3,5},{5,7},{7,1},{8,10},{10,12},{12... | collective-permute-start | bytes 1572872 | tf_op jit(solution)/shard_map/ppermute | solution.py:251
  30.1 16.5 %collective-permute-start.3 = (bf16[512,512]{1,0:T(8,128)(2,1)S(1)}, bf16[512,512]{1,0:T(8,128)(2,1)S(1)}, u32[]{:S(2)}, u32[]{:S(2)}) collective-permute-start(bf16[512,512]{1,0:T(8,128)(2,1)S(1)} %collective-permute-done.refs_0_), channel_id=1, source_target_pairs={{0,6},{2,0},{4,2},{6,4},{1,7},{3,1},{5,3},{7,5},{8,14},{10,8},{12,... | collective-permute-start | bytes 1572872 | tf_op jit(solution)/shard_map/ppermute | solution.py:251
  46.6 16.2 %collective-permute-start.4 = (bf16[512,512]{1,0:T(8,128)(2,1)S(1)}, bf16[512,512]{1,0:T(8,128)(2,1)S(1)}, u32[]{:S(2)}, u32[]{:S(2)}) collective-permute-start(bf16[512,512]{1,0:T(8,128)(2,1)S(1)} %collective-permute-done.2.refs_2_), channel_id=1, source_target_pairs={{0,2},{2,4},{4,6},{6,0},{1,3},{3,5},{5,7},{7,1},{8,10},{10,12},{12... | collective-permute-start | bytes 1572872 | tf_op jit(solution)/shard_map/ppermute | solution.py:251
  47.2 16.4 %collective-permute-start.5 = (bf16[512,512]{1,0:T(8,128)(2,1)S(1)}, bf16[512,512]{1,0:T(8,128)(2,1)}, u32[]{:S(2)}, u32[]{:S(2)}) collective-permute-start(bf16[512,512]{1,0:T(8,128)(2,1)S(1)} %collective-permute-done.1.refs_1_), channel_id=1, source_target_pairs={{0,6},{2,0},{4,2},{6,4},{1,7},{3,1},{5,3},{7,5},{8,14},{10,8},{12,... | collective-permute-start | bytes 1572872 | tf_op jit(solution)/shard_map/ppermute | solution.py:251
  53.3 30.9 %all-to-all-start.2 = ((bf16[16,32,640]{2,1,0:T(8,128)(2,1)}), bf16[16,32,640]{2,1,0:T(8,128)(2,1)S(1)}, u32[]{:S(2)}, u32[]{:S(2)}) async-start(bf16[16,32,640]{2,1,0:T(8,128)(2,1)} %shard_map.95), calls=%async_computation.2 | async-start | bytes 1310720 | tf_op jit(solution)/shard_map/all_to_all | solution.py:284
  62.8 22.0 %copy-start = (bf16[16,32,128]{2,1,0:T(8,128)(2,1)S(1)}, bf16[16,32,128]{2,1,0:T(8,128)(2,1)}, u32[]{:S(2)}) copy-start(bf16[16,32,128]{2,1,0:T(8,128)(2,1)} %all_to_all.16) | copy-start | bytes 393220
  62.8 22.0 %copy-start.1 = (s32[4,1]{0,1:T(1,128)S(1)}, s32[4,1]{0,1:T(1,128)}, u32[]{:S(2)}) copy-start(s32[4,1]{0,1:T(1,128)} %param.12) | copy-start | bytes 52
  62.8 22.0 %copy-start.2 = (s32[4]{0:T(128)S(1)}, s32[4]{0:T(128)}, u32[]{:S(2)}) copy-start(s32[4]{0:T(128)} %live.3) | copy-start | bytes 52
  62.8 0.8 copy-start.6
  63.6 13.6 %collective-permute-start.6 = (bf16[512,512]{1,0:T(8,128)(2,1)S(1)}, bf16[512,512]{1,0:T(8,128)(2,1)S(1)}, u32[]{:S(2)}, u32[]{:S(2)}) collective-permute-start(bf16[512,512]{1,0:T(8,128)(2,1)S(1)} %collective-permute-done.1.refs_1_), channel_id=1, source_target_pairs={{0,2},{2,4},{4,6},{6,0},{1,3},{3,5},{5,7},{7,1},{8,10},{10,12},{12... | collective-permute-start | bytes 1572872 | tf_op jit(solution)/shard_map/ppermute | solution.py:251
  63.6 13.6 %collective-permute-start.7 = (bf16[512,512]{1,0:T(8,128)(2,1)}, bf16[512,512]{1,0:T(8,128)(2,1)}, u32[]{:S(2)}, u32[]{:S(2)}) collective-permute-start(bf16[512,512]{1,0:T(8,128)(2,1)} %collective-permute-done.5.refs_5_), channel_id=1, source_target_pairs={{0,6},{2,0},{4,2},{6,4},{1,7},{3,1},{5,3},{7,5},{8,14},{10,8},{12,... | collective-permute-start | bytes 1572872 | tf_op jit(solution)/shard_map/ppermute | solution.py:251
  77.2 0.8 copy-start.4
  84.4 10.5 %collective-permute-start.8 = (bf16[64,512]{1,0:T(8,128)(2,1)S(1)}, bf16[64,512]{1,0:T(8,128)(2,1)S(1)}, u32[]{:S(2)}, u32[]{:S(2)}) collective-permute-start(bf16[64,512]{1,0:T(8,128)(2,1)S(1)} %shard_map.97), channel_id=1, source_target_pairs={{0,16},{16,0},{1,17},{17,1},{2,18},{18,2},{3,19},{19,3},{4,20},{20... | collective-permute-start | bytes 196616 | tf_op jit(solution)/shard_map/ppermute | solution.py:259
  84.7 0.6 copy-start.3
  85.4 1.0 copy-start.5
  94.9 17.9 %collective-permute-start.10 = (bf16[512,512]{1,0:T(8,128)(2,1)S(1)}, bf16[512,512]{1,0:T(8,128)(2,1)S(1)}, u32[]{:S(2)}, u32[]{:S(2)}) collective-permute-start(bf16[512,512]{1,0:T(8,128)(2,1)S(1)} %get-tuple-element.44), channel_id=1, source_target_pairs={{0,1},{1,17},{16,0},{17,16},{2,3},{3,19},{18,2},{19,18},{4,5},{5,2... | collective-permute-start | bytes 1572872 | tf_op jit(solution)/shard_map/ppermute | solution.py:296
  97.8 17.5 %collective-permute-start.9 = (bf16[512,512]{1,0:T(8,128)(2,1)S(1)}, bf16[512,512]{1,0:T(8,128)(2,1)S(1)}, u32[]{:S(2)}, u32[]{:S(2)}) collective-permute-start(bf16[512,512]{1,0:T(8,128)(2,1)S(1)} %get-tuple-element.43), channel_id=1, source_target_pairs={{1,16},{16,1},{3,18},{18,3},{5,20},{20,5},{7,22},{22,7},{9,24},{24... | collective-permute-start | bytes 1572872 | tf_op jit(solution)/shard_map/ppermute | solution.py:295
  104.4 7.0 %collective-permute-start.11 = (bf16[2,64,512]{2,1,0:T(8,128)(2,1)S(1)}, bf16[2,64,512]{2,1,0:T(8,128)(2,1)S(1)}, u32[]{:S(2)}, u32[]{:S(2)}) collective-permute-start(bf16[2,64,512]{2,1,0:T(8,128)(2,1)S(1)} %maximum_select_fusion.refs_0_), channel_id=1, source_target_pairs={{0,64},{32,96},{64,128},{96,160},{128,192},{160,224},{192,0},{224,... | collective-permute-start | bytes 393224 | tf_op jit(solution)/shard_map/ppermute | solution.py:251
  105.0 7.2 %collective-permute-start.13 = (bf16[2,64,512]{2,1,0:T(8,128)(2,1)S(1)}, bf16[2,64,512]{2,1,0:T(8,128)(2,1)S(1)}, u32[]{:S(2)}, u32[]{:S(2)}) collective-permute-start(bf16[2,64,512]{2,1,0:T(8,128)(2,1)S(1)} %maximum_select_fusion.refs_0_), channel_id=1, source_target_pairs={{0,192},{32,224},{64,0},{96,32},{128,64},{160,96},{192,128},{224,1... | collective-permute-start | bytes 393224 | tf_op jit(solution)/shard_map/ppermute | solution.py:251
  108.3 13.2 %collective-permute-start.16 = (bf16[2,64,512]{2,1,0:T(8,128)(2,1)S(1)}, bf16[2,64,512]{2,1,0:T(8,128)(2,1)S(1)}, u32[]{:S(2)}, u32[]{:S(2)}) collective-permute-start(bf16[2,64,512]{2,1,0:T(8,128)(2,1)S(1)} %maximum_select_fusion.refs_0_), channel_id=1, source_target_pairs={{0,32},{32,64},{64,96},{96,128},{128,160},{160,192},{192,224},{224... | collective-permute-start | bytes 393224 | tf_op jit(solution)/shard_map/ppermute | solution.py:251
  111.4 10.1 %collective-permute-start.17 = (bf16[2,64,512]{2,1,0:T(8,128)(2,1)S(1)}, bf16[2,64,512]{2,1,0:T(8,128)(2,1)S(1)}, u32[]{:S(2)}, u32[]{:S(2)}) collective-permute-start(bf16[2,64,512]{2,1,0:T(8,128)(2,1)S(1)} %maximum_select_fusion.refs_0_), channel_id=1, source_target_pairs={{0,224},{32,0},{64,32},{96,64},{128,96},{160,128},{192,160},{224,1... | collective-permute-start | bytes 393224 | tf_op jit(solution)/shard_map/ppermute | solution.py:251
  112.2 8.0 %collective-permute-start.12 = (bf16[2,64,512]{2,1,0:T(8,128)(2,1)S(1)}, bf16[2,64,512]{2,1,0:T(8,128)(2,1)S(1)}, u32[]{:S(2)}, u32[]{:S(2)}) collective-permute-start(bf16[2,64,512]{2,1,0:T(8,128)(2,1)S(1)} %collective-permute-done.11.refs_3_), channel_id=1, source_target_pairs={{0,32},{32,64},{64,96},{96,128},{128,160},{160,192},{192,224},{224... | collective-permute-start | bytes 393224 | tf_op jit(solution)/shard_map/ppermute | solution.py:251
  112.8 8.7 %collective-permute-start.15 = (bf16[2,64,512]{2,1,0:T(8,128)(2,1)S(1)}, bf16[2,64,512]{2,1,0:T(8,128)(2,1)S(1)}, u32[]{:S(2)}, u32[]{:S(2)}) collective-permute-start(bf16[2,64,512]{2,1,0:T(8,128)(2,1)S(1)} %collective-permute-done.11.refs_3_), channel_id=1, source_target_pairs={{0,64},{32,96},{64,128},{96,160},{128,192},{160,224},{192,0},{224,... | collective-permute-start | bytes 393224 | tf_op jit(solution)/shard_map/ppermute | solution.py:251
  115.3 4.9 %collective-permute-start.14 = (bf16[2,64,512]{2,1,0:T(8,128)(2,1)S(1)}, bf16[2,64,512]{2,1,0:T(8,128)(2,1)S(1)}, u32[]{:S(2)}, u32[]{:S(2)}) collective-permute-start(bf16[2,64,512]{2,1,0:T(8,128)(2,1)S(1)} %collective-permute-done.13.refs_4_), channel_id=1, source_target_pairs={{0,224},{32,0},{64,32},{96,64},{128,96},{160,128},{192,160},{224,1... | collective-permute-start | bytes 393224 | tf_op jit(solution)/shard_map/ppermute | solution.py:251
Sparse Core Ops, SparseCore 0:
  9.8 62.1 all-gather.2

commit v5 on v4

--- a/solution.py
+++ b/solution.py
@@ -283,12 +283,13 @@
     up2, beside_down1, beside, _ = tie(up2, beside_down1, beside, outer)
     outer = lax.all_to_all(outer, FS, 0, 0)
     beside_up1, beside_down2 = shift(beside, "y", Y, 1), shift(beside_down1, "y", Y, -1)
-    pieces = [turned, beside, up1, down1, beside_up1, beside_down1, up2, beside_down2]
-
-    place = arrived(place, up2, beside_up1, beside_down2)
-    outer, place = tie(outer, place)
+
+    beside_up1, beside_down2 = tie(beside_up1, beside_down2)
+    mark = arrived(place, beside_down2)
+    outer, mark = tie(outer, mark)
     total = sum_parts(outer, grad_scale)
     other = trade(total, "xh", XH, 1)
+    pieces = [turned, beside, up1, down1, beside_up1, beside_down1, up2, beside_down2]
     far, near, own = base_parts(place, roles, live, wide, *pieces, lb, adapter_down)
     total, other, far, near, own = tie(total, other, far, near, own)
 
@@ -302,7 +303,7 @@
     token_live = jnp.repeat(live, BLOCK)[:, None] > 0
     input_gradient = jnp.where(token_live, own + far.astype(f32) + near.astype(f32), 0.0).astype(bf16)
     input_gradient, s3, t3, s4 = tie(input_gradient, s3, t3, s4)
-    up_gradient, down_gradient = spread(place, [pair, s1, t1, s2, t2, s3, t3, s4])
+    up_gradient, down_gradient = spread(mark, [pair, s1, t1, s2, t2, s3, t3, s4])
     return (input_gradient, jnp.transpose(down_gradient, (0, 2, 1)), up_gradient)
 
 

time: 131 us -> 128 us (0.977)
  local copies, waits for them, and re-layouts: 4.53 us -> 1.57 us
  waiting for transfers between devices: 21.2 us -> 23.6 us
  starting transfers between devices: 42.6 us -> 40.7 us
    unnamed x14 -> x12, local copies, waits for them, and re-layouts: 3.25 us -> 0.81 us
    ppermute x13, starting transfers between devices: 17.8 us -> 15.8 us  [shift(): return lax.ppermute(x, axis, [(i, (i + step) % size) for i in range(size)])]
    ppermute x13, waiting for transfers between devices: 15.5 us -> 17.1 us  [shift(): return lax.ppermute(x, axis, [(i, (i + step) % size) for i in range(size)])]
  transfers between devices with their start and end apart: 20 -> 20, of which waited for: 5 -> 7; matrix products, arithmetic and copies ran while one was open for 3% -> 2% of each run, Pallas kernels for 13% -> 13%
where the time goes in v5:
time: 128 us; the launch traced here: 127 us
  starting transfers between devices  40.7 us (32%)
  blocking collectives  25.7 us (20%)
  waiting for transfers between devices  23.6 us (18%)
  Pallas kernels  19.1 us (15%)
  between operations  14.2 us (11%)
  other arithmetic  2.3 us (2%)
  local copies, waits for them, and re-layouts  1.57 us (1%)
    ppermute x13, waiting for transfers between devices, shift(): return lax.ppermute(x, axis, [(i, (i + step) % size) for i in range(size)])  17.1 us
    ppermute x13, starting transfers between devices, shift(): return lax.ppermute(x, axis, [(i, (i + step) % size) for i in range(size)])  15.8 us
    all_to_all x1, blocking collectives, shards(): lax.all_to_all(jnp.broadcast_to(mine[None], (16,) + mine.shape), TP, 0, 0)  13.9 us
    all_to_all x1, blocking collectives, shards(): ranks = lax.all_to_all(ranks.reshape(16, ROWS // 16, 2 * RANK), TP, 0, 0)  11.8 us
    all_to_all x1, starting transfers between devices, shards(): outer = lax.all_to_all(outer, FS, 0, 0)  9.47 us
    pallas_call x1, Pallas kernels, base_parts(): pl.pallas_call(base_kernel, grid_spec=spec, out_shape=[jax.ShapeDtypeStru...  8.5 us
    ppermute x1, starting transfers between devices, shards(): lax.ppermute(grad_out, ('xh', 'c'), [(0, 0), (1, 2), (2, 1), (3, 3)])  6.04 us
    all_to_all x1, waiting for transfers between devices, shards(): outer = lax.all_to_all(outer, FS, 0, 0)  5.78 us
  transfers between devices with their start and end apart: 20, of which 7 were waited for; matrix products, arithmetic and copies ran while one was open for 2% of the time, Pallas kernels for 13%

profile of v5, /device:TPU:1, one launch (start us, length us, event | category | flops | bytes accessed | tf_op | source)
XLA Modules:
  0.0 127.2 jit_solution(8443020295371200028)
XLA Ops:
  7.2 0.0 all-gather.3.cloned.1.call-start
  7.2 0.7 all-gather.3.cloned.1.call-update
  7.9 6.0 %collective-permute-start = (bf16[512,512]{1,0:T(8,128)(2,1)}, bf16[512,512]{1,0:T(8,128)(2,1)S(1)}, u32[]{:S(2)}, u32[]{:S(2)}) collective-permute-start(bf16[512,512]{1,0:T(8,128)(2,1)} %g_far.1), channel_id=1, source_target_pairs={{0,0},{1,16},{16,1},{17,17},{2,2},{3,18},{18,3},{19,19},{4,4},{5,2... | collective-permute-start | bytes 1572872 | tf_op jit(solution)/shard_map/ppermute | solution.py:270
  13.9 3.4 %shard_map.94 = f32[512,128]{1,0:T(8,128)} custom-call(s32[4]{0:T(128)} %bitcast.20, bf16[512,512]{1,0:T(8,128)(2,1)} %att_far.1, bf16[512,512]{1,0:T(8,128)(2,1)} %g_far.1, bf16[8,64,512]{2,1,0:T(8,128)(2,1)} %bitcast.24, bf16[8,64,512]{2,1,0:T(8,128)(2,1)} %up.1), custom_call_target="tpu_custom_call" | custom-call | flops 67108864 | bytes 2097152 | tf_op jit(solution)/shard_map/pallas_call | solution.py:59
  17.3 11.8 %all_to_all.15 = f32[16,32,128]{2,1,0:T(8,128)S(1)} all-to-all(f32[16,32,128]{2,1,0:T(8,128)} %bitcast.23), channel_id=1, replica_groups=mesh['z'=8,'xh'=2,'xl'=2,'y'=4,'c'=2] {'xl','y','c'}, dimensions={0} | all-to-all | bytes 524288 | tf_op jit(solution)/shard_map/all_to_all | solution.py:272
  29.1 0.0 collective-permute-done.refs_0_
  29.1 0.8 collective-permute-start.1
  29.9 0.2 collective-permute-start.2
  30.1 2.5 %collective-permute-start.3 = (bf16[512,512]{1,0:T(8,128)(2,1)S(1)}, bf16[512,512]{1,0:T(8,128)(2,1)S(1)}, u32[]{:S(2)}, u32[]{:S(2)}) collective-permute-start(bf16[512,512]{1,0:T(8,128)(2,1)S(1)} %collective-permute-done.refs_0_), channel_id=1, source_target_pairs={{0,6},{2,0},{4,2},{6,4},{1,7},{3,1},{5,3},{7,5},{8,14},{10,8},{12,... | collective-permute-start | bytes 1572872 | tf_op jit(solution)/shard_map/ppermute | solution.py:251
  32.6 13.9 %all_to_all.16 = bf16[16,32,128]{2,1,0:T(8,128)(2,1)} all-to-all(bf16[16,32,128]{2,1,0:T(8,128)(2,1)S(1)} %broadcast_in_dim.23), channel_id=1, replica_groups=mesh['z'=8,'xh'=2,'xl'=2,'y'=4,'c'=2] {'xl','y','c'}, dimensions={0} | all-to-all | bytes 262144 | tf_op jit(solution)/shard_map/all_to_all | solution.py:278
  46.6 0.0 collective-permute-done.1.refs_1_
  46.6 0.0 collective-permute-done.2.refs_2_
  46.6 0.6 collective-permute-start.4
  47.2 2.3 %collective-permute-start.5 = (bf16[512,512]{1,0:T(8,128)(2,1)S(1)}, bf16[512,512]{1,0:T(8,128)(2,1)}, u32[]{:S(2)}, u32[]{:S(2)}) collective-permute-start(bf16[512,512]{1,0:T(8,128)(2,1)S(1)} %collective-permute-done.1.refs_1_), channel_id=1, source_target_pairs={{0,6},{2,0},{4,2},{6,4},{1,7},{3,1},{5,3},{7,5},{8,14},{10,8},{12,... | collective-permute-start | bytes 1572872 | tf_op jit(solution)/shard_map/ppermute | solution.py:251
  49.4 3.8 %shard_map.95 = bf16[16,32,640]{2,1,0:T(8,128)(2,1)} custom-call(s32[4]{0:T(128)} %bitcast.21, s32[4]{0:T(128)} %live.3, bf16[512,128]{1,0:T(8,128)(2,1)} %bitcast.17, bf16[512,512]{1,0:T(8,128)(2,1)} %att_far.1, bf16[512,512]{1,0:T(8,128)(2,1)} %g_far.1), custom_call_target="tpu_custom_call" | custom-call | flops 67108864 | bytes 2097152 | tf_op jit(solution)/shard_map/pallas_call | solution.py:98
  53.3 9.5 %all-to-all-start.2 = ((bf16[16,32,640]{2,1,0:T(8,128)(2,1)}), bf16[16,32,640]{2,1,0:T(8,128)(2,1)S(1)}, u32[]{:S(2)}, u32[]{:S(2)}) async-start(bf16[16,32,640]{2,1,0:T(8,128)(2,1)} %shard_map.95), calls=%async_computation.2 | async-start | bytes 1310720 | tf_op jit(solution)/shard_map/all_to_all | solution.py:284
  62.8 0.0 copy-start.1
  62.8 0.0 copy-start.2
  62.8 0.0 collective-permute-done.4.refs_6_
  62.8 0.0 copy-start.5
  62.8 0.8 copy-done.5
  63.6 0.0 collective-permute-start.6
  63.6 2.7 %collective-permute-start.7 = (bf16[512,512]{1,0:T(8,128)(2,1)}, bf16[512,512]{1,0:T(8,128)(2,1)}, u32[]{:S(2)}, u32[]{:S(2)}) collective-permute-start(bf16[512,512]{1,0:T(8,128)(2,1)} %collective-permute-done.5.refs_5_), channel_id=1, source_target_pairs={{0,6},{2,0},{4,2},{6,4},{1,7},{3,1},{5,3},{7,5},{8,14},{10,8},{12,... | collective-permute-start | bytes 1572872 | tf_op jit(solution)/shard_map/ppermute | solution.py:251
  66.3 0.7 stack.37.x.place
  67.0 10.2 %collective-permute-done.6.refs_4_ = bf16[512,512]{1,0:T(8,128)(2,1)S(1)} collective-permute-done((bf16[512,512]{1,0:T(8,128)(2,1)S(1)}, bf16[512,512]{1,0:T(8,128)(2,1)S(1)}, u32[]{:S(2)}, u32[]{:S(2)}) %collective-permute-start.6) | collective-permute-done | bytes 524320 | tf_op jit(solution)/shard_map/ppermute | solution.py:251
  77.2 0.0 collective-permute-done.7.refs_0_.refs_7_
  77.2 1.2 shard_map.96.place
  78.4 5.8 %all-to-all-done.2 = bf16[16,32,640]{2,1,0:T(8,128)(2,1)S(1)} async-done(((bf16[16,32,640]{2,1,0:T(8,128)(2,1)}), bf16[16,32,640]{2,1,0:T(8,128)(2,1)S(1)}, u32[]{:S(2)}, u32[]{:S(2)}) %all-to-all-start.2) | async-done | bytes 655392 | tf_op jit(solution)/shard_map/all_to_all | solution.py:284
  84.2 0.3 shard_map.97
  84.4 0.3 collective-permute-start.8
  84.8 0.0 copy-start.3
  84.8 8.5 %shard_map.98 = (bf16[512,512]{1,0:T(8,128)(2,1)S(1)}, bf16[512,512]{1,0:T(8,128)(2,1)S(1)}, f32[512,512]{1,0:T(8,128)}) custom-call(s32[5]{0:T(128)S(1)} %copy-done.4, s32[4]{0:T(128)S(1)} %bitcast.22, s32[4]{0:T(128)S(1)} %copy-done.2, bf16[8,2,512,512]{3,2,1,0:T(8,128)(2,1)} %bitcast.27, bf16[512,512]{1,0:T(8,128)(2,1)S(1)} %collective-permute-done.refs_0_, ...), custom_call_target="tpu_custom_call" | custom-call | flops 4294967296 | bytes 14680064 | tf_op jit(solution)/shard_map/pallas_call | solution.py:237
  93.3 2.8 %collective-permute-start.10 = (bf16[512,512]{1,0:T(8,128)(2,1)S(1)}, bf16[512,512]{1,0:T(8,128)(2,1)S(1)}, u32[]{:S(2)}, u32[]{:S(2)}) collective-permute-start(bf16[512,512]{1,0:T(8,128)(2,1)S(1)} %get-tuple-element.47), channel_id=1, source_target_pairs={{0,1},{1,17},{16,0},{17,16},{2,3},{3,19},{18,2},{19,18},{4,5},{5,2... | collective-permute-start | bytes 1572872 | tf_op jit(solution)/shard_map/ppermute | solution.py:297
  96.1 5.4 %collective-permute-start.9 = (bf16[512,512]{1,0:T(8,128)(2,1)S(1)}, bf16[512,512]{1,0:T(8,128)(2,1)S(1)}, u32[]{:S(2)}, u32[]{:S(2)}) collective-permute-start(bf16[512,512]{1,0:T(8,128)(2,1)S(1)} %get-tuple-element.46), channel_id=1, source_target_pairs={{1,16},{16,1},{3,18},{18,3},{5,20},{20,5},{7,22},{22,7},{9,24},{24... | collective-permute-start | bytes 1572872 | tf_op jit(solution)/shard_map/ppermute | solution.py:296
  101.5 0.6 collective-permute-start.11
  102.1 3.2 %collective-permute-start.13 = (bf16[2,64,512]{2,1,0:T(8,128)(2,1)S(1)}, bf16[2,64,512]{2,1,0:T(8,128)(2,1)S(1)}, u32[]{:S(2)}, u32[]{:S(2)}) collective-permute-start(bf16[2,64,512]{2,1,0:T(8,128)(2,1)S(1)} %maximum_select_fusion.refs_0_), channel_id=1, source_target_pairs={{0,192},{32,224},{64,0},{96,32},{128,64},{160,96},{192,128},{224,1... | collective-permute-start | bytes 393224 | tf_op jit(solution)/shard_map/ppermute | solution.py:251
  105.4 0.1 broadcast_bitcast_fusion
  105.4 2.7 %collective-permute-done.11.refs_3_ = bf16[2,64,512]{2,1,0:T(8,128)(2,1)S(1)} collective-permute-done((bf16[2,64,512]{2,1,0:T(8,128)(2,1)S(1)}, bf16[2,64,512]{2,1,0:T(8,128)(2,1)S(1)}, u32[]{:S(2)}, u32[]{:S(2)}) %collective-permute-start.11) | collective-permute-done | bytes 131104 | tf_op jit(solution)/shard_map/ppermute | solution.py:251
  108.1 0.0 collective-permute-start.17
  108.1 1.0 collective-permute-done.13.refs_4_
  109.1 0.5 collective-permute-start.12
  109.6 2.9 %collective-permute-start.15 = (bf16[2,64,512]{2,1,0:T(8,128)(2,1)S(1)}, bf16[2,64,512]{2,1,0:T(8,128)(2,1)S(1)}, u32[]{:S(2)}, u32[]{:S(2)}) collective-permute-start(bf16[2,64,512]{2,1,0:T(8,128)(2,1)S(1)} %collective-permute-done.11.refs_3_), channel_id=1, source_target_pairs={{0,64},{32,96},{64,128},{96,160},{128,192},{160,224},{192,0},{224,... | collective-permute-start | bytes 393224 | tf_op jit(solution)/shard_map/ppermute | solution.py:251
  112.5 0.4 collective-permute-start.14
  112.9 2.3 %select_convert_fusion = bf16[512,512]{1,0:T(8,128)(2,1)} fusion(bf16[512,512]{1,0:T(8,128)(2,1)S(1)} %collective-permute-done.10, f32[512,512]{1,0:T(8,128)} %get-tuple-element.45, bf16[512,512]{1,0:T(8,128)(2,1)S(1)} %collective-permute-done.9, pred[512]{0:T(512)(128)(4,1)S(1)} %broadcast_bitcast_fusion), kind=kLoop, calls=%fused_computation | loop fusion | flops 1572864 | bytes 2621952 | tf_op jit(solution)/shard_map/convert_element_type | solution.py:304
  115.2 0.9 collective-permute-done.12.refs_5_
  116.1 0.3 collective-permute-done.14.refs_6_
  116.3 2.0 %collective-permute-done.15.refs_7_ = bf16[2,64,512]{2,1,0:T(8,128)(2,1)S(1)} collective-permute-done((bf16[2,64,512]{2,1,0:T(8,128)(2,1)S(1)}, bf16[2,64,512]{2,1,0:T(8,128)(2,1)S(1)}, u32[]{:S(2)}, u32[]{:S(2)}) %collective-permute-start.15) | collective-permute-done | bytes 131104 | tf_op jit(solution)/shard_map/ppermute | solution.py:251
  118.4 2.0 %shard_map.99 = (f32[8,64,512]{2,1,0:T(8,128)}, f32[8,64,512]{2,1,0:T(8,128)}) custom-call(s32[5]{0:T(128)S(1)} %copy-done.3, bf16[2,64,512]{2,1,0:T(8,128)(2,1)S(1)} %maximum_select_fusion.refs_0_, bf16[2,64,512]{2,1,0:T(8,128)(2,1)S(1)} %collective-permute-done.16.refs_1_, bf16[2,64,512]{2,1,0:T(8,128)(2,1)S(1)} %collective-permute-done.17.refs_2_, ...), custom_call_target="tpu_custom_call" | custom-call | bytes 4194304 | tf_op jit(solution)/shard_map/pallas_call | solution.py:154
  (20 shorter events, 0.1 us)
Async XLA Ops:
  7.2 77.6 %all-gather.3.cloned.1.call-start = ((), (), s32[]{:S(2)}) async-start(), calls=%async_computation.3 | async-start | bytes 8912896 | tf_op jit(solution)/shard_map/all_gather | solution.py:269
  7.9 21.2 %collective-permute-start = (bf16[512,512]{1,0:T(8,128)(2,1)}, bf16[512,512]{1,0:T(8,128)(2,1)S(1)}, u32[]{:S(2)}, u32[]{:S(2)}) collective-permute-start(bf16[512,512]{1,0:T(8,128)(2,1)} %g_far.1), channel_id=1, source_target_pairs={{0,0},{1,16},{16,1},{17,17},{2,2},{3,18},{18,3},{19,19},{4,4},{5,2... | collective-permute-start | bytes 1572872 | tf_op jit(solution)/shard_map/ppermute | solution.py:270
  29.1 17.5 %collective-permute-start.1 = (bf16[512,512]{1,0:T(8,128)(2,1)S(1)}, bf16[512,512]{1,0:T(8,128)(2,1)S(1)}, u32[]{:S(2)}, u32[]{:S(2)}) collective-permute-start(bf16[512,512]{1,0:T(8,128)(2,1)S(1)} %collective-permute-done.refs_0_), channel_id=1, source_target_pairs={{0,8},{8,0},{1,9},{9,1},{2,10},{10,2},{3,11},{11,3},{4,12},{12,4},... | collective-permute-start | bytes 1572872 | tf_op jit(solution)/shard_map/ppermute | solution.py:259
  29.9 16.7 %collective-permute-start.2 = (bf16[512,512]{1,0:T(8,128)(2,1)S(1)}, bf16[512,512]{1,0:T(8,128)(2,1)S(1)}, u32[]{:S(2)}, u32[]{:S(2)}) collective-permute-start(bf16[512,512]{1,0:T(8,128)(2,1)S(1)} %collective-permute-done.refs_0_), channel_id=1, source_target_pairs={{0,2},{2,4},{4,6},{6,0},{1,3},{3,5},{5,7},{7,1},{8,10},{10,12},{12... | collective-permute-start | bytes 1572872 | tf_op jit(solution)/shard_map/ppermute | solution.py:251
  30.1 16.5 %collective-permute-start.3 = (bf16[512,512]{1,0:T(8,128)(2,1)S(1)}, bf16[512,512]{1,0:T(8,128)(2,1)S(1)}, u32[]{:S(2)}, u32[]{:S(2)}) collective-permute-start(bf16[512,512]{1,0:T(8,128)(2,1)S(1)} %collective-permute-done.refs_0_), channel_id=1, source_target_pairs={{0,6},{2,0},{4,2},{6,4},{1,7},{3,1},{5,3},{7,5},{8,14},{10,8},{12,... | collective-permute-start | bytes 1572872 | tf_op jit(solution)/shard_map/ppermute | solution.py:251
  46.6 16.2 %collective-permute-start.4 = (bf16[512,512]{1,0:T(8,128)(2,1)S(1)}, bf16[512,512]{1,0:T(8,128)(2,1)S(1)}, u32[]{:S(2)}, u32[]{:S(2)}) collective-permute-start(bf16[512,512]{1,0:T(8,128)(2,1)S(1)} %collective-permute-done.2.refs_2_), channel_id=1, source_target_pairs={{0,2},{2,4},{4,6},{6,0},{1,3},{3,5},{5,7},{7,1},{8,10},{10,12},{12... | collective-permute-start | bytes 1572872 | tf_op jit(solution)/shard_map/ppermute | solution.py:251
  47.2 16.4 %collective-permute-start.5 = (bf16[512,512]{1,0:T(8,128)(2,1)S(1)}, bf16[512,512]{1,0:T(8,128)(2,1)}, u32[]{:S(2)}, u32[]{:S(2)}) collective-permute-start(bf16[512,512]{1,0:T(8,128)(2,1)S(1)} %collective-permute-done.1.refs_1_), channel_id=1, source_target_pairs={{0,6},{2,0},{4,2},{6,4},{1,7},{3,1},{5,3},{7,5},{8,14},{10,8},{12,... | collective-permute-start | bytes 1572872 | tf_op jit(solution)/shard_map/ppermute | solution.py:251
  53.3 30.9 %all-to-all-start.2 = ((bf16[16,32,640]{2,1,0:T(8,128)(2,1)}), bf16[16,32,640]{2,1,0:T(8,128)(2,1)S(1)}, u32[]{:S(2)}, u32[]{:S(2)}) async-start(bf16[16,32,640]{2,1,0:T(8,128)(2,1)} %shard_map.95), calls=%async_computation.2 | async-start | bytes 1310720 | tf_op jit(solution)/shard_map/all_to_all | solution.py:284
  62.8 22.0 %copy-start = (bf16[16,32,128]{2,1,0:T(8,128)(2,1)S(1)}, bf16[16,32,128]{2,1,0:T(8,128)(2,1)}, u32[]{:S(2)}) copy-start(bf16[16,32,128]{2,1,0:T(8,128)(2,1)} %all_to_all.16) | copy-start | bytes 393220
  62.8 22.0 %copy-start.1 = (s32[4,1]{0,1:T(1,128)S(1)}, s32[4,1]{0,1:T(1,128)}, u32[]{:S(2)}) copy-start(s32[4,1]{0,1:T(1,128)} %param.12) | copy-start | bytes 52
  62.8 22.0 %copy-start.2 = (s32[4]{0:T(128)S(1)}, s32[4]{0:T(128)}, u32[]{:S(2)}) copy-start(s32[4]{0:T(128)} %live.3) | copy-start | bytes 52
  62.8 0.8 copy-start.5
  63.6 13.6 %collective-permute-start.6 = (bf16[512,512]{1,0:T(8,128)(2,1)S(1)}, bf16[512,512]{1,0:T(8,128)(2,1)S(1)}, u32[]{:S(2)}, u32[]{:S(2)}) collective-permute-start(bf16[512,512]{1,0:T(8,128)(2,1)S(1)} %collective-permute-done.1.refs_1_), channel_id=1, source_target_pairs={{0,2},{2,4},{4,6},{6,0},{1,3},{3,5},{5,7},{7,1},{8,10},{10,12},{12... | collective-permute-start | bytes 1572872 | tf_op jit(solution)/shard_map/ppermute | solution.py:251
  63.6 13.6 %collective-permute-start.7 = (bf16[512,512]{1,0:T(8,128)(2,1)}, bf16[512,512]{1,0:T(8,128)(2,1)}, u32[]{:S(2)}, u32[]{:S(2)}) collective-permute-start(bf16[512,512]{1,0:T(8,128)(2,1)} %collective-permute-done.5.refs_5_), channel_id=1, source_target_pairs={{0,6},{2,0},{4,2},{6,4},{1,7},{3,1},{5,3},{7,5},{8,14},{10,8},{12,... | collective-permute-start | bytes 1572872 | tf_op jit(solution)/shard_map/ppermute | solution.py:251
  66.9 17.8 %copy-start.4 = (s32[5]{0:T(128)S(1)}, s32[5]{0:T(128)}, u32[]{:S(2)}) copy-start(s32[5]{0:T(128)} %stack.37.x.place) | copy-start | bytes 64
  84.4 8.9 %collective-permute-start.8 = (bf16[64,512]{1,0:T(8,128)(2,1)S(1)}, bf16[64,512]{1,0:T(8,128)(2,1)S(1)}, u32[]{:S(2)}, u32[]{:S(2)}) collective-permute-start(bf16[64,512]{1,0:T(8,128)(2,1)S(1)} %shard_map.97), channel_id=1, source_target_pairs={{0,16},{16,0},{1,17},{17,1},{2,18},{18,2},{3,19},{19,3},{4,20},{20... | collective-permute-start | bytes 196616 | tf_op jit(solution)/shard_map/ppermute | solution.py:259
  84.8 33.6 %copy-start.3 = (s32[5]{0:T(128)S(1)}, s32[5]{0:T(128)}, u32[]{:S(2)}) copy-start(s32[5]{0:T(128)} %shard_map.96.place) | copy-start | bytes 64
  93.3 16.3 %collective-permute-start.10 = (bf16[512,512]{1,0:T(8,128)(2,1)S(1)}, bf16[512,512]{1,0:T(8,128)(2,1)S(1)}, u32[]{:S(2)}, u32[]{:S(2)}) collective-permute-start(bf16[512,512]{1,0:T(8,128)(2,1)S(1)} %get-tuple-element.47), channel_id=1, source_target_pairs={{0,1},{1,17},{16,0},{17,16},{2,3},{3,19},{18,2},{19,18},{4,5},{5,2... | collective-permute-start | bytes 1572872 | tf_op jit(solution)/shard_map/ppermute | solution.py:297
  96.1 16.4 %collective-permute-start.9 = (bf16[512,512]{1,0:T(8,128)(2,1)S(1)}, bf16[512,512]{1,0:T(8,128)(2,1)S(1)}, u32[]{:S(2)}, u32[]{:S(2)}) collective-permute-start(bf16[512,512]{1,0:T(8,128)(2,1)S(1)} %get-tuple-element.46), channel_id=1, source_target_pairs={{1,16},{16,1},{3,18},{18,3},{5,20},{20,5},{7,22},{22,7},{9,24},{24... | collective-permute-start | bytes 1572872 | tf_op jit(solution)/shard_map/ppermute | solution.py:296
  101.5 6.6 %collective-permute-start.11 = (bf16[2,64,512]{2,1,0:T(8,128)(2,1)S(1)}, bf16[2,64,512]{2,1,0:T(8,128)(2,1)S(1)}, u32[]{:S(2)}, u32[]{:S(2)}) collective-permute-start(bf16[2,64,512]{2,1,0:T(8,128)(2,1)S(1)} %maximum_select_fusion.refs_0_), channel_id=1, source_target_pairs={{0,64},{32,96},{64,128},{96,160},{128,192},{160,224},{192,0},{224,... | collective-permute-start | bytes 393224 | tf_op jit(solution)/shard_map/ppermute | solution.py:251
  102.1 7.0 %collective-permute-start.13 = (bf16[2,64,512]{2,1,0:T(8,128)(2,1)S(1)}, bf16[2,64,512]{2,1,0:T(8,128)(2,1)S(1)}, u32[]{:S(2)}, u32[]{:S(2)}) collective-permute-start(bf16[2,64,512]{2,1,0:T(8,128)(2,1)S(1)} %maximum_select_fusion.refs_0_), channel_id=1, source_target_pairs={{0,192},{32,224},{64,0},{96,32},{128,64},{160,96},{192,128},{224,1... | collective-permute-start | bytes 393224 | tf_op jit(solution)/shard_map/ppermute | solution.py:251
  105.4 12.9 %collective-permute-start.16 = (bf16[2,64,512]{2,1,0:T(8,128)(2,1)S(1)}, bf16[2,64,512]{2,1,0:T(8,128)(2,1)S(1)}, u32[]{:S(2)}, u32[]{:S(2)}) collective-permute-start(bf16[2,64,512]{2,1,0:T(8,128)(2,1)S(1)} %maximum_select_fusion.refs_0_), channel_id=1, source_target_pairs={{0,32},{32,64},{64,96},{96,128},{128,160},{160,192},{192,224},{224... | collective-permute-start | bytes 393224 | tf_op jit(solution)/shard_map/ppermute | solution.py:251
  108.1 10.2 %collective-permute-start.17 = (bf16[2,64,512]{2,1,0:T(8,128)(2,1)S(1)}, bf16[2,64,512]{2,1,0:T(8,128)(2,1)S(1)}, u32[]{:S(2)}, u32[]{:S(2)}) collective-permute-start(bf16[2,64,512]{2,1,0:T(8,128)(2,1)S(1)} %maximum_select_fusion.refs_0_), channel_id=1, source_target_pairs={{0,224},{32,0},{64,32},{96,64},{128,96},{160,128},{192,160},{224,1... | collective-permute-start | bytes 393224 | tf_op jit(solution)/shard_map/ppermute | solution.py:251
  109.1 7.0 %collective-permute-start.12 = (bf16[2,64,512]{2,1,0:T(8,128)(2,1)S(1)}, bf16[2,64,512]{2,1,0:T(8,128)(2,1)S(1)}, u32[]{:S(2)}, u32[]{:S(2)}) collective-permute-start(bf16[2,64,512]{2,1,0:T(8,128)(2,1)S(1)} %collective-permute-done.11.refs_3_), channel_id=1, source_target_pairs={{0,32},{32,64},{64,96},{96,128},{128,160},{160,192},{192,224},{224... | collective-permute-start | bytes 393224 | tf_op jit(solution)/shard_map/ppermute | solution.py:251
  109.6 8.8 %collective-permute-start.15 = (bf16[2,64,512]{2,1,0:T(8,128)(2,1)S(1)}, bf16[2,64,512]{2,1,0:T(8,128)(2,1)S(1)}, u32[]{:S(2)}, u32[]{:S(2)}) collective-permute-start(bf16[2,64,512]{2,1,0:T(8,128)(2,1)S(1)} %collective-permute-done.11.refs_3_), channel_id=1, source_target_pairs={{0,64},{32,96},{64,128},{96,160},{128,192},{160,224},{192,0},{224,... | collective-permute-start | bytes 393224 | tf_op jit(solution)/shard_map/ppermute | solution.py:251
  112.5 3.8 %collective-permute-start.14 = (bf16[2,64,512]{2,1,0:T(8,128)(2,1)S(1)}, bf16[2,64,512]{2,1,0:T(8,128)(2,1)S(1)}, u32[]{:S(2)}, u32[]{:S(2)}) collective-permute-start(bf16[2,64,512]{2,1,0:T(8,128)(2,1)S(1)} %collective-permute-done.13.refs_4_), channel_id=1, source_target_pairs={{0,224},{32,0},{64,32},{96,64},{128,96},{160,128},{192,160},{224,1... | collective-permute-start | bytes 393224 | tf_op jit(solution)/shard_map/ppermute | solution.py:251
Sparse Core Ops, SparseCore 0:
  9.8 62.1 all-gather.2

commit v6 on v5

--- a/solution.py
+++ b/solution.py
@@ -19,7 +19,8 @@
 GROUP = RANK // Z
 ROWS = 512
 COLS = 512
-PAD = 128
+LANES = 128
+IDS = 8
 VMEM = 24 << 20
 FULL = 56 << 20
 OFFSETS = (0, -1, 1, -2, 2, -3, 3, -4)
@@ -65,7 +66,7 @@
     )(roles, att, g, down, up)
 
 
-def outer_kernel(roles, live, lb, att_far, g_far, out, att, g, sems):
+def outer_kernel(live, lb, att_far, g_far, out, att, g, sems):
     copies = []
     for b in range(BLOCKS):
         rows = pl.ds(b * BLOCK, BLOCK)
@@ -84,21 +85,16 @@
             ups.append(dot(ranks[:, :RANK], g[rows, :], 0, 0))
             downs.append(dot(ranks[:, RANK:], att[rows, :], 0, 0))
         at = pl.ds(2 * GROUP * pair, 2 * GROUP)
-        first = lax.broadcasted_iota(jnp.int32, (2 * GROUP, PAD), 0) < GROUP
-        ids = jnp.where(first, roles[2 * pair], roles[2 * pair + 1])
-        ids = ids.astype(f32).astype(bf16)
         for z in range(Z):
             for o, terms in enumerate((ups, downs)):
                 part = [t[GROUP * z : GROUP * (z + 1), :] for t in terms]
-                out[2 * z + o, at, :COLS] = jnp.concatenate(part, axis=0).astype(bf16)
-                out[2 * z + o, at, COLS:] = ids
-
-
-def outer_parts(roles, live, lb, att, g):
+                out[2 * z + o, at, :] = jnp.concatenate(part, axis=0).astype(bf16)
+
+
+def outer_parts(live, lb, att, g):
     return pl.pallas_call(
         outer_kernel,
-        in_specs=[pl.BlockSpec(memory_space=pltpu.SMEM)] * 2
-        + [pl.BlockSpec(memory_space=pltpu.VMEM)]
+        in_specs=[pl.BlockSpec(memory_space=pltpu.SMEM), pl.BlockSpec(memory_space=pltpu.VMEM)]
         + [pl.BlockSpec(memory_space=pl.ANY)] * 2,
         out_specs=pl.BlockSpec(memory_space=pltpu.VMEM),
         scratch_shapes=[
@@ -106,31 +102,41 @@
             pltpu.VMEM((ROWS, COLS), bf16),
             pltpu.SemaphoreType.DMA((BLOCKS, 2)),
         ],
-        out_shape=jax.ShapeDtypeStruct((Z * XH, BLOCKS * GROUP, COLS + PAD), bf16),
+        out_shape=jax.ShapeDtypeStruct((Z * XH, BLOCKS * GROUP, COLS), bf16),
         compiler_params=pltpu.CompilerParams(vmem_limit_bytes=FULL),
         cost_estimate=pl.CostEstimate(flops=2 * 2 * ROWS * COLS * RANK, bytes_accessed=2 << 20, transcendentals=0),
-    )(roles, live, lb, att, g)
-
-
-def sum_kernel(scale, recv, out):
-    got = recv[...]
-    shape = (Z * XH * BLOCKS * GROUP, PAD)
-    row = lax.broadcasted_iota(jnp.int32, shape, 0)
-    lane = lax.broadcasted_iota(jnp.int32, shape, 1)
-    role = got[:, COLS:].astype(f32)
-    pick = (role == (lane // GROUP).astype(f32)) & (lane % GROUP == row % GROUP)
-    total = dot(pick.astype(f32).astype(bf16), got[:, :COLS], 0, 0)
+    )(live, lb, att, g)
+
+
+def sum_kernel(scale, place, got, ids, out):
+    lane = lax.broadcasted_iota(jnp.int32, (GROUP, LANES), 1)
+    row = lax.broadcasted_iota(jnp.int32, (GROUP, LANES), 0)
+    rank = lane % GROUP == row
+    wanted = (lane // GROUP).astype(f32)
+    pick = []
+    for z in range(Z):
+        for h in range(XH):
+            theirs = ids[(place[0] ^ z) * XH + (place[1] ^ h)]
+            for b in range(BLOCKS):
+                at = IDS // BLOCKS * b
+                role = jnp.broadcast_to(theirs[at : at + 1, :], (GROUP, LANES))
+                pick.append(jnp.where(rank & (role == wanted), 1.0, 0.0))
+    pick = jnp.concatenate(pick, axis=0).astype(bf16)
+    total = dot(pick, got[...], 0, 0)
     out[...] = (scale * total[: ROLES * GROUP, :]).astype(bf16)
 
 
-def sum_parts(recv, scale):
+def sum_parts(place, recv, ids, scale):
     rows = Z * XH * BLOCKS * GROUP
+    here = pl.BlockSpec(memory_space=pltpu.VMEM)
     return pl.pallas_call(
         functools.partial(sum_kernel, scale),
+        in_specs=[pl.BlockSpec(memory_space=pltpu.SMEM)] + [here] * 2,
+        out_specs=here,
         out_shape=jax.ShapeDtypeStruct((ROLES * GROUP, COLS), bf16),
         compiler_params=pltpu.CompilerParams(vmem_limit_bytes=16 << 20),
-        cost_estimate=pl.CostEstimate(flops=2 * rows * PAD * COLS, bytes_accessed=2 << 20, transcendentals=0),
-    )(recv.reshape(rows, COLS + PAD))
+        cost_estimate=pl.CostEstimate(flops=2 * rows * LANES * COLS, bytes_accessed=2 << 20, transcendentals=0),
+    )(place, recv.reshape(rows, COLS), ids)
 
 
 def spread_kernel(place, *refs):
@@ -270,24 +276,29 @@
     turned = lax.ppermute(grad_out, ("xh", "c"), [(0, 0), (1, 2), (2, 1), (3, 3)])
     ranks = rank_parts(roles, attention_output, grad_out, adapter_down, adapter_up)
     ranks = lax.all_to_all(ranks.reshape(16, ROWS // 16, 2 * RANK), TP, 0, 0)
-    ranks, turned = tie(ranks, turned)
+    ids = jnp.broadcast_to(jnp.repeat(roles, IDS // BLOCKS)[:, None], (IDS, LANES)).astype(f32)
+    other = trade(ids, "xh", XH, 1)
+    ranks, turned, other = tie(ranks, turned, other)
+    ids = jnp.stack([ids, other])
+    ids = jnp.concatenate([ids] + [trade(ids, "z", Z, bits) for bits in (1, 2, 3)])
 
     beside = trade(turned, "xl", XL, 1)
     up1, down1 = shift(turned, "y", Y, 1), shift(turned, "y", Y, -1)
     mine = jnp.sum(ranks, axis=0).astype(bf16)
     lb = lax.all_to_all(jnp.broadcast_to(mine[None], (16,) + mine.shape), TP, 0, 0)
-    lb, beside, up1, down1 = tie(lb.reshape(ROWS, 2 * RANK), beside, up1, down1)
+    lb, beside, up1, down1, ids = tie(lb.reshape(ROWS, 2 * RANK), beside, up1, down1, ids)
+    ids = jnp.concatenate([ids, trade(ids, "z", Z, 4)])
 
     up2, beside_down1 = shift(up1, "y", Y, 1), shift(beside, "y", Y, -1)
-    outer = outer_parts(roles, live, lb, attention_output, grad_out)
-    up2, beside_down1, beside, _ = tie(up2, beside_down1, beside, outer)
+    outer = outer_parts(live, lb, attention_output, grad_out)
+    up2, beside_down1, beside, ids, _ = tie(up2, beside_down1, beside, ids, outer)
     outer = lax.all_to_all(outer, FS, 0, 0)
     beside_up1, beside_down2 = shift(beside, "y", Y, 1), shift(beside_down1, "y", Y, -1)
 
     beside_up1, beside_down2 = tie(beside_up1, beside_down2)
     mark = arrived(place, beside_down2)
-    outer, mark = tie(outer, mark)
-    total = sum_parts(outer, grad_scale)
+    outer, mark, ids = tie(outer, mark, ids)
+    total = sum_parts(place, outer, ids, grad_scale)
     other = trade(total, "xh", XH, 1)
     pieces = [turned, beside, up1, down1, beside_up1, beside_down1, up2, beside_down2]
     far, near, own = base_parts(place, roles, live, wide, *pieces, lb, adapter_down)

time: 128 us -> 128 us (level)
  blocking collectives: 25.7 us -> 0 us
  starting transfers between devices: 40.7 us -> 58.2 us
  waiting for transfers between devices: 23.6 us -> 30.1 us
    all_to_all x2 -> x0, blocking collectives: 25.7 us -> none  [the longest x1 13.9 us: shards(): lax.all_to_all(jnp.broadcast_to(mine[None], (16,) + mine.shape), TP, 0, 0)]
    ppermute x2 -> x7, starting transfers between devices: 1.11 us -> 11.8 us  [trade(): return lax.ppermute(x, axis, [(i, i ^ bit) for i in range(size)])]
    all_to_all x0 -> x2, starting transfers between devices: none -> 9.9 us  [the longest x1 5.27 us: shards(): lax.all_to_all(jnp.broadcast_to(mine[None], (16,) + mine.shape), TP, 0, 0)]
    ppermute x2 -> x7, waiting for transfers between devices: 0.01 us -> 7.88 us  [trade(): return lax.ppermute(x, axis, [(i, i ^ bit) for i in range(size)])]
    all_to_all x1, starting transfers between devices: 9.47 us -> 4.16 us  [shards(): outer = lax.all_to_all(outer, FS, 0, 0)]
    ppermute x13, waiting for transfers between devices: 17.1 us -> 13.1 us  [shift(): return lax.ppermute(x, axis, [(i, (i + step) % size) for i in range(size)])]
    ppermute x13, starting transfers between devices: 15.8 us -> 19 us  [shift(): return lax.ppermute(x, axis, [(i, (i + step) % size) for i in range(size)])]
    all_to_all x0 -> x2, waiting for transfers between devices: none -> 2.95 us  [the longest x1 1.57 us: shards(): ranks = lax.all_to_all(ranks.reshape(16, ROWS // 16, 2 * RANK), TP, 0, 0)]
  transfers between devices with their start and end apart: 20 -> 27, of which waited for: 7 -> 9; matrix products, arithmetic and copies ran while one was open for 2% -> 4% of each run, Pallas kernels for 13% -> 14%
where the time goes in v6:
time: 128 us; the launch traced here: 127 us
  starting transfers between devices  58.2 us (45%)
  waiting for transfers between devices  30.1 us (24%)
  Pallas kernels  19.6 us (15%)
  between operations  14.3 us (11%)
  other arithmetic  2.97 us (2%)
  local copies, waits for them, and re-layouts  1.73 us (1%)
    ppermute x13, starting transfers between devices, shift(): return lax.ppermute(x, axis, [(i, (i + step) % size) for i in range(size)])  19 us
    ppermute x13, waiting for transfers between devices, shift(): return lax.ppermute(x, axis, [(i, (i + step) % size) for i in range(size)])  13.1 us
    ppermute x7, starting transfers between devices, trade(): return lax.ppermute(x, axis, [(i, i ^ bit) for i in range(size)])  11.8 us
    pallas_call x1, Pallas kernels, base_parts(): pl.pallas_call(base_kernel, grid_spec=spec, out_shape=[jax.ShapeDtypeStru...  8.5 us
    ppermute x7, waiting for transfers between devices, trade(): return lax.ppermute(x, axis, [(i, i ^ bit) for i in range(size)])  7.88 us
    ppermute x1, starting transfers between devices, shards(): lax.ppermute(grad_out, ('xh', 'c'), [(0, 0), (1, 2), (2, 1), (3, 3)])  6.04 us
    all_to_all x1, waiting for transfers between devices, shards(): outer = lax.all_to_all(outer, FS, 0, 0)  5.56 us
    all_to_all x1, starting transfers between devices, shards(): lax.all_to_all(jnp.broadcast_to(mine[None], (16,) + mine.shape), TP, 0, 0)  5.27 us
  transfers between devices with their start and end apart: 27, of which 9 were waited for; matrix products, arithmetic and copies ran while one was open for 4% of the time, Pallas kernels for 14%

profile of v6, /device:TPU:1, one launch (start us, length us, event | category | flops | bytes accessed | tf_op | source)
XLA Modules:
  0.0 127.0 jit_solution(4227991109896259474)
XLA Ops:
  7.2 0.7 all-gather.3.cloned.1.call-update
  7.9 6.0 %collective-permute-start = (bf16[512,512]{1,0:T(8,128)(2,1)}, bf16[512,512]{1,0:T(8,128)(2,1)S(1)}, u32[]{:S(2)}, u32[]{:S(2)}) collective-permute-start(bf16[512,512]{1,0:T(8,128)(2,1)} %g_far.1), channel_id=1, source_target_pairs={{0,0},{1,16},{16,1},{17,17},{2,2},{3,18},{18,3},{19,19},{4,4},{5,2... | collective-permute-start | bytes 1572872 | tf_op jit(solution)/shard_map/ppermute | solution.py:276
  13.9 3.4 %shard_map.94 = f32[512,128]{1,0:T(8,128)} custom-call(s32[4]{0:T(128)} %bitcast.23, bf16[512,512]{1,0:T(8,128)(2,1)} %att_far.1, bf16[512,512]{1,0:T(8,128)(2,1)} %g_far.1, bf16[8,64,512]{2,1,0:T(8,128)(2,1)} %bitcast.26, bf16[8,64,512]{2,1,0:T(8,128)(2,1)} %up.1), custom_call_target="tpu_custom_call" | custom-call | flops 67108864 | bytes 2097152 | tf_op jit(solution)/shard_map/pallas_call | solution.py:60
  17.3 4.6 %all-to-all-start = ((f32[16,32,128]{2,1,0:T(8,128)}), f32[16,32,128]{2,1,0:T(8,128)S(1)}, u32[]{:S(2)}, u32[]{:S(2)}) async-start(f32[16,32,128]{2,1,0:T(8,128)} %bitcast.25), calls=%async_computation | async-start | bytes 524288 | tf_op jit(solution)/shard_map/all_to_all | solution.py:278
  21.9 0.7 bitcast_convert_fusion
  22.7 0.1 convert_element_type.25
  22.8 0.1 broadcast_in_dim.32
  22.8 1.5 %collective-permute-start.1 = (f32[8,128]{1,0:T(8,128)S(1)}, f32[8,128]{1,0:T(8,128)S(1)}, u32[]{:S(2)}, u32[]{:S(2)}) collective-permute-start(f32[8,128]{1,0:T(8,128)S(1)} %broadcast_in_dim.32), channel_id=1, source_target_pairs={{0,16},{16,0},{1,17},{17,1},{2,18},{18,2},{3,19},{19,3},{4,20},{20... | collective-permute-start | bytes 12296 | tf_op jit(solution)/shard_map/ppermute | solution.py:265
  24.4 3.2 %collective-permute-done.1 = f32[8,128]{1,0:T(8,128)S(1)} collective-permute-done((f32[8,128]{1,0:T(8,128)S(1)}, f32[8,128]{1,0:T(8,128)S(1)}, u32[]{:S(2)}, u32[]{:S(2)}) %collective-permute-start.1) | collective-permute-done | bytes 4128 | tf_op jit(solution)/shard_map/ppermute | solution.py:265
  27.6 1.6 %all-to-all-done = f32[16,32,128]{2,1,0:T(8,128)S(1)} async-done(((f32[16,32,128]{2,1,0:T(8,128)}), f32[16,32,128]{2,1,0:T(8,128)S(1)}, u32[]{:S(2)}, u32[]{:S(2)}) %all-to-all-start) | async-done | bytes 262176 | tf_op jit(solution)/shard_map/all_to_all | solution.py:278
  29.1 0.8 collective-permute-start.2
  29.9 0.2 collective-permute-start.3
  30.1 2.5 %collective-permute-start.4 = (bf16[512,512]{1,0:T(8,128)(2,1)S(1)}, bf16[512,512]{1,0:T(8,128)(2,1)S(1)}, u32[]{:S(2)}, u32[]{:S(2)}) collective-permute-start(bf16[512,512]{1,0:T(8,128)(2,1)S(1)} %collective-permute-done.refs_0_), channel_id=1, source_target_pairs={{0,6},{2,0},{4,2},{6,4},{1,7},{3,1},{5,3},{7,5},{8,14},{10,8},{12,... | collective-permute-start | bytes 1572872 | tf_op jit(solution)/shard_map/ppermute | solution.py:257
  32.7 1.6 %collective-permute-start.5 = (f32[2,8,128]{2,1,0:T(8,128)S(1)}, f32[2,8,128]{2,1,0:T(8,128)S(1)}, u32[]{:S(2)}, u32[]{:S(2)}) collective-permute-start(f32[2,8,128]{2,1,0:T(8,128)S(1)} %pad_maximum_fusion.1), channel_id=1, source_target_pairs={{0,32},{32,0},{64,96},{96,64},{128,160},{160,128},{192,224},{224,1... | collective-permute-start | bytes 24584 | tf_op jit(solution)/shard_map/ppermute | solution.py:265
  34.3 3.0 %collective-permute-start.6 = (f32[2,8,128]{2,1,0:T(8,128)S(1)}, f32[2,8,128]{2,1,0:T(8,128)S(1)}, u32[]{:S(2)}, u32[]{:S(2)}) collective-permute-start(f32[2,8,128]{2,1,0:T(8,128)S(1)} %pad_maximum_fusion.1), channel_id=1, source_target_pairs={{0,64},{32,96},{64,0},{96,32},{128,192},{160,224},{192,128},{224,1... | collective-permute-start | bytes 24584 | tf_op jit(solution)/shard_map/ppermute | solution.py:265
  37.3 0.7 broadcast_in_dim.33
  38.0 5.3 %all-to-all-start.1 = ((bf16[16,32,128]{2,1,0:T(8,128)(2,1)}), bf16[16,32,128]{2,1,0:T(8,128)(2,1)S(1)}, u32[]{:S(2)}, u32[]{:S(2)}) async-start(bf16[16,32,128]{2,1,0:T(8,128)(2,1)} %broadcast_in_dim.33), calls=%async_computation.1 | async-start | bytes 262144 | tf_op jit(solution)/shard_map/all_to_all | solution.py:288
  43.3 0.1 collective-permute-start.7
  43.4 4.7 %collective-permute-done.7 = f32[2,8,128]{2,1,0:T(8,128)S(1)} collective-permute-done((f32[2,8,128]{2,1,0:T(8,128)S(1)}, f32[2,8,128]{2,1,0:T(8,128)S(1)}, u32[]{:S(2)}, u32[]{:S(2)}) %collective-permute-start.7) | collective-permute-done | bytes 8224 | tf_op jit(solution)/shard_map/ppermute | solution.py:265
  48.1 1.4 %all-to-all-done.1 = bf16[16,32,128]{2,1,0:T(8,128)(2,1)S(1)} async-done(((bf16[16,32,128]{2,1,0:T(8,128)(2,1)}), bf16[16,32,128]{2,1,0:T(8,128)(2,1)S(1)}, u32[]{:S(2)}, u32[]{:S(2)}) %all-to-all-start.1) | async-done | bytes 131104 | tf_op jit(solution)/shard_map/all_to_all | solution.py:288
  49.5 0.5 collective-permute-start.8
  50.0 2.2 %collective-permute-start.9 = (bf16[512,512]{1,0:T(8,128)(2,1)S(1)}, bf16[512,512]{1,0:T(8,128)(2,1)}, u32[]{:S(2)}, u32[]{:S(2)}) collective-permute-start(bf16[512,512]{1,0:T(8,128)(2,1)S(1)} %collective-permute-done.2.refs_1_), channel_id=1, source_target_pairs={{0,6},{2,0},{4,2},{6,4},{1,7},{3,1},{5,3},{7,5},{8,14},{10,8},{12,... | collective-permute-start | bytes 1572872 | tf_op jit(solution)/shard_map/ppermute | solution.py:257
  52.3 4.2 %collective-permute-start.10 = (f32[8,8,128]{2,1,0:T(8,128)S(1)}, f32[8,8,128]{2,1,0:T(8,128)S(1)}, u32[]{:S(2)}, u32[]{:S(2)}) collective-permute-start(f32[8,8,128]{2,1,0:T(8,128)S(1)} %constant_dynamic-update-slice_fusion), channel_id=1, source_target_pairs={{0,128},{32,160},{64,192},{96,224},{128,0},{160,32},{192,64},{224,... | collective-permute-start | bytes 98312 | tf_op jit(solution)/shard_map/ppermute | solution.py:265
  56.5 3.8 %shard_map.95 = bf16[16,32,512]{2,1,0:T(8,128)(2,1)} custom-call(s32[4]{0:T(128)} %live.3, bf16[512,128]{1,0:T(8,128)(2,1)} %bitcast.20, bf16[512,512]{1,0:T(8,128)(2,1)} %att_far.1, bf16[512,512]{1,0:T(8,128)(2,1)} %g_far.1), custom_call_target="tpu_custom_call" | custom-call | flops 67108864 | bytes 2097152 | tf_op jit(solution)/shard_map/pallas_call | solution.py:95
  60.3 4.2 %all-to-all-start.2 = ((bf16[16,32,512]{2,1,0:T(8,128)(2,1)}), bf16[16,32,512]{2,1,0:T(8,128)(2,1)S(1)}, u32[]{:S(2)}, u32[]{:S(2)}) async-start(bf16[16,32,512]{2,1,0:T(8,128)(2,1)} %shard_map.95), calls=%async_computation.2 | async-start | bytes 1048576 | tf_op jit(solution)/shard_map/all_to_all | solution.py:295
  64.6 0.1 collective-permute-start.11
  64.6 2.7 %collective-permute-start.12 = (bf16[512,512]{1,0:T(8,128)(2,1)}, bf16[512,512]{1,0:T(8,128)(2,1)}, u32[]{:S(2)}, u32[]{:S(2)}) collective-permute-start(bf16[512,512]{1,0:T(8,128)(2,1)} %collective-permute-done.9.refs_5_), channel_id=1, source_target_pairs={{0,6},{2,0},{4,2},{6,4},{1,7},{3,1},{5,3},{7,5},{8,14},{10,8},{12,... | collective-permute-start | bytes 1572872 | tf_op jit(solution)/shard_map/ppermute | solution.py:257
  67.3 0.6 stack.46.x.place
  67.9 9.6 %collective-permute-done.11.refs_4_ = bf16[512,512]{1,0:T(8,128)(2,1)S(1)} collective-permute-done((bf16[512,512]{1,0:T(8,128)(2,1)S(1)}, bf16[512,512]{1,0:T(8,128)(2,1)S(1)}, u32[]{:S(2)}, u32[]{:S(2)}) %collective-permute-start.11) | collective-permute-done | bytes 524320 | tf_op jit(solution)/shard_map/ppermute | solution.py:257
  77.5 1.2 shard_map.96.place
  78.7 5.6 %all-to-all-done.2 = bf16[16,32,512]{2,1,0:T(8,128)(2,1)S(1)} async-done(((bf16[16,32,512]{2,1,0:T(8,128)(2,1)}), bf16[16,32,512]{2,1,0:T(8,128)(2,1)S(1)}, u32[]{:S(2)}, u32[]{:S(2)}) %all-to-all-start.2) | async-done | bytes 524320 | tf_op jit(solution)/shard_map/all_to_all | solution.py:295
  84.2 0.8 shard_map.97
  85.0 0.6 collective-permute-start.13
  85.6 8.5 %shard_map.98 = (bf16[512,512]{1,0:T(8,128)(2,1)S(1)}, bf16[512,512]{1,0:T(8,128)(2,1)S(1)}, f32[512,512]{1,0:T(8,128)}) custom-call(s32[5]{0:T(128)S(1)} %copy-done.2, s32[4]{0:T(128)S(1)} %bitcast.24, s32[4]{0:T(128)S(1)} %copy-done.3, bf16[8,2,512,512]{3,2,1,0:T(8,128)(2,1)} %bitcast.30, bf16[512,512]{1,0:T(8,128)(2,1)S(1)} %collective-permute-done.refs_0_, ...), custom_call_target="tpu_custom_call" | custom-call | flops 4294967296 | bytes 14680064 | tf_op jit(solution)/shard_map/pallas_call | solution.py:243
  94.1 2.8 %collective-permute-start.15 = (bf16[512,512]{1,0:T(8,128)(2,1)S(1)}, bf16[512,512]{1,0:T(8,128)(2,1)S(1)}, u32[]{:S(2)}, u32[]{:S(2)}) collective-permute-start(bf16[512,512]{1,0:T(8,128)(2,1)S(1)} %get-tuple-element.55), channel_id=1, source_target_pairs={{0,1},{1,17},{16,0},{17,16},{2,3},{3,19},{18,2},{19,18},{4,5},{5,2... | collective-permute-start | bytes 1572872 | tf_op jit(solution)/shard_map/ppermute | solution.py:308
  96.9 4.6 %collective-permute-start.14 = (bf16[512,512]{1,0:T(8,128)(2,1)S(1)}, bf16[512,512]{1,0:T(8,128)(2,1)S(1)}, u32[]{:S(2)}, u32[]{:S(2)}) collective-permute-start(bf16[512,512]{1,0:T(8,128)(2,1)S(1)} %get-tuple-element.54), channel_id=1, source_target_pairs={{1,16},{16,1},{3,18},{18,3},{5,20},{20,5},{7,22},{22,7},{9,24},{24... | collective-permute-start | bytes 1572872 | tf_op jit(solution)/shard_map/ppermute | solution.py:307
  101.5 0.1 collective-permute-start.16
  101.6 3.6 %collective-permute-start.18 = (bf16[2,64,512]{2,1,0:T(8,128)(2,1)S(1)}, bf16[2,64,512]{2,1,0:T(8,128)(2,1)S(1)}, u32[]{:S(2)}, u32[]{:S(2)}) collective-permute-start(bf16[2,64,512]{2,1,0:T(8,128)(2,1)S(1)} %maximum_select_fusion.refs_0_), channel_id=1, source_target_pairs={{0,192},{32,224},{64,0},{96,32},{128,64},{160,96},{192,128},{224,1... | collective-permute-start | bytes 393224 | tf_op jit(solution)/shard_map/ppermute | solution.py:257
  105.2 0.1 broadcast_bitcast_fusion
  105.2 2.7 %collective-permute-done.16.refs_3_ = bf16[2,64,512]{2,1,0:T(8,128)(2,1)S(1)} collective-permute-done((bf16[2,64,512]{2,1,0:T(8,128)(2,1)S(1)}, bf16[2,64,512]{2,1,0:T(8,128)(2,1)S(1)}, u32[]{:S(2)}, u32[]{:S(2)}) %collective-permute-start.16) | collective-permute-done | bytes 131104 | tf_op jit(solution)/shard_map/ppermute | solution.py:257
  107.9 1.4 %collective-permute-start.22 = (bf16[2,64,512]{2,1,0:T(8,128)(2,1)S(1)}, bf16[2,64,512]{2,1,0:T(8,128)(2,1)S(1)}, u32[]{:S(2)}, u32[]{:S(2)}) collective-permute-start(bf16[2,64,512]{2,1,0:T(8,128)(2,1)S(1)} %maximum_select_fusion.refs_0_), channel_id=1, source_target_pairs={{0,224},{32,0},{64,32},{96,64},{128,96},{160,128},{192,160},{224,1... | collective-permute-start | bytes 393224 | tf_op jit(solution)/shard_map/ppermute | solution.py:257
  109.4 0.5 collective-permute-done.18.refs_4_
  109.9 0.5 collective-permute-start.17
  110.4 2.5 %collective-permute-start.20 = (bf16[2,64,512]{2,1,0:T(8,128)(2,1)S(1)}, bf16[2,64,512]{2,1,0:T(8,128)(2,1)S(1)}, u32[]{:S(2)}, u32[]{:S(2)}) collective-permute-start(bf16[2,64,512]{2,1,0:T(8,128)(2,1)S(1)} %collective-permute-done.16.refs_3_), channel_id=1, source_target_pairs={{0,64},{32,96},{64,128},{96,160},{128,192},{160,224},{192,0},{224,... | collective-permute-start | bytes 393224 | tf_op jit(solution)/shard_map/ppermute | solution.py:257
  113.0 2.7 %collective-permute-start.19 = (bf16[2,64,512]{2,1,0:T(8,128)(2,1)S(1)}, bf16[2,64,512]{2,1,0:T(8,128)(2,1)S(1)}, u32[]{:S(2)}, u32[]{:S(2)}) collective-permute-start(bf16[2,64,512]{2,1,0:T(8,128)(2,1)S(1)} %collective-permute-done.18.refs_4_), channel_id=1, source_target_pairs={{0,224},{32,0},{64,32},{96,64},{128,96},{160,128},{192,160},{224,1... | collective-permute-start | bytes 393224 | tf_op jit(solution)/shard_map/ppermute | solution.py:257
  115.6 2.2 %select_convert_fusion = bf16[512,512]{1,0:T(8,128)(2,1)} fusion(bf16[512,512]{1,0:T(8,128)(2,1)S(1)} %collective-permute-done.15, f32[512,512]{1,0:T(8,128)} %get-tuple-element.53, bf16[512,512]{1,0:T(8,128)(2,1)S(1)} %collective-permute-done.14, pred[512]{0:T(512)(128)(4,1)S(1)} %broadcast_bitcast_fusion), kind=kLoop, calls=%fused_computation | loop fusion | flops 1572864 | bytes 2621952 | tf_op jit(solution)/shard_map/convert_element_type | solution.py:315
  117.9 0.2 collective-permute-done.20.refs_7_
  118.1 2.0 %shard_map.99 = (f32[8,64,512]{2,1,0:T(8,128)}, f32[8,64,512]{2,1,0:T(8,128)}) custom-call(s32[5]{0:T(128)S(1)} %copy-done.5, bf16[2,64,512]{2,1,0:T(8,128)(2,1)S(1)} %maximum_select_fusion.refs_0_, bf16[2,64,512]{2,1,0:T(8,128)(2,1)S(1)} %collective-permute-done.21.refs_1_, bf16[2,64,512]{2,1,0:T(8,128)(2,1)S(1)} %collective-permute-done.22.refs_2_, ...), custom_call_target="tpu_custom_call" | custom-call | bytes 4194304 | tf_op jit(solution)/shard_map/pallas_call | solution.py:160
  (44 shorter events, 0.4 us)
Async XLA Ops:
  7.2 78.4 %all-gather.3.cloned.1.call-start = ((), (), s32[]{:S(2)}) async-start(), calls=%async_computation.3 | async-start | bytes 8912896 | tf_op jit(solution)/shard_map/all_gather | solution.py:275
  7.9 21.2 %collective-permute-start = (bf16[512,512]{1,0:T(8,128)(2,1)}, bf16[512,512]{1,0:T(8,128)(2,1)S(1)}, u32[]{:S(2)}, u32[]{:S(2)}) collective-permute-start(bf16[512,512]{1,0:T(8,128)(2,1)} %g_far.1), channel_id=1, source_target_pairs={{0,0},{1,16},{16,1},{17,17},{2,2},{3,18},{18,3},{19,19},{4,4},{5,2... | collective-permute-start | bytes 1572872 | tf_op jit(solution)/shard_map/ppermute | solution.py:276
  17.3 11.8 %all-to-all-start = ((f32[16,32,128]{2,1,0:T(8,128)}), f32[16,32,128]{2,1,0:T(8,128)S(1)}, u32[]{:S(2)}, u32[]{:S(2)}) async-start(f32[16,32,128]{2,1,0:T(8,128)} %bitcast.25), calls=%async_computation | async-start | bytes 524288 | tf_op jit(solution)/shard_map/all_to_all | solution.py:278
  22.8 4.7 %collective-permute-start.1 = (f32[8,128]{1,0:T(8,128)S(1)}, f32[8,128]{1,0:T(8,128)S(1)}, u32[]{:S(2)}, u32[]{:S(2)}) collective-permute-start(f32[8,128]{1,0:T(8,128)S(1)} %broadcast_in_dim.32), channel_id=1, source_target_pairs={{0,16},{16,0},{1,17},{17,1},{2,18},{18,2},{3,19},{19,3},{4,20},{20... | collective-permute-start | bytes 12296 | tf_op jit(solution)/shard_map/ppermute | solution.py:265
  29.1 20.4 %collective-permute-start.2 = (bf16[512,512]{1,0:T(8,128)(2,1)S(1)}, bf16[512,512]{1,0:T(8,128)(2,1)S(1)}, u32[]{:S(2)}, u32[]{:S(2)}) collective-permute-start(bf16[512,512]{1,0:T(8,128)(2,1)S(1)} %collective-permute-done.refs_0_), channel_id=1, source_target_pairs={{0,8},{8,0},{1,9},{9,1},{2,10},{10,2},{3,11},{11,3},{4,12},{12,4},... | collective-permute-start | bytes 1572872 | tf_op jit(solution)/shard_map/ppermute | solution.py:265
  29.9 19.6 %collective-permute-start.3 = (bf16[512,512]{1,0:T(8,128)(2,1)S(1)}, bf16[512,512]{1,0:T(8,128)(2,1)S(1)}, u32[]{:S(2)}, u32[]{:S(2)}) collective-permute-start(bf16[512,512]{1,0:T(8,128)(2,1)S(1)} %collective-permute-done.refs_0_), channel_id=1, source_target_pairs={{0,2},{2,4},{4,6},{6,0},{1,3},{3,5},{5,7},{7,1},{8,10},{10,12},{12... | collective-permute-start | bytes 1572872 | tf_op jit(solution)/shard_map/ppermute | solution.py:257
  30.1 19.4 %collective-permute-start.4 = (bf16[512,512]{1,0:T(8,128)(2,1)S(1)}, bf16[512,512]{1,0:T(8,128)(2,1)S(1)}, u32[]{:S(2)}, u32[]{:S(2)}) collective-permute-start(bf16[512,512]{1,0:T(8,128)(2,1)S(1)} %collective-permute-done.refs_0_), channel_id=1, source_target_pairs={{0,6},{2,0},{4,2},{6,4},{1,7},{3,1},{5,3},{7,5},{8,14},{10,8},{12,... | collective-permute-start | bytes 1572872 | tf_op jit(solution)/shard_map/ppermute | solution.py:257
  32.7 10.6 %collective-permute-start.5 = (f32[2,8,128]{2,1,0:T(8,128)S(1)}, f32[2,8,128]{2,1,0:T(8,128)S(1)}, u32[]{:S(2)}, u32[]{:S(2)}) collective-permute-start(f32[2,8,128]{2,1,0:T(8,128)S(1)} %pad_maximum_fusion.1), channel_id=1, source_target_pairs={{0,32},{32,0},{64,96},{96,64},{128,160},{160,128},{192,224},{224,1... | collective-permute-start | bytes 24584 | tf_op jit(solution)/shard_map/ppermute | solution.py:265
  34.3 9.1 %collective-permute-start.6 = (f32[2,8,128]{2,1,0:T(8,128)S(1)}, f32[2,8,128]{2,1,0:T(8,128)S(1)}, u32[]{:S(2)}, u32[]{:S(2)}) collective-permute-start(f32[2,8,128]{2,1,0:T(8,128)S(1)} %pad_maximum_fusion.1), channel_id=1, source_target_pairs={{0,64},{32,96},{64,0},{96,32},{128,192},{160,224},{192,128},{224,1... | collective-permute-start | bytes 24584 | tf_op jit(solution)/shard_map/ppermute | solution.py:265
  38.0 11.5 %all-to-all-start.1 = ((bf16[16,32,128]{2,1,0:T(8,128)(2,1)}), bf16[16,32,128]{2,1,0:T(8,128)(2,1)S(1)}, u32[]{:S(2)}, u32[]{:S(2)}) async-start(bf16[16,32,128]{2,1,0:T(8,128)(2,1)} %broadcast_in_dim.33), calls=%async_computation.1 | async-start | bytes 262144 | tf_op jit(solution)/shard_map/all_to_all | solution.py:288
  43.3 4.8 %collective-permute-start.7 = (f32[2,8,128]{2,1,0:T(8,128)S(1)}, f32[2,8,128]{2,1,0:T(8,128)S(1)}, u32[]{:S(2)}, u32[]{:S(2)}) collective-permute-start(f32[2,8,128]{2,1,0:T(8,128)S(1)} %pad_maximum_fusion.1), channel_id=1, source_target_pairs={{0,96},{32,64},{64,32},{96,0},{128,224},{160,192},{192,160},{224,1... | collective-permute-start | bytes 24584 | tf_op jit(solution)/shard_map/ppermute | solution.py:265
  49.5 7.0 %copy-start = (bf16[16,32,128]{2,1,0:T(8,128)(2,1)}, bf16[16,32,128]{2,1,0:T(8,128)(2,1)S(1)}, u32[]{:S(2)}) copy-start(bf16[16,32,128]{2,1,0:T(8,128)(2,1)S(1)} %all-to-all-done.1) | copy-start | bytes 393220
  49.5 15.0 %collective-permute-start.8 = (bf16[512,512]{1,0:T(8,128)(2,1)S(1)}, bf16[512,512]{1,0:T(8,128)(2,1)}, u32[]{:S(2)}, u32[]{:S(2)}) collective-permute-start(bf16[512,512]{1,0:T(8,128)(2,1)S(1)} %collective-permute-done.3.refs_2_), channel_id=1, source_target_pairs={{0,2},{2,4},{4,6},{6,0},{1,3},{3,5},{5,7},{7,1},{8,10},{10,12},{12... | collective-permute-start | bytes 1572872 | tf_op jit(solution)/shard_map/ppermute | solution.py:257
  50.0 14.5 %collective-permute-start.9 = (bf16[512,512]{1,0:T(8,128)(2,1)S(1)}, bf16[512,512]{1,0:T(8,128)(2,1)}, u32[]{:S(2)}, u32[]{:S(2)}) collective-permute-start(bf16[512,512]{1,0:T(8,128)(2,1)S(1)} %collective-permute-done.2.refs_1_), channel_id=1, source_target_pairs={{0,6},{2,0},{4,2},{6,4},{1,7},{3,1},{5,3},{7,5},{8,14},{10,8},{12,... | collective-permute-start | bytes 1572872 | tf_op jit(solution)/shard_map/ppermute | solution.py:257
  52.3 12.2 %collective-permute-start.10 = (f32[8,8,128]{2,1,0:T(8,128)S(1)}, f32[8,8,128]{2,1,0:T(8,128)S(1)}, u32[]{:S(2)}, u32[]{:S(2)}) collective-permute-start(f32[8,8,128]{2,1,0:T(8,128)S(1)} %constant_dynamic-update-slice_fusion), channel_id=1, source_target_pairs={{0,128},{32,160},{64,192},{96,224},{128,0},{160,32},{192,64},{224,... | collective-permute-start | bytes 98312 | tf_op jit(solution)/shard_map/ppermute | solution.py:265
  60.3 23.9 %all-to-all-start.2 = ((bf16[16,32,512]{2,1,0:T(8,128)(2,1)}), bf16[16,32,512]{2,1,0:T(8,128)(2,1)S(1)}, u32[]{:S(2)}, u32[]{:S(2)}) async-start(bf16[16,32,512]{2,1,0:T(8,128)(2,1)} %shard_map.95), calls=%async_computation.2 | async-start | bytes 1048576 | tf_op jit(solution)/shard_map/all_to_all | solution.py:295
  64.5 21.1 %copy-start.1 = (bf16[16,32,128]{2,1,0:T(8,128)(2,1)S(1)}, bf16[16,32,128]{2,1,0:T(8,128)(2,1)}, u32[]{:S(2)}) copy-start(bf16[16,32,128]{2,1,0:T(8,128)(2,1)} %copy-done) | copy-start | bytes 393220
  64.5 21.1 %copy-start.3 = (s32[4]{0:T(128)S(1)}, s32[4]{0:T(128)}, u32[]{:S(2)}) copy-start(s32[4]{0:T(128)} %live.3) | copy-start | bytes 52
  64.5 21.1 %copy-start.4 = (s32[4,1]{0,1:T(1,128)S(1)}, s32[4,1]{0,1:T(1,128)}, u32[]{:S(2)}) copy-start(s32[4,1]{0,1:T(1,128)} %param.12) | copy-start | bytes 52
  64.6 12.9 %collective-permute-start.11 = (bf16[512,512]{1,0:T(8,128)(2,1)S(1)}, bf16[512,512]{1,0:T(8,128)(2,1)S(1)}, u32[]{:S(2)}, u32[]{:S(2)}) collective-permute-start(bf16[512,512]{1,0:T(8,128)(2,1)S(1)} %collective-permute-done.2.refs_1_), channel_id=1, source_target_pairs={{0,2},{2,4},{4,6},{6,0},{1,3},{3,5},{5,7},{7,1},{8,10},{10,12},{12... | collective-permute-start | bytes 1572872 | tf_op jit(solution)/shard_map/ppermute | solution.py:257
  64.6 12.8 %collective-permute-start.12 = (bf16[512,512]{1,0:T(8,128)(2,1)}, bf16[512,512]{1,0:T(8,128)(2,1)}, u32[]{:S(2)}, u32[]{:S(2)}) collective-permute-start(bf16[512,512]{1,0:T(8,128)(2,1)} %collective-permute-done.9.refs_5_), channel_id=1, source_target_pairs={{0,6},{2,0},{4,2},{6,4},{1,7},{3,1},{5,3},{7,5},{8,14},{10,8},{12,... | collective-permute-start | bytes 1572872 | tf_op jit(solution)/shard_map/ppermute | solution.py:257
  67.9 16.3 %copy-start.2 = (s32[5]{0:T(128)S(1)}, s32[5]{0:T(128)}, u32[]{:S(2)}) copy-start(s32[5]{0:T(128)} %stack.46.x.place) | copy-start | bytes 64
  85.0 9.1 %collective-permute-start.13 = (bf16[64,512]{1,0:T(8,128)(2,1)S(1)}, bf16[64,512]{1,0:T(8,128)(2,1)S(1)}, u32[]{:S(2)}, u32[]{:S(2)}) collective-permute-start(bf16[64,512]{1,0:T(8,128)(2,1)S(1)} %shard_map.97), channel_id=1, source_target_pairs={{0,16},{16,0},{1,17},{17,1},{2,18},{18,2},{3,19},{19,3},{4,20},{20... | collective-permute-start | bytes 196616 | tf_op jit(solution)/shard_map/ppermute | solution.py:265
  85.6 32.5 %copy-start.5 = (s32[5]{0:T(128)S(1)}, s32[5]{0:T(128)}, u32[]{:S(2)}) copy-start(s32[5]{0:T(128)} %shard_map.96.place) | copy-start | bytes 64
  94.1 16.3 %collective-permute-start.15 = (bf16[512,512]{1,0:T(8,128)(2,1)S(1)}, bf16[512,512]{1,0:T(8,128)(2,1)S(1)}, u32[]{:S(2)}, u32[]{:S(2)}) collective-permute-start(bf16[512,512]{1,0:T(8,128)(2,1)S(1)} %get-tuple-element.55), channel_id=1, source_target_pairs={{0,1},{1,17},{16,0},{17,16},{2,3},{3,19},{18,2},{19,18},{4,5},{5,2... | collective-permute-start | bytes 1572872 | tf_op jit(solution)/shard_map/ppermute | solution.py:308
  96.9 16.1 %collective-permute-start.14 = (bf16[512,512]{1,0:T(8,128)(2,1)S(1)}, bf16[512,512]{1,0:T(8,128)(2,1)S(1)}, u32[]{:S(2)}, u32[]{:S(2)}) collective-permute-start(bf16[512,512]{1,0:T(8,128)(2,1)S(1)} %get-tuple-element.54), channel_id=1, source_target_pairs={{1,16},{16,1},{3,18},{18,3},{5,20},{20,5},{7,22},{22,7},{9,24},{24... | collective-permute-start | bytes 1572872 | tf_op jit(solution)/shard_map/ppermute | solution.py:307
  101.5 6.4 %collective-permute-start.16 = (bf16[2,64,512]{2,1,0:T(8,128)(2,1)S(1)}, bf16[2,64,512]{2,1,0:T(8,128)(2,1)S(1)}, u32[]{:S(2)}, u32[]{:S(2)}) collective-permute-start(bf16[2,64,512]{2,1,0:T(8,128)(2,1)S(1)} %maximum_select_fusion.refs_0_), channel_id=1, source_target_pairs={{0,64},{32,96},{64,128},{96,160},{128,192},{160,224},{192,0},{224,... | collective-permute-start | bytes 393224 | tf_op jit(solution)/shard_map/ppermute | solution.py:257
  101.6 8.3 %collective-permute-start.18 = (bf16[2,64,512]{2,1,0:T(8,128)(2,1)S(1)}, bf16[2,64,512]{2,1,0:T(8,128)(2,1)S(1)}, u32[]{:S(2)}, u32[]{:S(2)}) collective-permute-start(bf16[2,64,512]{2,1,0:T(8,128)(2,1)S(1)} %maximum_select_fusion.refs_0_), channel_id=1, source_target_pairs={{0,192},{32,224},{64,0},{96,32},{128,64},{160,96},{192,128},{224,1... | collective-permute-start | bytes 393224 | tf_op jit(solution)/shard_map/ppermute | solution.py:257
  105.2 12.9 %collective-permute-start.21 = (bf16[2,64,512]{2,1,0:T(8,128)(2,1)S(1)}, bf16[2,64,512]{2,1,0:T(8,128)(2,1)S(1)}, u32[]{:S(2)}, u32[]{:S(2)}) collective-permute-start(bf16[2,64,512]{2,1,0:T(8,128)(2,1)S(1)} %maximum_select_fusion.refs_0_), channel_id=1, source_target_pairs={{0,32},{32,64},{64,96},{96,128},{128,160},{160,192},{192,224},{224... | collective-permute-start | bytes 393224 | tf_op jit(solution)/shard_map/ppermute | solution.py:257
  107.9 10.2 %collective-permute-start.22 = (bf16[2,64,512]{2,1,0:T(8,128)(2,1)S(1)}, bf16[2,64,512]{2,1,0:T(8,128)(2,1)S(1)}, u32[]{:S(2)}, u32[]{:S(2)}) collective-permute-start(bf16[2,64,512]{2,1,0:T(8,128)(2,1)S(1)} %maximum_select_fusion.refs_0_), channel_id=1, source_target_pairs={{0,224},{32,0},{64,32},{96,64},{128,96},{160,128},{192,160},{224,1... | collective-permute-start | bytes 393224 | tf_op jit(solution)/shard_map/ppermute | solution.py:257
  109.9 8.0 %collective-permute-start.17 = (bf16[2,64,512]{2,1,0:T(8,128)(2,1)S(1)}, bf16[2,64,512]{2,1,0:T(8,128)(2,1)S(1)}, u32[]{:S(2)}, u32[]{:S(2)}) collective-permute-start(bf16[2,64,512]{2,1,0:T(8,128)(2,1)S(1)} %collective-permute-done.16.refs_3_), channel_id=1, source_target_pairs={{0,32},{32,64},{64,96},{96,128},{128,160},{160,192},{192,224},{224... | collective-permute-start | bytes 393224 | tf_op jit(solution)/shard_map/ppermute | solution.py:257
  110.4 7.7 %collective-permute-start.20 = (bf16[2,64,512]{2,1,0:T(8,128)(2,1)S(1)}, bf16[2,64,512]{2,1,0:T(8,128)(2,1)S(1)}, u32[]{:S(2)}, u32[]{:S(2)}) collective-permute-start(bf16[2,64,512]{2,1,0:T(8,128)(2,1)S(1)} %collective-permute-done.16.refs_3_), channel_id=1, source_target_pairs={{0,64},{32,96},{64,128},{96,160},{128,192},{160,224},{192,0},{224,... | collective-permute-start | bytes 393224 | tf_op jit(solution)/shard_map/ppermute | solution.py:257
  113.0 4.9 %collective-permute-start.19 = (bf16[2,64,512]{2,1,0:T(8,128)(2,1)S(1)}, bf16[2,64,512]{2,1,0:T(8,128)(2,1)S(1)}, u32[]{:S(2)}, u32[]{:S(2)}) collective-permute-start(bf16[2,64,512]{2,1,0:T(8,128)(2,1)S(1)} %collective-permute-done.18.refs_4_), channel_id=1, source_target_pairs={{0,224},{32,0},{64,32},{96,64},{128,96},{160,128},{192,160},{224,1... | collective-permute-start | bytes 393224 | tf_op jit(solution)/shard_map/ppermute | solution.py:257
Sparse Core Ops, SparseCore 0:
  9.8 62.5 all-gather.2
